TPU v7x, 32 devices: a whole 2x2x4 slice. The times are simulated.
32 devices in a mesh: section: 2 (over core), ctx: 16 (over z, y, x).
Axes of the slice: x: 2, y: 2, z: 4, core: 2. Of those that a mesh axis runs over, the one named last changes fastest.
Arguments:
- down_queries: bfloat16 [2, 2048, 2304], P('section', 'ctx'), may hold values from -40 to 40
- down_keys: bfloat16 [2, 2048, 2304], P('section', 'ctx'), may hold values from -40 to 40
- down_values: bfloat16 [2, 2048, 2304], P('section', 'ctx'), may hold values from -6 to 6
- up_queries: bfloat16 [2, 2048, 2304], P('section', 'ctx'), may hold values from -40 to 40
- up_keys: bfloat16 [2, 2048, 2304], P('section', 'ctx'), may hold values from -40 to 40
- up_values: bfloat16 [2, 2048, 2304], P('section', 'ctx'), may hold values from -6 to 6
- key_blocks: int32 [16, 2], P('ctx'), may hold values from -1 to 11, as said below
Outputs:
- forward: bfloat16 [2, 2048, 2304], P('section', 'ctx')
- handed: bfloat16 [2, 2048, 2304], P('section', 'ctx')
Inputs may be any that keep to these rules, and one draw needn't show every extreme that they name: `key_blocks`: slot k (counting from 1) of query block i holds i - k * 4 or -1, and -1 wherever i - k * 4 is negative.
All inputs are finite; a program needn't handle non-finite values.
Results may differ from a plain program's by a relative error of at most 0.0038.
Values may be sent and summed in bfloat16 or wider, within the bound.
No kernel may reach another device: no remote copies, remote signals or barrier semaphores. Data moves between devices by JAX's collectives and lax.ppermute only.
A program may use at most 64 MiB of HBM per device.

v0:
```python
import math

import jax
import jax.numpy as jnp
from jax import lax
from jax.sharding import PartitionSpec as P

HEAD_DIM = 64
BLOCK = 128


def shifted(block, axis, distance):
    devices = range(lax.axis_size(axis))
    route = [(i - distance, i) for i in devices if i - distance in devices]
    return lax.ppermute(block, axis, route)


def on_device(down_queries, down_keys, down_values, up_queries, up_keys, up_values, key_blocks):
    queries = jnp.concatenate([down_queries, up_queries], 0)
    key_values = jnp.stack(
        [jnp.concatenate([down_keys, down_values], 0), jnp.concatenate([up_keys, up_values], 0)]
    )
    tok_rows = queries.shape[1]
    width = queries.shape[2]
    blocks_dev = key_blocks.shape[0]
    strided_count = key_blocks.shape[1]
    head_count = width // HEAD_DIM
    spacing = lax.axis_size("ctx") // 4
    far_pairs = []
    for offset_step in range(1, strided_count + 1):
        far_pairs.append(shifted(key_values, "ctx", offset_step * spacing))
    present = key_blocks >= 0
    causal = jnp.arange(BLOCK)[:, None] >= jnp.arange(BLOCK)[None, :]
    allowed_parts = [causal[None, None]]
    for offset_step in range(strided_count):
        allowed_parts.append(
            jnp.broadcast_to(
                present[:, offset_step][:, None, None, None], (blocks_dev, 1, BLOCK, BLOCK)
            )
        )
    allowed_all = jnp.concatenate(allowed_parts, 3)
    block_shape = (blocks_dev, BLOCK, head_count, HEAD_DIM)
    scale = 1.0 / math.sqrt(HEAD_DIM)
    results = []
    for group_side in range(2):
        query_rows = queries[group_side].reshape(block_shape)
        key_all = jnp.concatenate(
            [key_values[group_side, 0].reshape(block_shape)]
            + [pair_rows[group_side, 0].reshape(block_shape) for pair_rows in far_pairs],
            1,
        )
        value_all = jnp.concatenate(
            [key_values[group_side, 1].reshape(block_shape)]
            + [pair_rows[group_side, 1].reshape(block_shape) for pair_rows in far_pairs],
            1,
        )
        scores = (
            jnp.einsum("nqhd,nkhd->nhqk", query_rows, key_all, preferred_element_type=jnp.float32)
            * scale
        )
        scores = jnp.where(allowed_all, scores, -1e30)
        highest = jnp.max(scores, -1, keepdims=True)
        expo = jnp.exp(scores - highest)
        weights = (expo / jnp.sum(expo, -1, keepdims=True)).astype(jnp.bfloat16)
        mixture = jnp.einsum(
            "nhqk,nkhd->nqhd", weights, value_all, preferred_element_type=jnp.float32
        )
        results.append(mixture.reshape(tok_rows, width).astype(jnp.bfloat16)[None])
    lowered = results[0]
    raised = results[1]
    section_index = lax.axis_index("section")
    last_section = lax.axis_size("section") - 1
    forward = shifted(lowered, "section", 1)
    forward = jnp.where(section_index == 0, raised, forward)
    handed = shifted(raised, "section", -1)
    handed = jnp.where(section_index == last_section, lowered, handed)
    return (forward, handed)


def solution(mesh):
    placed = (
        P("section", "ctx", None),
        P("section", "ctx", None),
        P("section", "ctx", None),
        P("section", "ctx", None),
        P("section", "ctx", None),
        P("section", "ctx", None),
        P("ctx", None),
    )
    return jax.shard_map(
        on_device,
        mesh=mesh,
        in_specs=placed,
        out_specs=(P("section", "ctx", None), P("section", "ctx", None)),
        check_vma=False,
    )
```

profile of v0, /device:TPU:25, one launch (start us, length us, event | category | flops | bytes accessed | tf_op | source)
XLA Modules:
  0.0 203.6 jit_solution(11333530985273968557)
XLA Ops:
  0.6 1.8 maximum_bitcast_fusion.12
  2.5 1.6 pad_maximum_fusion
  4.1 1.4 collective-permute-start
  5.5 1.3 collective-permute-start.1
  10.9 1.4 copy.35
  12.3 1.1 copy.29
  14.1 44.4 %collective-permute-done = bf16[2,2,128,2304]{3,2,1,0:T(8,128)(2,1)} collective-permute-done((bf16[2,2,128,2304]{3,2,1,0:T(8,128)(2,1)}, bf16[2,2,128,2304]{3,2,1,0:T(8,128)(2,1)}, u32[]{:S(2)}, u32[]{:S(2)}) %collective-permute-start) | collective-permute-done | bytes 2359328 | tf_op jit(solution)/shard_map/ppermute | solution.py:15
  58.5 2.8 %fusion.40 = (bf16[1,1,128,2304]{3,2,1,0:T(8,128)(2,1)}, bf16[1,1,128,2304]{3,2,1,0:T(8,128)(2,1)S(1)}, bf16[1,1,128,2304]{3,2,1,0:T(8,128)(2,1)}, bf16[1,1,128,2304]{3,2,1,0:T(8,128)(2,1)S(1)}) fusion(bf16[2,2,128,2304]{3,2,1,0:T(8,128)(2,1)} %collective-permute-done), kind=kLoop, calls=%fused_computation.58 | loop fusion | bytes 4718592 | tf_op jit(solution)/shard_map/slice | solution.py:54
  62.3 97.2 %collective-permute-done.1 = bf16[2,2,128,2304]{3,2,1,0:T(8,128)(2,1)} collective-permute-done((bf16[2,2,128,2304]{3,2,1,0:T(8,128)(2,1)}, bf16[2,2,128,2304]{3,2,1,0:T(8,128)(2,1)}, u32[]{:S(2)}, u32[]{:S(2)}) %collective-permute-start.1) | collective-permute-done | bytes 2359328 | tf_op jit(solution)/shard_map/ppermute | solution.py:15
  159.5 2.9 %fusion.41 = (bf16[1,1,128,2304]{3,2,1,0:T(8,128)(2,1)}, bf16[1,1,128,2304]{3,2,1,0:T(8,128)(2,1)}, bf16[1,1,128,2304]{3,2,1,0:T(8,128)(2,1)}, bf16[1,1,128,2304]{3,2,1,0:T(8,128)(2,1)S(1)}) fusion(bf16[2,2,128,2304]{3,2,1,0:T(8,128)(2,1)} %collective-permute-done.1), kind=kLoop, calls=%fused_computation.59 | loop fusion | bytes 4718592 | tf_op jit(solution)/shard_map/slice | solution.py:54
  162.4 2.1 %copy.42 = bf16[1,1,128,2304]{2,3,1,0:T(8,128)(2,1)} copy(bf16[1,1,128,2304]{3,2,1,0:T(8,128)(2,1)} %get-tuple-element.7) | data formatting | bytes 1179648 | tf_op jit(solution)/shard_map/slice | solution.py:49
  164.5 2.1 %copy.38 = bf16[1,1,128,2304]{2,3,1,0:T(8,128)(2,1)} copy(bf16[1,1,128,2304]{3,2,1,0:T(8,128)(2,1)} %get-tuple-element.2) | data formatting | bytes 1179648 | tf_op jit(solution)/shard_map/slice | solution.py:54
  166.7 2.1 %copy.39 = bf16[1,1,128,2304]{2,3,1,0:T(8,128)(2,1)} copy(bf16[1,1,128,2304]{3,2,1,0:T(8,128)(2,1)} %get-tuple-element.6) | data formatting | bytes 1179648 | tf_op jit(solution)/shard_map/slice | solution.py:54
  168.8 2.1 %copy.33 = bf16[1,1,128,2304]{2,3,1,0:T(8,128)(2,1)} copy(bf16[1,1,128,2304]{3,2,1,0:T(8,128)(2,1)} %get-tuple-element.4) | data formatting | bytes 1179648 | tf_op jit(solution)/shard_map/slice | solution.py:49
  170.9 2.1 %copy.34 = bf16[1,1,128,2304]{2,3,1,0:T(8,128)(2,1)} copy(bf16[1,1,128,2304]{3,2,1,0:T(8,128)(2,1)} %get-tuple-element.8) | data formatting | bytes 1179648 | tf_op jit(solution)/shard_map/slice | solution.py:49
  173.0 2.4 %fusion.25 = f32[36,384,128]{2,1,0:T(8,128)S(1)} fusion(bf16[128,36,64]{0,2,1:T(8,128)(2,1)S(1)} %bitcast.73, bf16[1,128,36,64]{1,3,2,0:T(8,128)(2,1)} %bitcast.79, bf16[1,128,36,64]{1,3,2,0:T(8,128)(2,1)} %bitcast.76, bf16[1,128,36,64]{1,3,2,0:T(8,128)(2,1)S(1)} %bitcast.72), kind=kOutput, calls=%fused_computation.36 | convolution fusion | flops 231800832 | bytes 9437184 | tf_op jit(solution)/shard_map/nqhd,nkhd->nhqk/dot_general | solution.py:58
  175.5 4.5 %fusion.46 = (f32[36,128]{1,0:T(8,128)}, f32[36,128,384]{1,2,0:T(8,128)}) fusion(f32[36,384,128]{2,1,0:T(8,128)S(1)} %fusion.25, pred[128,384]{0,1:T(8,128)(4,1)S(1)} %copy-done.7), kind=kOutput, calls=%fused_computation.64 | output fusion | flops 10617215 | bytes 14223360 | tf_op jit(solution)/shard_map/sub | solution.py:63
  180.0 1.1 fusion.16
  181.1 4.5 %fusion.45 = (f32[36,128]{1,0:T(8,128)}, f32[36,128,384]{1,2,0:T(8,128)}) fusion(f32[36,384,128]{2,1,0:T(8,128)S(1)} %fusion.16, pred[128,384]{0,1:T(8,128)(4,1)S(1)} %copy-done.7), kind=kOutput, calls=%fused_computation.63 | output fusion | flops 10617215 | bytes 14223360 | tf_op jit(solution)/shard_map/sub | solution.py:63
  187.0 4.0 %fusion.31 = bf16[36,64,128]{2,1,0:T(8,128)(2,1)S(1)} fusion(f32[36,128,384]{1,2,0:T(8,128)} %get-tuple-element.17, f32[36,128]{1,0:T(8,128)} %get-tuple-element.16, bf16[1,128,36,64]{1,3,2,0:T(8,128)(2,1)S(1)} %bitcast.85, bf16[1,128,36,64]{1,3,2,0:T(8,128)(2,1)} %bitcast.84, bf16[1,128,36,64]{1,3,2,0:T(8,128)(2,1)S(1)} %bitcast.81), kind=kOutput, calls=%fused_computation.42 | convolution fusion | flops 235634688 | bytes 9455616 | tf_op jit(solution)/shard_map/nhqk,nkhd->nqhd/dot_general | solution.py:65
  191.2 3.5 %collective-permute-start.3 = (bf16[1,128,2304]{2,1,0:T(8,128)(2,1)S(1)}, bf16[1,128,2304]{2,1,0:T(8,128)(2,1)S(1)}, u32[]{:S(2)}, u32[]{:S(2)}) collective-permute-start(bf16[1,128,2304]{2,1,0:T(8,128)(2,1)S(1)} %copy.46), channel_id=1, source_target_pairs={{16,0},{17,1},{18,2},{19,3},{20,4},{21,5},{22,6},{23,7},{24,8},{25... | collective-permute-start | bytes 1769480 | tf_op jit(solution)/shard_map/ppermute | solution.py:15
  194.8 3.8 %fusion.30 = bf16[36,64,128]{2,1,0:T(8,128)(2,1)S(1)} fusion(f32[36,128,384]{1,2,0:T(8,128)} %get-tuple-element.19, f32[36,128]{1,0:T(8,128)} %get-tuple-element.18, bf16[1,128,36,64]{1,3,2,0:T(8,128)(2,1)S(1)} %bitcast.83, bf16[1,128,36,64]{1,3,2,0:T(8,128)(2,1)S(1)} %bitcast.82, bf16[1,128,36,64]{1,3,2,0:T(8,128)(2,1)S(1)} %bitcast.80), kind=kOutput, calls=%fused_computation.41 | convolution fusion | flops 235634688 | bytes 9455616 | tf_op jit(solution)/shard_map/nhqk,nkhd->nqhd/dot_general | solution.py:65
  198.8 1.3 collective-permute-start.2
  201.0 1.7 collective-permute-done.2
  (40 shorter events, 9.5 us)
Async XLA Ops:
  2.4 4.7 %copy-start.2 = (bf16[1,128,2304]{2,1,0:T(8,128)(2,1)S(1)}, bf16[1,128,2304]{2,1,0:T(8,128)(2,1)}, u32[]{:S(2)}) copy-start(bf16[1,128,2304]{2,1,0:T(8,128)(2,1)} %param.7) | copy-start | bytes 1769476
  4.1 3.4 %copy-start.8 = (s32[1,2]{1,0:T(1,128)S(1)}, s32[1,2]{1,0:T(1,128)}, u32[]{:S(2)}) copy-start(s32[1,2]{1,0:T(1,128)} %param.13) | copy-start | bytes 28
  4.1 54.4 %collective-permute-start = (bf16[2,2,128,2304]{3,2,1,0:T(8,128)(2,1)}, bf16[2,2,128,2304]{3,2,1,0:T(8,128)(2,1)}, u32[]{:S(2)}, u32[]{:S(2)}) collective-permute-start(bf16[2,2,128,2304]{3,2,1,0:T(8,128)(2,1)} %pad_maximum_fusion), channel_id=1, source_target_pairs={{0,4},{1,5},{2,6},{3,7},{4,8},{5,9},{6,10},{7,11},{8,12},{9,13},{1... | collective-permute-start | bytes 7077896 | tf_op jit(solution)/shard_map/ppermute | solution.py:15
  5.5 154.0 %collective-permute-start.1 = (bf16[2,2,128,2304]{3,2,1,0:T(8,128)(2,1)}, bf16[2,2,128,2304]{3,2,1,0:T(8,128)(2,1)}, u32[]{:S(2)}, u32[]{:S(2)}) collective-permute-start(bf16[2,2,128,2304]{3,2,1,0:T(8,128)(2,1)} %pad_maximum_fusion), channel_id=1, source_target_pairs={{0,8},{1,9},{2,10},{3,11},{4,12},{5,13},{6,14},{7,15},{16,24},{17,... | collective-permute-start | bytes 7077896 | tf_op jit(solution)/shard_map/ppermute | solution.py:15
  173.0 2.4 %copy-start.7 = (pred[128,384]{0,1:T(8,128)(4,1)S(1)}, pred[128,384]{0,1:T(8,128)(4,1)}, u32[]{:S(2)}) copy-start(pred[128,384]{0,1:T(8,128)(4,1)} %add_bitcast_fusion) | copy-start | bytes 147460
  175.4 4.5 %copy-start = (bf16[1,1,128,2304]{2,3,1,0:T(8,128)(2,1)S(1)}, bf16[1,1,128,2304]{2,3,1,0:T(8,128)(2,1)}, u32[]{:S(2)}) copy-start(bf16[1,1,128,2304]{2,3,1,0:T(8,128)(2,1)} %copy.33) | copy-start | bytes 1769476
  175.4 4.5 %copy-start.1 = (bf16[1,1,128,2304]{2,3,1,0:T(8,128)(2,1)S(1)}, bf16[1,1,128,2304]{2,3,1,0:T(8,128)(2,1)}, u32[]{:S(2)}) copy-start(bf16[1,1,128,2304]{2,3,1,0:T(8,128)(2,1)} %copy.34) | copy-start | bytes 1769476
  181.1 5.9 %copy-start.4 = (bf16[1,1,128,2304]{2,3,1,0:T(8,128)(2,1)S(1)}, bf16[1,1,128,2304]{2,3,1,0:T(8,128)(2,1)}, u32[]{:S(2)}) copy-start(bf16[1,1,128,2304]{2,3,1,0:T(8,128)(2,1)} %copy.29) | copy-start | bytes 1769476
  187.0 7.8 %copy-start.3 = (bf16[1,1,128,2304]{2,3,1,0:T(8,128)(2,1)S(1)}, bf16[1,1,128,2304]{2,3,1,0:T(8,128)(2,1)}, u32[]{:S(2)}) copy-start(bf16[1,1,128,2304]{2,3,1,0:T(8,128)(2,1)} %copy.37) | copy-start | bytes 1769476
  187.0 7.8 %copy-start.5 = (bf16[1,1,128,2304]{2,3,1,0:T(8,128)(2,1)S(1)}, bf16[1,1,128,2304]{2,3,1,0:T(8,128)(2,1)}, u32[]{:S(2)}) copy-start(bf16[1,1,128,2304]{2,3,1,0:T(8,128)(2,1)} %copy.38) | copy-start | bytes 1769476
  187.0 7.8 %copy-start.6 = (bf16[1,1,128,2304]{2,3,1,0:T(8,128)(2,1)S(1)}, bf16[1,1,128,2304]{2,3,1,0:T(8,128)(2,1)}, u32[]{:S(2)}) copy-start(bf16[1,1,128,2304]{2,3,1,0:T(8,128)(2,1)} %copy.39) | copy-start | bytes 1769476
  191.2 8.9 %collective-permute-start.3 = (bf16[1,128,2304]{2,1,0:T(8,128)(2,1)S(1)}, bf16[1,128,2304]{2,1,0:T(8,128)(2,1)S(1)}, u32[]{:S(2)}, u32[]{:S(2)}) collective-permute-start(bf16[1,128,2304]{2,1,0:T(8,128)(2,1)S(1)} %copy.46), channel_id=1, source_target_pairs={{16,0},{17,1},{18,2},{19,3},{20,4},{21,5},{22,6},{23,7},{24,8},{25... | collective-permute-start | bytes 1769480 | tf_op jit(solution)/shard_map/ppermute | solution.py:15
  198.8 3.9 %collective-permute-start.2 = (bf16[1,128,2304]{2,1,0:T(8,128)(2,1)S(1)}, bf16[1,128,2304]{2,1,0:T(8,128)(2,1)S(1)}, u32[]{:S(2)}, u32[]{:S(2)}) collective-permute-start(bf16[1,128,2304]{2,1,0:T(8,128)(2,1)S(1)} %copy.45), channel_id=1, source_target_pairs={{0,16},{1,17},{2,18},{3,19},{4,20},{5,21},{6,22},{7,23},{8,24},{9,... | collective-permute-start | bytes 1769480 | tf_op jit(solution)/shard_map/ppermute | solution.py:15
where the time goes:
time: 204 us
  waiting for transfers between devices  143 us (70%)
  local copies, waits for them, and re-layouts  25.7 us (13%)
  other arithmetic  15 us (7%)
  matrix products  11.3 us (6%)
  starting transfers between devices  7.48 us (4%)
    ppermute x4, waiting for transfers between devices, shifted(): return lax.ppermute(block, axis, route)  143 us
    slice x6, local copies, waits for them, and re-layouts, on_device(): pair_rows[group_side, 1].reshape(block_shape)  11.3 us
    sub x2, other arithmetic, on_device(): expo = jnp.exp(scores - highest)  9.01 us
    dot_general x2, matrix products, on_device(): jnp.einsum('nhqk,nkhd->nqhd', weights, value_all, preferred_element_type=...  7.74 us
    ppermute x4, starting transfers between devices, shifted(): return lax.ppermute(block, axis, route)  7.48 us
    slice x4, local copies, waits for them, and re-layouts, on_device(): pair_rows[group_side, 0].reshape(block_shape)  7.42 us
  transfers between devices with their start and end apart: 4, of which 3 were waited for; matrix products, arithmetic and copies ran while one was open for 8% of the time, Pallas kernels for 0%

commit v1 on v0

v1 whole, which is shorter than its diff:
```python
import functools
import math

import jax
import jax.numpy as jnp
from jax import lax
from jax.experimental import pallas as pl
from jax.experimental.pallas import tpu as pltpu
from jax.sharding import PartitionSpec as P

HEAD_DIM = 64
BLOCK = 128
TILE = 2 * HEAD_DIM
FIELD = 21
ABSENT = -1e30
FACTOR = math.log2(math.e) / math.sqrt(HEAD_DIM)


def lanes():
    return lax.broadcasted_iota(jnp.int32, (BLOCK, TILE), 1)


def by_head(tile, low):
    zero = jnp.zeros_like(tile)
    return jnp.concatenate([jnp.where(low, tile, zero), jnp.where(low, zero, tile)], 0)


def partial(query, key, value, low, low16, causal):
    scores = lax.dot_general(
        query, by_head(key, low16), (((1,), (1,)), ((), ())), preferred_element_type=jnp.float32
    ) * FACTOR
    first, second = scores[:, :BLOCK], scores[:, BLOCK:]
    if causal is not None:
        first = jnp.where(causal, first, ABSENT)
        second = jnp.where(causal, second, ABSENT)
    top_first = jnp.max(first, -1, keepdims=True)
    top_second = jnp.max(second, -1, keepdims=True)
    weights = jnp.concatenate(
        [jnp.exp2(first - top_first), jnp.exp2(second - top_second)], 1
    ).astype(jnp.bfloat16)
    ones = jnp.ones_like(value)
    columns = jnp.concatenate([by_head(value, low16), by_head(ones, low16)], 1)
    sums = jnp.dot(weights, columns, preferred_element_type=jnp.float32)
    return sums[:, :TILE], sums[:, TILE:], jnp.where(low, top_first, top_second)


def pack(logs):
    high = logs.astype(jnp.bfloat16).astype(jnp.float32)
    rest = logs - high
    middle = rest.astype(jnp.bfloat16).astype(jnp.float32)
    last = (rest - middle).astype(jnp.bfloat16).astype(jnp.float32)
    return (high + pltpu.roll(middle, FIELD, 1) + pltpu.roll(last, 2 * FIELD, 1)).astype(jnp.bfloat16)


def unpack(packed, j):
    row = lax.broadcasted_iota(jnp.int32, (TILE, TILE), 0)
    lane = lax.broadcasted_iota(jnp.int32, (TILE, TILE), 1)
    place = row % HEAD_DIM
    piece = (place == j) | (place == j + FIELD) | (place == j + 2 * FIELD)
    pick = jnp.where(piece & (row // HEAD_DIM == lane // HEAD_DIM), 1.0, 0.0).astype(jnp.bfloat16)
    return jnp.dot(packed, pick, preferred_element_type=jnp.float32)


def kernel(tiles, part, flags_ref, query_ref, key_ref, value_ref, *refs):
    if part == 0:
        carried_ref, (out_ref,) = None, refs
    elif part == 1:
        carried_ref, out_ref = refs
    else:
        carried_ref, _, out_ref = refs
    lane = lanes()
    low = lane < HEAD_DIM
    low16 = lax.broadcasted_iota(jnp.int16, (BLOCK, TILE), 1) < HEAD_DIM
    place = lane % HEAD_DIM
    causal = None
    if part == 2:
        causal = lax.broadcasted_iota(jnp.int32, (BLOCK, BLOCK), 0) >= lax.broadcasted_iota(
            jnp.int32, (BLOCK, BLOCK), 1
        )
    if carried_ref is not None:
        packed = carried_ref[:, tiles * TILE :]
        near, far = flags_ref[0, 0] >= 0, flags_ref[0, 1] >= 0
        have = far if part == 1 else near | far

    def step(j, logs):
        columns = pl.ds(pl.multiple_of(j * TILE, TILE), TILE)
        sums, total, top = partial(
            query_ref[:, columns], key_ref[:, columns], value_ref[:, columns], low, low16, causal
        )
        if carried_ref is None:
            out_ref[:, columns] = (sums / total).astype(jnp.bfloat16)
            here = top + jnp.log2(total)
        else:
            came = jnp.where(have, unpack(packed, j), ABSENT)
            if part == 1:
                top = jnp.where(near, top, ABSENT)
            most = jnp.maximum(top, came)
            own, other = jnp.exp2(top - most), jnp.exp2(came - most)
            whole = own * total + other
            out_ref[:, columns] = (
                (own * sums + other * carried_ref[:, columns].astype(jnp.float32)) / whole
            ).astype(jnp.bfloat16)
            here = most + jnp.log2(whole)
        return jnp.where(place == j, here, logs) if part < 2 else logs

    logs = lax.fori_loop(0, tiles, step, jnp.zeros((BLOCK, TILE), jnp.float32))
    if part < 2:
        out_ref[:, tiles * TILE :] = pack(logs)


def attend(part, tiles, first, flags, query, query_first, key, value, carried=None, into=None):
    width = tiles * TILE
    place = lambda start: pl.BlockSpec((BLOCK, width), lambda _: (0, start // tiles))
    operands = [flags, query, key, value]
    specs = [pl.BlockSpec(memory_space=pltpu.SMEM), place(query_first), place(first), place(first)]
    if carried is not None:
        operands.append(carried)
        specs.append(pl.BlockSpec((BLOCK, width + TILE), lambda _: (0, 0)))
    aliases = {}
    if part < 2:
        shape, out_spec = (BLOCK, width + TILE), pl.BlockSpec((BLOCK, width + TILE), lambda _: (0, 0))
    else:
        shape, out_spec = key.shape, place(first)
        operands.append(into)
        specs.append(pl.BlockSpec(memory_space=pl.ANY))
        aliases = {len(operands) - 1: 0}
    flops = tiles * 2 * (2 * BLOCK * BLOCK * TILE * 2)
    return pl.pallas_call(
        functools.partial(kernel, tiles, part),
        grid=(1,),
        out_shape=jax.ShapeDtypeStruct(shape, jnp.bfloat16),
        in_specs=specs,
        out_specs=out_spec,
        input_output_aliases=aliases,
        name=("far", "near", "own")[part],
        compiler_params=pltpu.CompilerParams(vmem_limit_bytes=32 * 1024 * 1024),
        cost_estimate=pl.CostEstimate(
            flops=flops, bytes_accessed=5 * BLOCK * width * 2, transcendentals=tiles * 2 * BLOCK * BLOCK
        ),
    )(*operands)


def shifted(block, axis, distance):
    devices = range(lax.axis_size(axis))
    route = [(i - distance, i) for i in devices if i - distance in devices]
    return lax.ppermute(block, axis, route)


def on_device(down_queries, down_keys, down_values, up_queries, up_keys, up_values, key_blocks):
    spacing = lax.axis_size("ctx") // 4
    groups = (
        tuple(a[0] for a in (down_queries, down_keys, down_values)),
        tuple(a[0] for a in (up_queries, up_keys, up_values)),
    )
    all_tiles = down_queries.shape[2] // TILE
    tiles = all_tiles // 2
    chunks = [(g, first) for first in range(0, all_tiles, tiles) for g in range(2)]
    nearer = lambda x: shifted(x, "ctx", -spacing)
    back = lambda x: shifted(x, "ctx", spacing)
    later_flags = nearer(key_blocks)
    once = [nearer(groups[g][0][:, first * TILE : (first + tiles) * TILE]) for g, first in chunks]
    twice = [nearer(x) for x in once]
    outs = [jnp.zeros_like(groups[0][0]), jnp.zeros_like(groups[0][0])]
    for c, (g, first) in enumerate(chunks):
        _, key, value = groups[g]
        far = attend(0, tiles, first, later_flags, twice[c], 0, key, value)
        near = attend(1, tiles, first, later_flags, once[c], 0, key, value, back(far))
        outs[g] = attend(2, tiles, first, key_blocks, groups[g][0], first, key, value, back(near), outs[g])
    lowered, raised = outs[0][None], outs[1][None]
    section_index = lax.axis_index("section")
    last_section = lax.axis_size("section") - 1
    forward = shifted(lowered, "section", 1)
    forward = jnp.where(section_index == 0, raised, forward)
    handed = shifted(raised, "section", -1)
    handed = jnp.where(section_index == last_section, lowered, handed)
    return (forward, handed)


def solution(mesh):
    placed = (P("section", "ctx", None),) * 6 + (P("ctx", None),)
    return jax.shard_map(
        on_device,
        mesh=mesh,
        in_specs=placed,
        out_specs=(P("section", "ctx", None), P("section", "ctx", None)),
        check_vma=False,
    )
```

time: 204 us -> 122 us (0.60)
  the two profiles are of different devices: /device:TPU:25 before, /device:TPU:0 now
where the time goes in v1:
time: 122 us; the launch traced here: 121 us
  Pallas kernels  52.2 us (43%)
  starting transfers between devices  43.5 us (36%)
  waiting for transfers between devices  20.5 us (17%)
  other arithmetic  2.83 us (2%)
  local copies, waits for them, and re-layouts  1.33 us (1%)
    pallas_call x12, Pallas kernels, attend(): pl.pallas_call(functools.partial(kernel, tiles, part), grid=(1,), out_sha...  52.2 us
    ppermute x19, starting transfers between devices, shifted(): return lax.ppermute(block, axis, route)  43.5 us
    ppermute x19, waiting for transfers between devices, shifted(): return lax.ppermute(block, axis, route)  20.5 us
  transfers between devices with their start and end apart: 19, of which 4 were waited for; matrix products, arithmetic and copies ran while one was open for 2% of the time, Pallas kernels for 43%

profile of v1, /device:TPU:0, one launch (start us, length us, event | category | flops | bytes accessed | tf_op | source)
XLA Modules:
  0.0 121.5 jit_solution(13915814166521905963)
XLA Ops:
  5.7 8.8 %collective-permute-done.5.query_ref = bf16[128,1152]{1,0:T(8,128)(2,1)S(1)} collective-permute-done((bf16[128,1152]{1,0:T(8,128)(2,1)S(1)}, bf16[128,1152]{1,0:T(8,128)(2,1)S(1)}, u32[]{:S(2)}, u32[]{:S(2)}) %collective-permute-start.5) | collective-permute-done | bytes 294944 | tf_op jit(solution)/shard_map/ppermute | solution.py:146
  15.9 5.0 %collective-permute-done.1.query_ref = bf16[128,1152]{1,0:T(8,128)(2,1)S(1)} collective-permute-done((bf16[128,1152]{1,0:T(8,128)(2,1)S(1)}, bf16[128,1152]{1,0:T(8,128)(2,1)S(1)}, u32[]{:S(2)}, u32[]{:S(2)}) %collective-permute-start.1) | collective-permute-done | bytes 294944 | tf_op jit(solution)/shard_map/ppermute | solution.py:146
  23.7 3.5 %collective-permute-done.6.query_ref = bf16[128,1152]{1,0:T(8,128)(2,1)S(1)} collective-permute-done((bf16[128,1152]{1,0:T(8,128)(2,1)S(1)}, bf16[128,1152]{1,0:T(8,128)(2,1)S(1)}, u32[]{:S(2)}, u32[]{:S(2)}) %collective-permute-start.6) | collective-permute-done | bytes 294944 | tf_op jit(solution)/shard_map/ppermute | solution.py:146
  27.2 4.2 %far.5 = bf16[128,1280]{1,0:T(8,128)(2,1)S(1)} custom-call(s32[1,2]{1,0:T(1,128)S(1)} %collective-permute-done.flags_ref, bf16[128,1152]{1,0:T(8,128)(2,1)S(1)} %collective-permute-done.6.query_ref, bf16[128,2304]{1,0:T(8,128)(2,1)S(1)} %bitcast.10, bf16[128,2304]{1,0:T(8,128)(2,1)S(1)} %bitcast.16), custom_call_target="tpu_custom_call" | custom-call | flops 150994944 | bytes 1474560 | tf_op jit(solution)/shard_map/far/pallas_call | solution.py:128
  31.4 4.0 %collective-permute-start.7 = (bf16[128,1280]{1,0:T(8,128)(2,1)S(1)}, bf16[128,1280]{1,0:T(8,128)(2,1)S(1)}, u32[]{:S(2)}, u32[]{:S(2)}) collective-permute-start(bf16[128,1280]{1,0:T(8,128)(2,1)S(1)} %far.5), channel_id=1, source_target_pairs={{0,4},{1,5},{2,6},{3,7},{4,8},{5,9},{6,10},{7,11},{8,12},{9,13},{1... | collective-permute-start | bytes 983048 | tf_op jit(solution)/shard_map/ppermute | solution.py:146
  36.7 4.2 %far.4 = bf16[128,1280]{1,0:T(8,128)(2,1)S(1)} custom-call(s32[1,2]{1,0:T(1,128)S(1)} %collective-permute-done.flags_ref, bf16[128,1152]{1,0:T(8,128)(2,1)S(1)} %collective-permute-done.2.query_ref, bf16[128,2304]{1,0:T(8,128)(2,1)S(1)} %bitcast.11, bf16[128,2304]{1,0:T(8,128)(2,1)S(1)} %bitcast.17), custom_call_target="tpu_custom_call" | custom-call | flops 150994944 | bytes 1474560 | tf_op jit(solution)/shard_map/far/pallas_call | solution.py:128
  40.9 4.6 %collective-permute-start.3 = (bf16[128,1280]{1,0:T(8,128)(2,1)S(1)}, bf16[128,1280]{1,0:T(8,128)(2,1)S(1)}, u32[]{:S(2)}, u32[]{:S(2)}) collective-permute-start(bf16[128,1280]{1,0:T(8,128)(2,1)S(1)} %far.4), channel_id=1, source_target_pairs={{0,4},{1,5},{2,6},{3,7},{4,8},{5,9},{6,10},{7,11},{8,12},{9,13},{1... | collective-permute-start | bytes 983048 | tf_op jit(solution)/shard_map/ppermute | solution.py:146
  48.1 4.4 %near.5 = bf16[128,1280]{1,0:T(8,128)(2,1)S(1)} custom-call(s32[1,2]{1,0:T(1,128)S(1)} %collective-permute-done.flags_ref, bf16[128,1152]{1,0:T(8,128)(2,1)S(1)} %collective-permute-done.5.query_ref, bf16[128,2304]{1,0:T(8,128)(2,1)S(1)} %bitcast.12, bf16[128,2304]{1,0:T(8,128)(2,1)S(1)} %bitcast.18, bf16[128,1280]{1,0:T(8,128)(2,1)S(1)} %collective-permute-done.7.refs_0_), custom_call_target="tpu_custom_call" | custom-call | flops 150994944 | bytes 1474560 | tf_op jit(solution)/shard_map/near/pallas_call | solution.py:128
  52.6 5.3 %collective-permute-start.8 = (bf16[128,1280]{1,0:T(8,128)(2,1)S(1)}, bf16[128,1280]{1,0:T(8,128)(2,1)S(1)}, u32[]{:S(2)}, u32[]{:S(2)}) collective-permute-start(bf16[128,1280]{1,0:T(8,128)(2,1)S(1)} %near.5), channel_id=1, source_target_pairs={{0,4},{1,5},{2,6},{3,7},{4,8},{5,9},{6,10},{7,11},{8,12},{9,13},{1... | collective-permute-start | bytes 983048 | tf_op jit(solution)/shard_map/ppermute | solution.py:146
  57.9 4.4 %near.4 = bf16[128,1280]{1,0:T(8,128)(2,1)S(1)} custom-call(s32[1,2]{1,0:T(1,128)S(1)} %collective-permute-done.flags_ref, bf16[128,1152]{1,0:T(8,128)(2,1)S(1)} %collective-permute-done.1.query_ref, bf16[128,2304]{1,0:T(8,128)(2,1)S(1)} %bitcast.13, bf16[128,2304]{1,0:T(8,128)(2,1)S(1)} %bitcast.19, bf16[128,1280]{1,0:T(8,128)(2,1)S(1)} %collective-permute-done.3.refs_0_), custom_call_target="tpu_custom_call" | custom-call | flops 150994944 | bytes 1474560 | tf_op jit(solution)/shard_map/near/pallas_call | solution.py:128
  62.4 3.9 %collective-permute-start.4 = (bf16[128,1280]{1,0:T(8,128)(2,1)S(1)}, bf16[128,1280]{1,0:T(8,128)(2,1)S(1)}, u32[]{:S(2)}, u32[]{:S(2)}) collective-permute-start(bf16[128,1280]{1,0:T(8,128)(2,1)S(1)} %near.4), channel_id=1, source_target_pairs={{0,4},{1,5},{2,6},{3,7},{4,8},{5,9},{6,10},{7,11},{8,12},{9,13},{1... | collective-permute-start | bytes 983048 | tf_op jit(solution)/shard_map/ppermute | solution.py:146
  66.3 4.2 %far.7 = bf16[128,1280]{1,0:T(8,128)(2,1)S(1)} custom-call(s32[1,2]{1,0:T(1,128)S(1)} %collective-permute-done.flags_ref, bf16[128,1152]{1,0:T(8,128)(2,1)S(1)} %collective-permute-done.14.query_ref, bf16[128,2304]{1,0:T(8,128)(2,1)S(1)} %bitcast.22, bf16[128,2304]{1,0:T(8,128)(2,1)S(1)} %bitcast.28), custom_call_target="tpu_custom_call" | custom-call | flops 150994944 | bytes 1474560 | tf_op jit(solution)/shard_map/far/pallas_call | solution.py:128
  70.5 3.5 %collective-permute-start.15 = (bf16[128,1280]{1,0:T(8,128)(2,1)S(1)}, bf16[128,1280]{1,0:T(8,128)(2,1)S(1)}, u32[]{:S(2)}, u32[]{:S(2)}) collective-permute-start(bf16[128,1280]{1,0:T(8,128)(2,1)S(1)} %far.7), channel_id=1, source_target_pairs={{0,4},{1,5},{2,6},{3,7},{4,8},{5,9},{6,10},{7,11},{8,12},{9,13},{1... | collective-permute-start | bytes 983048 | tf_op jit(solution)/shard_map/ppermute | solution.py:146
  74.0 4.2 %far.6 = bf16[128,1280]{1,0:T(8,128)(2,1)S(1)} custom-call(s32[1,2]{1,0:T(1,128)S(1)} %collective-permute-done.flags_ref, bf16[128,1152]{1,0:T(8,128)(2,1)S(1)} %collective-permute-done.10.query_ref, bf16[128,2304]{1,0:T(8,128)(2,1)S(1)} %bitcast.23, bf16[128,2304]{1,0:T(8,128)(2,1)S(1)} %bitcast.29), custom_call_target="tpu_custom_call" | custom-call | flops 150994944 | bytes 1474560 | tf_op jit(solution)/shard_map/far/pallas_call | solution.py:128
  78.2 2.1 %collective-permute-start.11 = (bf16[128,1280]{1,0:T(8,128)(2,1)S(1)}, bf16[128,1280]{1,0:T(8,128)(2,1)S(1)}, u32[]{:S(2)}, u32[]{:S(2)}) collective-permute-start(bf16[128,1280]{1,0:T(8,128)(2,1)S(1)} %far.6), channel_id=1, source_target_pairs={{0,4},{1,5},{2,6},{3,7},{4,8},{5,9},{6,10},{7,11},{8,12},{9,13},{1... | collective-permute-start | bytes 983048 | tf_op jit(solution)/shard_map/ppermute | solution.py:146
  80.3 4.3 %own.4.refs_1_ = bf16[128,2304]{1,0:T(8,128)(2,1)S(1)} custom-call(s32[1,2]{1,0:T(1,128)S(1)} %copy-done.6, bf16[128,2304]{1,0:T(8,128)(2,1)S(1)} %bitcast.37, bf16[128,2304]{1,0:T(8,128)(2,1)S(1)} %bitcast.14, bf16[128,2304]{1,0:T(8,128)(2,1)S(1)} %bitcast.20, bf16[128,1280]{1,0:T(8,128)(2,1)S(1)} %collective-permute-done.8.refs_0_, ...), custom_call_target="tpu_custom_call", output_to_operand_aliasing={{}: (5, {})} | custom-call | flops 150994944 | bytes 1474560 | tf_op jit(solution)/shard_map/own/pallas_call | solution.py:128
  84.6 4.3 %own.5 = bf16[128,2304]{1,0:T(8,128)(2,1)S(1)} custom-call(s32[1,2]{1,0:T(1,128)S(1)} %copy-done.6, bf16[128,2304]{1,0:T(8,128)(2,1)S(1)} %bitcast.38, bf16[128,2304]{1,0:T(8,128)(2,1)S(1)} %bitcast.15, bf16[128,2304]{1,0:T(8,128)(2,1)S(1)} %bitcast.21, bf16[128,1280]{1,0:T(8,128)(2,1)S(1)} %collective-permute-done.4.refs_0_, ...), custom_call_target="tpu_custom_call", output_to_operand_aliasing={{}: (5, {})} | custom-call | flops 150994944 | bytes 1474560 | tf_op jit(solution)/shard_map/own/pallas_call | solution.py:128
  90.3 4.4 %near.7 = bf16[128,1280]{1,0:T(8,128)(2,1)S(1)} custom-call(s32[1,2]{1,0:T(1,128)S(1)} %collective-permute-done.flags_ref, bf16[128,1152]{1,0:T(8,128)(2,1)S(1)} %collective-permute-done.13.query_ref, bf16[128,2304]{1,0:T(8,128)(2,1)S(1)} %bitcast.24, bf16[128,2304]{1,0:T(8,128)(2,1)S(1)} %bitcast.30, bf16[128,1280]{1,0:T(8,128)(2,1)S(1)} %collective-permute-done.15.refs_0_), custom_call_target="tpu_custom_call" | custom-call | flops 150994944 | bytes 1474560 | tf_op jit(solution)/shard_map/near/pallas_call | solution.py:128
  96.7 4.4 %near.6 = bf16[128,1280]{1,0:T(8,128)(2,1)S(1)} custom-call(s32[1,2]{1,0:T(1,128)S(1)} %collective-permute-done.flags_ref, bf16[128,1152]{1,0:T(8,128)(2,1)S(1)} %collective-permute-done.9.query_ref, bf16[128,2304]{1,0:T(8,128)(2,1)S(1)} %bitcast.25, bf16[128,2304]{1,0:T(8,128)(2,1)S(1)} %bitcast.31, bf16[128,1280]{1,0:T(8,128)(2,1)S(1)} %collective-permute-done.11.refs_0_), custom_call_target="tpu_custom_call" | custom-call | flops 150994944 | bytes 1474560 | tf_op jit(solution)/shard_map/near/pallas_call | solution.py:128
  101.1 2.6 %collective-permute-start.12 = (bf16[128,1280]{1,0:T(8,128)(2,1)S(1)}, bf16[128,1280]{1,0:T(8,128)(2,1)}, u32[]{:S(2)}, u32[]{:S(2)}) collective-permute-start(bf16[128,1280]{1,0:T(8,128)(2,1)S(1)} %near.6), channel_id=1, source_target_pairs={{0,4},{1,5},{2,6},{3,7},{4,8},{5,9},{6,10},{7,11},{8,12},{9,13},{1... | collective-permute-start | bytes 983048 | tf_op jit(solution)/shard_map/ppermute | solution.py:146
  103.8 4.3 %own.6.refs_1_ = bf16[128,2304]{1,0:T(8,128)(2,1)S(1)} custom-call(s32[1,2]{1,0:T(1,128)S(1)} %copy-done.6, bf16[128,2304]{1,0:T(8,128)(2,1)S(1)} %bitcast.40, bf16[128,2304]{1,0:T(8,128)(2,1)S(1)} %bitcast.26, bf16[128,2304]{1,0:T(8,128)(2,1)S(1)} %bitcast.32, ...), custom_call_target="tpu_custom_call", output_to_operand_aliasing={{}: (5, {})} | custom-call | flops 150994944 | bytes 1474560 | tf_op jit(solution)/shard_map/own/pallas_call | solution.py:128
  108.1 3.0 %collective-permute-done.12.refs_0_ = bf16[128,1280]{1,0:T(8,128)(2,1)} collective-permute-done((bf16[128,1280]{1,0:T(8,128)(2,1)S(1)}, bf16[128,1280]{1,0:T(8,128)(2,1)}, u32[]{:S(2)}, u32[]{:S(2)}) %collective-permute-start.12) | collective-permute-done | bytes 327712 | tf_op jit(solution)/shard_map/ppermute | solution.py:146
  111.2 4.8 %own.7 = bf16[128,2304]{1,0:T(8,128)(2,1)S(1)} custom-call(s32[1,2]{1,0:T(1,128)S(1)} %copy-done.6, bf16[128,2304]{1,0:T(8,128)(2,1)S(1)} %bitcast.41, bf16[128,2304]{1,0:T(8,128)(2,1)S(1)} %bitcast.27, bf16[128,2304]{1,0:T(8,128)(2,1)S(1)} %bitcast.33, bf16[128,1280]{1,0:T(8,128)(2,1)} %collective-permute-done.12.refs_0_, ...), custom_call_target="tpu_custom_call", output_to_operand_aliasing={{}: (5, {})} | custom-call | flops 150994944 | bytes 1474560 | tf_op jit(solution)/shard_map/own/pallas_call | solution.py:128
  116.0 2.6 %collective-permute-start.17 = (bf16[1,128,2304]{2,1,0:T(8,128)(2,1)S(1)}, bf16[1,128,2304]{2,1,0:T(8,128)(2,1)S(1)}, u32[]{:S(2)}, u32[]{:S(2)}) collective-permute-start(bf16[1,128,2304]{2,1,0:T(8,128)(2,1)S(1)} %bitcast.34), channel_id=1, source_target_pairs={{0,16},{1,17},{2,18},{3,19},{4,20},{5,21},{6,22},{7,23},{8,24},{9,... | collective-permute-start | bytes 1769480 | tf_op jit(solution)/shard_map/ppermute | solution.py:146
  (46 shorter events, 19.2 us)
Async XLA Ops:
  0.6 21.6 %copy-start.5 = (bf16[1,128,2304]{2,1,0:T(8,128)(2,1)S(1)}, bf16[1,128,2304]{2,1,0:T(8,128)(2,1)}, u32[]{:S(2)}) copy-start(bf16[1,128,2304]{2,1,0:T(8,128)(2,1)} %param.7) | copy-start | bytes 1769476
  1.8 12.8 %collective-permute-start.5 = (bf16[128,1152]{1,0:T(8,128)(2,1)S(1)}, bf16[128,1152]{1,0:T(8,128)(2,1)S(1)}, u32[]{:S(2)}, u32[]{:S(2)}) collective-permute-start(bf16[128,1152]{1,0:T(8,128)(2,1)S(1)} %get-tuple-element.2), channel_id=1, source_target_pairs={{4,0},{5,1},{6,2},{7,3},{8,4},{9,5},{10,6},{11,7},{12,8},{13,9},{1... | collective-permute-start | bytes 884744 | tf_op jit(solution)/shard_map/ppermute | solution.py:146
  3.1 17.8 %collective-permute-start.1 = (bf16[128,1152]{1,0:T(8,128)(2,1)S(1)}, bf16[128,1152]{1,0:T(8,128)(2,1)S(1)}, u32[]{:S(2)}, u32[]{:S(2)}) collective-permute-start(bf16[128,1152]{1,0:T(8,128)(2,1)S(1)} %get-tuple-element.3), channel_id=1, source_target_pairs={{4,0},{5,1},{6,2},{7,3},{8,4},{9,5},{10,6},{11,7},{12,8},{13,9},{1... | collective-permute-start | bytes 884744 | tf_op jit(solution)/shard_map/ppermute | solution.py:146
  4.4 19.3 %collective-permute-start = (s32[1,2]{1,0:T(1,128)S(1)}, s32[1,2]{1,0:T(1,128)S(1)}, u32[]{:S(2)}, u32[]{:S(2)}) collective-permute-start(s32[1,2]{1,0:T(1,128)S(1)} %copy-done.6), channel_id=1, source_target_pairs={{4,0},{5,1},{6,2},{7,3},{8,4},{9,5},{10,6},{11,7},{12,8},{13,9},{1... | collective-permute-start | bytes 32 | tf_op jit(solution)/shard_map/ppermute | solution.py:146
  14.6 12.7 %collective-permute-start.6 = (bf16[128,1152]{1,0:T(8,128)(2,1)S(1)}, bf16[128,1152]{1,0:T(8,128)(2,1)S(1)}, u32[]{:S(2)}, u32[]{:S(2)}) collective-permute-start(bf16[128,1152]{1,0:T(8,128)(2,1)S(1)} %collective-permute-done.5.query_ref), channel_id=1, source_target_pairs={{4,0},{5,1},{6,2},{7,3},{8,4},{9,5},{10,6},{11,7},{12,8},{13,9},{1... | collective-permute-start | bytes 884744 | tf_op jit(solution)/shard_map/ppermute | solution.py:146
  20.9 15.8 %collective-permute-start.2 = (bf16[128,1152]{1,0:T(8,128)(2,1)S(1)}, bf16[128,1152]{1,0:T(8,128)(2,1)S(1)}, u32[]{:S(2)}, u32[]{:S(2)}) collective-permute-start(bf16[128,1152]{1,0:T(8,128)(2,1)S(1)} %collective-permute-done.1.query_ref), channel_id=1, source_target_pairs={{4,0},{5,1},{6,2},{7,3},{8,4},{9,5},{10,6},{11,7},{12,8},{13,9},{1... | collective-permute-start | bytes 884744 | tf_op jit(solution)/shard_map/ppermute | solution.py:146
  22.2 5.0 %copy-start = (bf16[1,128,2304]{2,1,0:T(8,128)(2,1)S(1)}, bf16[1,128,2304]{2,1,0:T(8,128)(2,1)}, u32[]{:S(2)}) copy-start(bf16[1,128,2304]{2,1,0:T(8,128)(2,1)} %param.11) | copy-start | bytes 1769476
  22.2 5.0 %copy-start.1 = (bf16[1,128,2304]{2,1,0:T(8,128)(2,1)S(1)}, bf16[1,128,2304]{2,1,0:T(8,128)(2,1)}, u32[]{:S(2)}) copy-start(bf16[1,128,2304]{2,1,0:T(8,128)(2,1)} %param.12) | copy-start | bytes 1769476
  22.3 23.2 %collective-permute-start.13 = (bf16[128,1152]{1,0:T(8,128)(2,1)S(1)}, bf16[128,1152]{1,0:T(8,128)(2,1)S(1)}, u32[]{:S(2)}, u32[]{:S(2)}) collective-permute-start(bf16[128,1152]{1,0:T(8,128)(2,1)S(1)} %get-tuple-element.4), channel_id=1, source_target_pairs={{4,0},{5,1},{6,2},{7,3},{8,4},{9,5},{10,6},{11,7},{12,8},{13,9},{1... | collective-permute-start | bytes 884744 | tf_op jit(solution)/shard_map/ppermute | solution.py:146
  31.4 16.7 %collective-permute-start.7 = (bf16[128,1280]{1,0:T(8,128)(2,1)S(1)}, bf16[128,1280]{1,0:T(8,128)(2,1)S(1)}, u32[]{:S(2)}, u32[]{:S(2)}) collective-permute-start(bf16[128,1280]{1,0:T(8,128)(2,1)S(1)} %far.5), channel_id=1, source_target_pairs={{0,4},{1,5},{2,6},{3,7},{4,8},{5,9},{6,10},{7,11},{8,12},{9,13},{1... | collective-permute-start | bytes 983048 | tf_op jit(solution)/shard_map/ppermute | solution.py:146
  35.4 11.4 %collective-permute-start.9 = (bf16[128,1152]{1,0:T(8,128)(2,1)S(1)}, bf16[128,1152]{1,0:T(8,128)(2,1)S(1)}, u32[]{:S(2)}, u32[]{:S(2)}) collective-permute-start(bf16[128,1152]{1,0:T(8,128)(2,1)S(1)} %get-tuple-element.5), channel_id=1, source_target_pairs={{4,0},{5,1},{6,2},{7,3},{8,4},{9,5},{10,6},{11,7},{12,8},{13,9},{1... | collective-permute-start | bytes 884744 | tf_op jit(solution)/shard_map/ppermute | solution.py:146
  40.9 17.0 %collective-permute-start.3 = (bf16[128,1280]{1,0:T(8,128)(2,1)S(1)}, bf16[128,1280]{1,0:T(8,128)(2,1)S(1)}, u32[]{:S(2)}, u32[]{:S(2)}) collective-permute-start(bf16[128,1280]{1,0:T(8,128)(2,1)S(1)} %far.4), channel_id=1, source_target_pairs={{0,4},{1,5},{2,6},{3,7},{4,8},{5,9},{6,10},{7,11},{8,12},{9,13},{1... | collective-permute-start | bytes 983048 | tf_op jit(solution)/shard_map/ppermute | solution.py:146
  45.5 20.8 %collective-permute-start.14 = (bf16[128,1152]{1,0:T(8,128)(2,1)S(1)}, bf16[128,1152]{1,0:T(8,128)(2,1)S(1)}, u32[]{:S(2)}, u32[]{:S(2)}) collective-permute-start(bf16[128,1152]{1,0:T(8,128)(2,1)S(1)} %collective-permute-done.13.query_ref), channel_id=1, source_target_pairs={{4,0},{5,1},{6,2},{7,3},{8,4},{9,5},{10,6},{11,7},{12,8},{13,9},{1... | collective-permute-start | bytes 884744 | tf_op jit(solution)/shard_map/ppermute | solution.py:146
  46.8 27.2 %collective-permute-start.10 = (bf16[128,1152]{1,0:T(8,128)(2,1)S(1)}, bf16[128,1152]{1,0:T(8,128)(2,1)S(1)}, u32[]{:S(2)}, u32[]{:S(2)}) collective-permute-start(bf16[128,1152]{1,0:T(8,128)(2,1)S(1)} %collective-permute-done.9.query_ref), channel_id=1, source_target_pairs={{4,0},{5,1},{6,2},{7,3},{8,4},{9,5},{10,6},{11,7},{12,8},{13,9},{1... | collective-permute-start | bytes 884744 | tf_op jit(solution)/shard_map/ppermute | solution.py:146
  52.5 13.8 %copy-start.2 = (bf16[1,128,2304]{2,1,0:T(8,128)(2,1)S(1)}, bf16[1,128,2304]{2,1,0:T(8,128)(2,1)}, u32[]{:S(2)}) copy-start(bf16[1,128,2304]{2,1,0:T(8,128)(2,1)} %param.8) | copy-start | bytes 1769476
  52.6 13.8 %copy-start.3 = (bf16[1,128,2304]{2,1,0:T(8,128)(2,1)S(1)}, bf16[1,128,2304]{2,1,0:T(8,128)(2,1)}, u32[]{:S(2)}) copy-start(bf16[1,128,2304]{2,1,0:T(8,128)(2,1)} %param.9) | copy-start | bytes 1769476
  52.6 27.7 %collective-permute-start.8 = (bf16[128,1280]{1,0:T(8,128)(2,1)S(1)}, bf16[128,1280]{1,0:T(8,128)(2,1)S(1)}, u32[]{:S(2)}, u32[]{:S(2)}) collective-permute-start(bf16[128,1280]{1,0:T(8,128)(2,1)S(1)} %near.5), channel_id=1, source_target_pairs={{0,4},{1,5},{2,6},{3,7},{4,8},{5,9},{6,10},{7,11},{8,12},{9,13},{1... | collective-permute-start | bytes 983048 | tf_op jit(solution)/shard_map/ppermute | solution.py:146
  62.4 22.3 %collective-permute-start.4 = (bf16[128,1280]{1,0:T(8,128)(2,1)S(1)}, bf16[128,1280]{1,0:T(8,128)(2,1)S(1)}, u32[]{:S(2)}, u32[]{:S(2)}) collective-permute-start(bf16[128,1280]{1,0:T(8,128)(2,1)S(1)} %near.4), channel_id=1, source_target_pairs={{0,4},{1,5},{2,6},{3,7},{4,8},{5,9},{6,10},{7,11},{8,12},{9,13},{1... | collective-permute-start | bytes 983048 | tf_op jit(solution)/shard_map/ppermute | solution.py:146
  70.5 19.8 %collective-permute-start.15 = (bf16[128,1280]{1,0:T(8,128)(2,1)S(1)}, bf16[128,1280]{1,0:T(8,128)(2,1)S(1)}, u32[]{:S(2)}, u32[]{:S(2)}) collective-permute-start(bf16[128,1280]{1,0:T(8,128)(2,1)S(1)} %far.7), channel_id=1, source_target_pairs={{0,4},{1,5},{2,6},{3,7},{4,8},{5,9},{6,10},{7,11},{8,12},{9,13},{1... | collective-permute-start | bytes 983048 | tf_op jit(solution)/shard_map/ppermute | solution.py:146
  78.2 18.5 %collective-permute-start.11 = (bf16[128,1280]{1,0:T(8,128)(2,1)S(1)}, bf16[128,1280]{1,0:T(8,128)(2,1)S(1)}, u32[]{:S(2)}, u32[]{:S(2)}) collective-permute-start(bf16[128,1280]{1,0:T(8,128)(2,1)S(1)} %far.6), channel_id=1, source_target_pairs={{0,4},{1,5},{2,6},{3,7},{4,8},{5,9},{6,10},{7,11},{8,12},{9,13},{1... | collective-permute-start | bytes 983048 | tf_op jit(solution)/shard_map/ppermute | solution.py:146
  89.0 29.7 %collective-permute-start.18 = (bf16[1,128,2304]{2,1,0:T(8,128)(2,1)S(1)}, bf16[1,128,2304]{2,1,0:T(8,128)(2,1)}, u32[]{:S(2)}, u32[]{:S(2)}) collective-permute-start(bf16[1,128,2304]{2,1,0:T(8,128)(2,1)S(1)} %bitcast.35), channel_id=1, source_target_pairs={{16,0},{17,1},{18,2},{19,3},{20,4},{21,5},{22,6},{23,7},{24,8},{25... | collective-permute-start | bytes 1769480 | tf_op jit(solution)/shard_map/ppermute | solution.py:146
  94.7 9.0 %collective-permute-start.16 = (bf16[128,1280]{1,0:T(8,128)(2,1)S(1)}, bf16[128,1280]{1,0:T(8,128)(2,1)S(1)}, u32[]{:S(2)}, u32[]{:S(2)}) collective-permute-start(bf16[128,1280]{1,0:T(8,128)(2,1)S(1)} %near.7), channel_id=1, source_target_pairs={{0,4},{1,5},{2,6},{3,7},{4,8},{5,9},{6,10},{7,11},{8,12},{9,13},{1... | collective-permute-start | bytes 983048 | tf_op jit(solution)/shard_map/ppermute | solution.py:146
  101.1 10.1 %collective-permute-start.12 = (bf16[128,1280]{1,0:T(8,128)(2,1)S(1)}, bf16[128,1280]{1,0:T(8,128)(2,1)}, u32[]{:S(2)}, u32[]{:S(2)}) collective-permute-start(bf16[128,1280]{1,0:T(8,128)(2,1)S(1)} %near.6), channel_id=1, source_target_pairs={{0,4},{1,5},{2,6},{3,7},{4,8},{5,9},{6,10},{7,11},{8,12},{9,13},{1... | collective-permute-start | bytes 983048 | tf_op jit(solution)/shard_map/ppermute | solution.py:146
  116.0 4.6 %collective-permute-start.17 = (bf16[1,128,2304]{2,1,0:T(8,128)(2,1)S(1)}, bf16[1,128,2304]{2,1,0:T(8,128)(2,1)S(1)}, u32[]{:S(2)}, u32[]{:S(2)}) collective-permute-start(bf16[1,128,2304]{2,1,0:T(8,128)(2,1)S(1)} %bitcast.34), channel_id=1, source_target_pairs={{0,16},{1,17},{2,18},{3,19},{4,20},{5,21},{6,22},{7,23},{8,24},{9,... | collective-permute-start | bytes 1769480 | tf_op jit(solution)/shard_map/ppermute | solution.py:146
  (2 other events, 4.8 us)

commit v2 on v0

v2 whole, which is shorter than its diff:
```python
import functools
import math

import jax
import jax.numpy as jnp
from jax import lax
from jax.experimental import pallas as pl
from jax.experimental.pallas import tpu as pltpu
from jax.sharding import PartitionSpec as P

HEAD_DIM = 64
BLOCK = 128
TILE = 2 * HEAD_DIM
FIELD = 21
ABSENT = -1e30
WEIGHT = 30
FACTOR = math.log2(math.e) / math.sqrt(HEAD_DIM)
FAR, NEAR, BOTH, OWN = range(4)


def iota(shape, dimension):
    return lax.broadcasted_iota(jnp.int32, shape, dimension)


def by_head(tile, low):
    zero = jnp.zeros_like(tile)
    return jnp.concatenate([jnp.where(low, tile, zero), jnp.where(low, zero, tile)], 0)


def pieces(x, count):
    found = []
    for _ in range(count):
        found.append(x.astype(jnp.bfloat16).astype(jnp.float32))
        x = x - found[-1]
    return found


def fields(parts, tiles):
    within = iota((BLOCK, TILE), 1) % HEAD_DIM < tiles
    packed = jnp.where(within, parts[0], 0.0)
    for place, part in enumerate(parts[1:], 1):
        packed = packed + pltpu.roll(jnp.where(within, part, 0.0), place * FIELD, 1)
    return packed.astype(jnp.bfloat16)


def field_sum(packed, start, count):
    packed = packed.astype(jnp.float32)
    return sum(
        packed if i == 0 else pltpu.roll(packed, TILE - i * FIELD, 1) for i in range(start, start + count)
    )


def spreader():
    row, column = iota((TILE, 2 * TILE), 0), iota((TILE, 2 * TILE), 1)
    place = row % HEAD_DIM
    same = (row // HEAD_DIM == (column // HEAD_DIM) % 2) & (place < 2 * FIELD)
    return jnp.where(same & (column < TILE), place % FIELD, -1).astype(jnp.int16)


def share(query, key, value, low, heads, causal=None):
    scores = lax.dot_general(
        query, by_head(key, low), (((1,), (1,)), ((), ())), preferred_element_type=jnp.float32
    ) * FACTOR
    weights, tops = [], []
    for half in (scores[:, :BLOCK], scores[:, BLOCK:]):
        if causal is not None:
            half = jnp.where(causal, half, ABSENT)
        tops.append(jnp.max(half, -1, keepdims=True))
        weights.append(jnp.exp2(half - tops[-1]).astype(jnp.bfloat16))
    sums = jnp.dot(
        jnp.concatenate(weights, 1),
        jnp.concatenate([by_head(value, low), heads], 1),
        preferred_element_type=jnp.float32,
    )
    return sums[:, :TILE], sums[:, TILE:], tops


def kernel(tiles, first, part, *refs):
    query_ref, key_ref, value_ref, *refs = refs
    width = tiles * TILE
    if part in (NEAR, OWN):
        other_ref, flags_ref, *refs = refs
    elif part == BOTH:
        far_pair_ref, flags_ref, *refs = refs
    if part != FAR:
        sums_ref = refs.pop()
    if part == BOTH:
        far_ref = refs.pop()
    out_ref = refs[-1]
    lane = iota((BLOCK, TILE), 1)
    low = lane < HEAD_DIM
    place = lane % HEAD_DIM
    low16 = lax.broadcasted_iota(jnp.int16, (BLOCK, TILE), 1) < HEAD_DIM
    heads = by_head(jnp.ones((BLOCK, TILE), jnp.bfloat16), low16)
    causal = iota((BLOCK, BLOCK), 0) >= iota((BLOCK, BLOCK), 1) if part == OWN else None
    top = total = far_top = far_total = jnp.zeros((BLOCK, TILE), jnp.float32)
    for j in range(tiles):
        columns = slice(j * TILE, (j + 1) * TILE)
        there = slice((first + j) * TILE, (first + j + 1) * TILE)
        query = query_ref[:, there if part == OWN else columns]
        sums, totals, tops = share(query, key_ref[:, there], value_ref[:, there], low16, heads, causal)
        top = jnp.where(place == j, jnp.where(low, tops[0], tops[1]), top)
        total = jnp.where(place == j, totals, total)
        if part == FAR:
            out_ref[:, columns] = (sums / totals).astype(jnp.bfloat16)
        else:
            sums_ref[:, columns] = sums
        if part == BOTH:
            sums, totals, tops = share(query, far_pair_ref[:BLOCK, columns], far_pair_ref[BLOCK:, columns], low16, heads)
            far_top = jnp.where(place == j, jnp.where(low, tops[0], tops[1]), far_top)
            far_total = jnp.where(place == j, totals, far_total)
            far_ref[:, columns] = sums
    if part != FAR:
        near, far = flags_ref[0:1, :] > 0, flags_ref[1:2, :] > 0
        if part != BOTH:
            far_ref = other_ref
            far_top, far_total = field_sum(other_ref[:, width:], 0, 3), 1.0
        far_top = jnp.where(near | far if part == OWN else far, far_top, ABSENT)
        if part != OWN:
            top = jnp.where(near, top, ABSENT)
        most = jnp.maximum(top, far_top)
        here, there = jnp.exp2(top - most), jnp.exp2(far_top - most)
        top, total = most, here * total + there * far_total
        spread = spreader()
        here, there = fields(pieces(here / total, 2), tiles), fields(pieces(there / total, 2), tiles)
        for j in range(tiles):
            columns = slice(j * TILE, (j + 1) * TILE)
            pick = jnp.where(spread[:, :TILE] == j, 1.0, 0.0).astype(jnp.bfloat16)
            both = jnp.dot(jnp.concatenate([here, there], 0), pick, preferred_element_type=jnp.float32)
            result = both[:BLOCK] * sums_ref[:, columns]
            result = result + both[BLOCK:] * far_ref[:, columns].astype(jnp.float32)
            if part == OWN:
                columns = slice((first + j) * TILE, (first + j + 1) * TILE)
            out_ref[:, columns] = result.astype(jnp.bfloat16)
    if part != OWN:
        out_ref[:, width:] = fields(pieces(top + jnp.log2(total), 3), tiles)


def attend(part, tiles, first, query, key, value, *others):
    width = tiles * TILE
    operands = (query, key, value) + others
    out_shape = key.shape if part == OWN else (BLOCK, width + TILE)
    in_vmem = pl.BlockSpec(memory_space=pltpu.VMEM)
    return pl.pallas_call(
        functools.partial(kernel, tiles, first, part),
        out_shape=jax.ShapeDtypeStruct(out_shape, jnp.bfloat16),
        in_specs=[in_vmem] * len(operands),
        out_specs=in_vmem,
        scratch_shapes=[pltpu.VMEM((BLOCK, width), jnp.float32)] * (0, 1, 2, 1)[part],
        input_output_aliases={len(operands) - 1: 0} if part == OWN and first else {},
        name=("far", "near", "both", "own")[part],
        compiler_params=pltpu.CompilerParams(vmem_limit_bytes=16 * 1024 * 1024),
        cost_estimate=pl.CostEstimate(
            flops=tiles * 8 * BLOCK * BLOCK * TILE * WEIGHT,
            bytes_accessed=5 * BLOCK * width * 2,
            transcendentals=tiles * 2 * BLOCK * BLOCK,
        ),
    )(*operands)


def shifted(block, axis, distance):
    devices = range(lax.axis_size(axis))
    route = [(i - distance, i) for i in devices if i - distance in devices]
    return lax.ppermute(block, axis, route)


def stays(below, above):
    section, size = lax.axis_index("section"), lax.axis_size("section")
    here = jnp.where(section == size - 1, below, above)
    if size > 2:
        here = jnp.where((section == size - 1) | (section == 0), here, shifted(below, "section", 1))
    return here


def crosses(below, above):
    section, size = lax.axis_index("section"), lax.axis_size("section")
    if size == 2:
        return lax.ppermute(jnp.where(section == size - 1, above, below), "section", [(0, 1), (1, 0)])
    return jnp.where(section == size - 1, shifted(below, "section", 1), shifted(above, "section", -1))


def after(x, *others):
    return lax.optimization_barrier((x, *others))[0]


def on_device(down_queries, down_keys, down_values, up_queries, up_keys, up_values, key_blocks):
    spacing = lax.axis_size("ctx") // 4
    onward = lambda x: shifted(x, "ctx", -spacing)
    back = lambda x: shifted(x, "ctx", spacing)
    pairs = tuple((d[0], u[0]) for d, u in ((down_queries, up_queries), (down_keys, up_keys), (down_values, up_values)))
    count = down_queries.shape[2] // TILE
    half = count // 2
    spread_flags = lambda x: jnp.broadcast_to(jnp.where(x >= 0, 1.0, 0.0).astype(jnp.float32).reshape(2, 1), (2, TILE))

    key, value = stays(*pairs[1]), stays(*pairs[2])
    far = back(jnp.concatenate([key, value], 0))
    query2 = crosses(*pairs[0])
    query = stays(*pairs[0])
    key2, value2 = crosses(*pairs[1]), crosses(*pairs[2])
    once_a = onward(query2[:, : half * TILE])
    once_b = onward(query2[:, half * TILE :])
    twice_a = onward(once_a)
    twice_b = onward(after(once_b, once_a))
    once = onward(after(query, once_b))
    flags = spread_flags(key_blocks)
    next_blocks = onward(key_blocks)

    far_a = attend(FAR, half, 0, twice_a, key2, value2)
    back_a = back(far_a)
    far_b = attend(FAR, count - half, half, after(twice_b, far_a, far), key2, value2)
    back_b = back(far_b)
    next_flags = spread_flags(after(next_blocks, far_b))
    near_a = attend(NEAR, half, 0, once_a, key2, value2, after(back_a, far_b), next_flags)
    done_a = back(near_a)
    near_b = attend(NEAR, count - half, half, once_b, key2, value2, after(back_b, near_a), next_flags)
    done_b = back(near_b)
    near = attend(BOTH, count, 0, after(once, near_b), key, value, far, next_flags)
    done = back(near)
    out2 = attend(OWN, half, 0, query2, key2, value2, after(done_a, near), flags)
    out2 = attend(OWN, count - half, half, query2, key2, value2, done_b, flags, out2)
    out = attend(OWN, count, 0, query, key, value, after(done, out2), flags)

    at_end = lax.axis_index("section") == lax.axis_size("section") - 1
    forward = jnp.where(at_end, out2, out)
    handed = jnp.where(at_end, out, out2)
    return forward[None], handed[None]


def solution(mesh):
    placed = (P("section", "ctx", None),) * 6 + (P("ctx", None),)
    return jax.shard_map(
        on_device,
        mesh=mesh,
        in_specs=placed,
        out_specs=(P("section", "ctx", None), P("section", "ctx", None)),
        check_vma=False,
    )
```

time: 204 us -> 80.6 us (0.40)
  the two profiles are of different devices: /device:TPU:25 before, /device:TPU:0 now
where the time goes in v2:
time: 80.6 us; the launch traced here: 80.2 us
  starting transfers between devices  33.3 us (41%)
  waiting for transfers between devices  32.8 us (41%)
  Pallas kernels  9.66 us (12%)
  other arithmetic  2.75 us (3%)
  between operations  0.93 us (1%)
    ppermute x12, waiting for transfers between devices, shifted(): return lax.ppermute(block, axis, route)  32.8 us
    ppermute x12, starting transfers between devices, shifted(): return lax.ppermute(block, axis, route)  32.2 us
    pallas_call x8, Pallas kernels, attend(): pl.pallas_call(functools.partial(kernel, tiles, first, part), out_shape=j...  9.66 us
  transfers between devices with their start and end apart: 15, of which 7 were waited for; matrix products, arithmetic and copies ran while one was open for 1% of the time, Pallas kernels for 10%

profile of v2, /device:TPU:0, one launch (start us, length us, event | category | flops | bytes accessed | tf_op | source)
XLA Modules:
  0.0 80.2 jit_solution(5769206209947347320)
XLA Ops:
  0.7 1.4 %select_bitcast_fusion.2 = (bf16[128,2304]{1,0:T(8,128)(2,1)S(1)}, bf16[128,2304]{1,0:T(8,128)(2,1)S(1)}) fusion(bf16[1,128,2304]{2,1,0:T(8,128)(2,1)} %param.7, bf16[1,128,2304]{2,1,0:T(8,128)(2,1)} %param.10, pred[]{:T(512)S(6)} %eq.2), kind=kLoop, calls=%fused_computation.3 | loop fusion | flops 589824 | bytes 2359297 | tf_op jit(solution)/shard_map/jit(_where)/select_n | solution.py:169
  4.1 4.6 %collective-permute-start.7 = (bf16[256,2304]{1,0:T(8,128)(2,1)S(1)}, bf16[256,2304]{1,0:T(8,128)(2,1)S(1)}, u32[]{:S(2)}, u32[]{:S(2)}) collective-permute-start(bf16[256,2304]{1,0:T(8,128)(2,1)S(1)} %pad_maximum_fusion), channel_id=1, source_target_pairs={{0,4},{1,5},{2,6},{3,7},{4,8},{5,9},{6,10},{7,11},{8,12},{9,13},{1... | collective-permute-start | bytes 3538952 | tf_op jit(solution)/shard_map/ppermute | solution.py:164
  8.7 1.3 %collective-permute-start.4 = (bf16[128,1152]{1,0:T(8,128)(2,1)S(1)}, bf16[128,1152]{1,0:T(8,128)(2,1)S(1)}, u32[]{:S(2)}, u32[]{:S(2)}) collective-permute-start(bf16[128,1152]{1,0:T(8,128)(2,1)S(1)} %get-tuple-element.28), channel_id=1, source_target_pairs={{4,0},{5,1},{6,2},{7,3},{8,4},{9,5},{10,6},{11,7},{12,8},{13,9},{1... | collective-permute-start | bytes 884744 | tf_op jit(solution)/shard_map/ppermute | solution.py:164
  10.0 1.3 %collective-permute-start.3 = (bf16[128,1152]{1,0:T(8,128)(2,1)S(1)}, bf16[128,1152]{1,0:T(8,128)(2,1)S(1)}, u32[]{:S(2)}, u32[]{:S(2)}) collective-permute-start(bf16[128,1152]{1,0:T(8,128)(2,1)S(1)} %get-tuple-element.29), channel_id=1, source_target_pairs={{4,0},{5,1},{6,2},{7,3},{8,4},{9,5},{10,6},{11,7},{12,8},{13,9},{1... | collective-permute-start | bytes 884744 | tf_op jit(solution)/shard_map/ppermute | solution.py:164
  11.3 9.1 %collective-permute-done.4.refs_0_ = bf16[128,1152]{1,0:T(8,128)(2,1)S(1)} collective-permute-done((bf16[128,1152]{1,0:T(8,128)(2,1)S(1)}, bf16[128,1152]{1,0:T(8,128)(2,1)S(1)}, u32[]{:S(2)}, u32[]{:S(2)}) %collective-permute-start.4) | collective-permute-done | bytes 294944 | tf_op jit(solution)/shard_map/ppermute | solution.py:164
  20.4 1.3 %collective-permute-start.6 = (bf16[128,1152]{1,0:T(8,128)(2,1)S(1)}, bf16[128,1152]{1,0:T(8,128)(2,1)S(1)}, u32[]{:S(2)}, u32[]{:S(2)}) collective-permute-start(bf16[128,1152]{1,0:T(8,128)(2,1)S(1)} %collective-permute-done.4.refs_0_), channel_id=1, source_target_pairs={{4,0},{5,1},{6,2},{7,3},{8,4},{9,5},{10,6},{11,7},{12,8},{13,9},{1... | collective-permute-start | bytes 884744 | tf_op jit(solution)/shard_map/ppermute | solution.py:164
  21.7 5.0 %collective-permute-done.3.refs_0_ = bf16[128,1152]{1,0:T(8,128)(2,1)S(1)} collective-permute-done((bf16[128,1152]{1,0:T(8,128)(2,1)S(1)}, bf16[128,1152]{1,0:T(8,128)(2,1)S(1)}, u32[]{:S(2)}, u32[]{:S(2)}) %collective-permute-start.3) | collective-permute-done | bytes 294944 | tf_op jit(solution)/shard_map/ppermute | solution.py:164
  26.8 1.3 %collective-permute-start.10 = (s32[1,2]{1,0:T(1,128)S(1)}, s32[1,2]{1,0:T(1,128)S(1)}, u32[]{:S(2)}, u32[]{:S(2)}) collective-permute-start(s32[1,2]{1,0:T(1,128)S(1)} %copy-done.4), channel_id=1, source_target_pairs={{4,0},{5,1},{6,2},{7,3},{8,4},{9,5},{10,6},{11,7},{12,8},{13,9},{1... | collective-permute-start | bytes 32 | tf_op jit(solution)/shard_map/ppermute | solution.py:164
  28.0 1.3 %collective-permute-start.5 = (bf16[128,1152]{1,0:T(8,128)(2,1)S(1)}, bf16[128,1152]{1,0:T(8,128)(2,1)S(1)}, u32[]{:S(2)}, u32[]{:S(2)}) collective-permute-start(bf16[128,1152]{1,0:T(8,128)(2,1)S(1)} %collective-permute-done.3.refs_0_), channel_id=1, source_target_pairs={{4,0},{5,1},{6,2},{7,3},{8,4},{9,5},{10,6},{11,7},{12,8},{13,9},{1... | collective-permute-start | bytes 884744 | tf_op jit(solution)/shard_map/ppermute | solution.py:164
  29.4 1.3 %collective-permute-start.13 = (bf16[128,2304]{1,0:T(8,128)(2,1)S(1)}, bf16[128,2304]{1,0:T(8,128)(2,1)S(1)}, u32[]{:S(2)}, u32[]{:S(2)}) collective-permute-start(bf16[128,2304]{1,0:T(8,128)(2,1)S(1)} %get-tuple-element.16.refs_0_), channel_id=1, source_target_pairs={{4,0},{5,1},{6,2},{7,3},{8,4},{9,5},{10,6},{11,7},{12,8},{13,9},{1... | collective-permute-start | bytes 1769480 | tf_op jit(solution)/shard_map/ppermute | solution.py:164
  30.7 2.1 %collective-permute-done.6.refs_0_ = bf16[128,1152]{1,0:T(8,128)(2,1)S(1)} collective-permute-done((bf16[128,1152]{1,0:T(8,128)(2,1)S(1)}, bf16[128,1152]{1,0:T(8,128)(2,1)S(1)}, u32[]{:S(2)}, u32[]{:S(2)}) %collective-permute-start.6) | collective-permute-done | bytes 294944 | tf_op jit(solution)/shard_map/ppermute | solution.py:164
  33.6 3.7 %collective-permute-start.9 = (bf16[128,1280]{1,0:T(8,128)(2,1)S(1)}, bf16[128,1280]{1,0:T(8,128)(2,1)S(1)}, u32[]{:S(2)}, u32[]{:S(2)}) collective-permute-start(bf16[128,1280]{1,0:T(8,128)(2,1)S(1)} %far.2), channel_id=1, source_target_pairs={{0,4},{1,5},{2,6},{3,7},{4,8},{5,9},{6,10},{7,11},{8,12},{9,13},{1... | collective-permute-start | bytes 983048 | tf_op jit(solution)/shard_map/ppermute | solution.py:164
  37.3 3.2 %collective-permute-done.5.refs_0_ = bf16[128,1152]{1,0:T(8,128)(2,1)S(1)} collective-permute-done((bf16[128,1152]{1,0:T(8,128)(2,1)S(1)}, bf16[128,1152]{1,0:T(8,128)(2,1)S(1)}, u32[]{:S(2)}, u32[]{:S(2)}) %collective-permute-start.5) | collective-permute-done | bytes 294944 | tf_op jit(solution)/shard_map/ppermute | solution.py:164
  41.3 3.9 %collective-permute-start.8 = (bf16[128,1280]{1,0:T(8,128)(2,1)S(1)}, bf16[128,1280]{1,0:T(8,128)(2,1)S(1)}, u32[]{:S(2)}, u32[]{:S(2)}) collective-permute-start(bf16[128,1280]{1,0:T(8,128)(2,1)S(1)} %far.3), channel_id=1, source_target_pairs={{0,4},{1,5},{2,6},{3,7},{4,8},{5,9},{6,10},{7,11},{8,12},{9,13},{1... | collective-permute-start | bytes 983048 | tf_op jit(solution)/shard_map/ppermute | solution.py:164
  45.4 1.1 %near.2 = bf16[128,1280]{1,0:T(8,128)(2,1)S(1)} custom-call(bf16[128,1152]{1,0:T(8,128)(2,1)S(1)} %collective-permute-done.4.refs_0_, bf16[128,2304]{1,0:T(8,128)(2,1)S(1)} %collective-permute-done.1.refs_1_, bf16[128,2304]{1,0:T(8,128)(2,1)S(1)} %collective-permute-done.2.refs_2_, bf16[128,1280]{1,0:T(8,128)(2,1)S(1)} %collective-permute-done.9.refs_3_, ...), custom_call_target="tpu_custom_call" | custom-call | flops 4529848320 | bytes 1474560 | tf_op jit(solution)/shard_map/near/pallas_call | solution.py:144
  46.4 4.4 %collective-permute-start.12 = (bf16[128,1280]{1,0:T(8,128)(2,1)S(1)}, bf16[128,1280]{1,0:T(8,128)(2,1)S(1)}, u32[]{:S(2)}, u32[]{:S(2)}) collective-permute-start(bf16[128,1280]{1,0:T(8,128)(2,1)S(1)} %near.2), channel_id=1, source_target_pairs={{0,4},{1,5},{2,6},{3,7},{4,8},{5,9},{6,10},{7,11},{8,12},{9,13},{1... | collective-permute-start | bytes 983048 | tf_op jit(solution)/shard_map/ppermute | solution.py:164
  50.9 2.5 %collective-permute-done.8.refs_3_ = bf16[128,1280]{1,0:T(8,128)(2,1)S(1)} collective-permute-done((bf16[128,1280]{1,0:T(8,128)(2,1)S(1)}, bf16[128,1280]{1,0:T(8,128)(2,1)S(1)}, u32[]{:S(2)}, u32[]{:S(2)}) %collective-permute-start.8) | collective-permute-done | bytes 327712 | tf_op jit(solution)/shard_map/ppermute | solution.py:164
  54.5 4.4 %collective-permute-start.11 = (bf16[128,1280]{1,0:T(8,128)(2,1)S(1)}, bf16[128,1280]{1,0:T(8,128)(2,1)S(1)}, u32[]{:S(2)}, u32[]{:S(2)}) collective-permute-start(bf16[128,1280]{1,0:T(8,128)(2,1)S(1)} %near.3), channel_id=1, source_target_pairs={{0,4},{1,5},{2,6},{3,7},{4,8},{5,9},{6,10},{7,11},{8,12},{9,13},{1... | collective-permute-start | bytes 983048 | tf_op jit(solution)/shard_map/ppermute | solution.py:164
  58.9 2.3 %both.1 = bf16[128,2432]{1,0:T(8,128)(2,1)S(1)} custom-call(bf16[128,2304]{1,0:T(8,128)(2,1)S(1)} %collective-permute-done.13.refs_0_, bf16[128,2304]{1,0:T(8,128)(2,1)S(1)} %get-tuple-element.24.refs_1_, bf16[128,2304]{1,0:T(8,128)(2,1)S(1)} %get-tuple-element.26.refs_2_, bf16[256,2304]{1,0:T(8,128)(2,1)S(1)} %collective-permute-done.7.refs_3_, ...), custom_call_target="tpu_custom_call" | custom-call | flops 9059696640 | bytes 2949120 | tf_op jit(solution)/shard_map/both/pallas_call | solution.py:144
  61.2 3.4 %collective-permute-start.14 = (bf16[128,2432]{1,0:T(8,128)(2,1)S(1)}, bf16[128,2432]{1,0:T(8,128)(2,1)S(1)}, u32[]{:S(2)}, u32[]{:S(2)}) collective-permute-start(bf16[128,2432]{1,0:T(8,128)(2,1)S(1)} %both.1), channel_id=1, source_target_pairs={{0,4},{1,5},{2,6},{3,7},{4,8},{5,9},{6,10},{7,11},{8,12},{9,13},{1... | collective-permute-start | bytes 1867784 | tf_op jit(solution)/shard_map/ppermute | solution.py:164
  65.7 1.7 %collective-permute-done.11.refs_3_ = bf16[128,1280]{1,0:T(8,128)(2,1)S(1)} collective-permute-done((bf16[128,1280]{1,0:T(8,128)(2,1)S(1)}, bf16[128,1280]{1,0:T(8,128)(2,1)S(1)}, u32[]{:S(2)}, u32[]{:S(2)}) %collective-permute-start.11) | collective-permute-done | bytes 327712 | tf_op jit(solution)/shard_map/ppermute | solution.py:164
  68.4 9.0 %collective-permute-done.14.refs_3_ = bf16[128,2432]{1,0:T(8,128)(2,1)S(1)} collective-permute-done((bf16[128,2432]{1,0:T(8,128)(2,1)S(1)}, bf16[128,2432]{1,0:T(8,128)(2,1)S(1)}, u32[]{:S(2)}, u32[]{:S(2)}) %collective-permute-start.14) | collective-permute-done | bytes 622624 | tf_op jit(solution)/shard_map/ppermute | solution.py:164
  77.5 1.6 %own.5 = bf16[128,2304]{1,0:T(8,128)(2,1)S(1)} custom-call(bf16[128,2304]{1,0:T(8,128)(2,1)S(1)} %get-tuple-element.16.refs_0_, bf16[128,2304]{1,0:T(8,128)(2,1)S(1)} %get-tuple-element.24.refs_1_, bf16[128,2304]{1,0:T(8,128)(2,1)S(1)} %get-tuple-element.26.refs_2_, bf16[128,2432]{1,0:T(8,128)(2,1)S(1)} %collective-permute-done.14.refs_3_, ...), custom_call_target="tpu_custom_call" | custom-call | flops 9059696640 | bytes 2949120 | tf_op jit(solution)/shard_map/own/pallas_call | solution.py:144
  79.1 1.1 %select_bitcast_fusion = (bf16[1,128,2304]{2,1,0:T(8,128)(2,1)}, bf16[1,128,2304]{2,1,0:T(8,128)(2,1)}) fusion(bf16[128,2304]{1,0:T(8,128)(2,1)S(1)} %own.5, bf16[128,2304]{1,0:T(8,128)(2,1)S(1)} %own.4, pred[]{:T(512)S(6)} %eq.2), kind=kLoop, calls=%fused_computation.1 | loop fusion | flops 589824 | bytes 2359297 | tf_op jit(solution)/shard_map/broadcast_in_dim | solution.py:226
  (34 shorter events, 6.8 us)
Async XLA Ops:
  0.6 2.0 %copy-start = (bf16[1,128,2304]{2,1,0:T(8,128)(2,1)S(1)}, bf16[1,128,2304]{2,1,0:T(8,128)(2,1)}, u32[]{:S(2)}) copy-start(bf16[1,128,2304]{2,1,0:T(8,128)(2,1)} %param.8) | copy-start | bytes 1769476
  0.6 2.0 %copy-start.1 = (bf16[1,128,2304]{2,1,0:T(8,128)(2,1)S(1)}, bf16[1,128,2304]{2,1,0:T(8,128)(2,1)}, u32[]{:S(2)}) copy-start(bf16[1,128,2304]{2,1,0:T(8,128)(2,1)} %param.11) | copy-start | bytes 1769476
  2.1 1.1 %copy-start.2 = (bf16[1,128,2304]{2,1,0:T(8,128)(2,1)S(1)}, bf16[1,128,2304]{2,1,0:T(8,128)(2,1)}, u32[]{:S(2)}) copy-start(bf16[1,128,2304]{2,1,0:T(8,128)(2,1)} %param.9) | copy-start | bytes 1769476
  2.1 1.3 %copy-start.3 = (bf16[1,128,2304]{2,1,0:T(8,128)(2,1)S(1)}, bf16[1,128,2304]{2,1,0:T(8,128)(2,1)}, u32[]{:S(2)}) copy-start(bf16[1,128,2304]{2,1,0:T(8,128)(2,1)} %param.12) | copy-start | bytes 1769476
  2.1 6.5 %collective-permute-start = (bf16[128,2304]{1,0:T(8,128)(2,1)S(1)}, bf16[128,2304]{1,0:T(8,128)(2,1)S(1)}, u32[]{:S(2)}, u32[]{:S(2)}) collective-permute-start(bf16[128,2304]{1,0:T(8,128)(2,1)S(1)} %get-tuple-element.23), channel_id=1, source_target_pairs={{0,16},{16,0},{1,17},{17,1},{2,18},{18,2},{3,19},{19,3},{4,20},{20... | collective-permute-start | bytes 1769480 | tf_op jit(solution)/shard_map/ppermute | solution.py:178
  2.7 25.3 %collective-permute-start.1 = (bf16[128,2304]{1,0:T(8,128)(2,1)S(1)}, bf16[128,2304]{1,0:T(8,128)(2,1)S(1)}, u32[]{:S(2)}, u32[]{:S(2)}) collective-permute-start(bf16[128,2304]{1,0:T(8,128)(2,1)S(1)} %get-tuple-element.25), channel_id=1, source_target_pairs={{0,16},{16,0},{1,17},{17,1},{2,18},{18,2},{3,19},{19,3},{4,20},{20... | collective-permute-start | bytes 1769480 | tf_op jit(solution)/shard_map/ppermute | solution.py:178
  3.4 25.9 %collective-permute-start.2 = (bf16[128,2304]{1,0:T(8,128)(2,1)S(1)}, bf16[128,2304]{1,0:T(8,128)(2,1)S(1)}, u32[]{:S(2)}, u32[]{:S(2)}) collective-permute-start(bf16[128,2304]{1,0:T(8,128)(2,1)S(1)} %get-tuple-element.27), channel_id=1, source_target_pairs={{0,16},{16,0},{1,17},{17,1},{2,18},{18,2},{3,19},{19,3},{4,20},{20... | collective-permute-start | bytes 1769480 | tf_op jit(solution)/shard_map/ppermute | solution.py:178
  4.0 17.7 %copy-start.4 = (s32[1,2]{1,0:T(1,128)S(1)}, s32[1,2]{1,0:T(1,128)}, u32[]{:S(2)}) copy-start(s32[1,2]{1,0:T(1,128)} %param.13) | copy-start | bytes 28
  4.1 36.5 %collective-permute-start.7 = (bf16[256,2304]{1,0:T(8,128)(2,1)S(1)}, bf16[256,2304]{1,0:T(8,128)(2,1)S(1)}, u32[]{:S(2)}, u32[]{:S(2)}) collective-permute-start(bf16[256,2304]{1,0:T(8,128)(2,1)S(1)} %pad_maximum_fusion), channel_id=1, source_target_pairs={{0,4},{1,5},{2,6},{3,7},{4,8},{5,9},{6,10},{7,11},{8,12},{9,13},{1... | collective-permute-start | bytes 3538952 | tf_op jit(solution)/shard_map/ppermute | solution.py:164
  8.7 11.7 %collective-permute-start.4 = (bf16[128,1152]{1,0:T(8,128)(2,1)S(1)}, bf16[128,1152]{1,0:T(8,128)(2,1)S(1)}, u32[]{:S(2)}, u32[]{:S(2)}) collective-permute-start(bf16[128,1152]{1,0:T(8,128)(2,1)S(1)} %get-tuple-element.28), channel_id=1, source_target_pairs={{4,0},{5,1},{6,2},{7,3},{8,4},{9,5},{10,6},{11,7},{12,8},{13,9},{1... | collective-permute-start | bytes 884744 | tf_op jit(solution)/shard_map/ppermute | solution.py:164
  10.0 16.8 %collective-permute-start.3 = (bf16[128,1152]{1,0:T(8,128)(2,1)S(1)}, bf16[128,1152]{1,0:T(8,128)(2,1)S(1)}, u32[]{:S(2)}, u32[]{:S(2)}) collective-permute-start(bf16[128,1152]{1,0:T(8,128)(2,1)S(1)} %get-tuple-element.29), channel_id=1, source_target_pairs={{4,0},{5,1},{6,2},{7,3},{8,4},{9,5},{10,6},{11,7},{12,8},{13,9},{1... | collective-permute-start | bytes 884744 | tf_op jit(solution)/shard_map/ppermute | solution.py:164
  20.4 12.4 %collective-permute-start.6 = (bf16[128,1152]{1,0:T(8,128)(2,1)S(1)}, bf16[128,1152]{1,0:T(8,128)(2,1)S(1)}, u32[]{:S(2)}, u32[]{:S(2)}) collective-permute-start(bf16[128,1152]{1,0:T(8,128)(2,1)S(1)} %collective-permute-done.4.refs_0_), channel_id=1, source_target_pairs={{4,0},{5,1},{6,2},{7,3},{8,4},{9,5},{10,6},{11,7},{12,8},{13,9},{1... | collective-permute-start | bytes 884744 | tf_op jit(solution)/shard_map/ppermute | solution.py:164
  26.8 18.5 %collective-permute-start.10 = (s32[1,2]{1,0:T(1,128)S(1)}, s32[1,2]{1,0:T(1,128)S(1)}, u32[]{:S(2)}, u32[]{:S(2)}) collective-permute-start(s32[1,2]{1,0:T(1,128)S(1)} %copy-done.4), channel_id=1, source_target_pairs={{4,0},{5,1},{6,2},{7,3},{8,4},{9,5},{10,6},{11,7},{12,8},{13,9},{1... | collective-permute-start | bytes 32 | tf_op jit(solution)/shard_map/ppermute | solution.py:164
  28.0 12.5 %collective-permute-start.5 = (bf16[128,1152]{1,0:T(8,128)(2,1)S(1)}, bf16[128,1152]{1,0:T(8,128)(2,1)S(1)}, u32[]{:S(2)}, u32[]{:S(2)}) collective-permute-start(bf16[128,1152]{1,0:T(8,128)(2,1)S(1)} %collective-permute-done.3.refs_0_), channel_id=1, source_target_pairs={{4,0},{5,1},{6,2},{7,3},{8,4},{9,5},{10,6},{11,7},{12,8},{13,9},{1... | collective-permute-start | bytes 884744 | tf_op jit(solution)/shard_map/ppermute | solution.py:164
  29.4 29.5 %collective-permute-start.13 = (bf16[128,2304]{1,0:T(8,128)(2,1)S(1)}, bf16[128,2304]{1,0:T(8,128)(2,1)S(1)}, u32[]{:S(2)}, u32[]{:S(2)}) collective-permute-start(bf16[128,2304]{1,0:T(8,128)(2,1)S(1)} %get-tuple-element.16.refs_0_), channel_id=1, source_target_pairs={{4,0},{5,1},{6,2},{7,3},{8,4},{9,5},{10,6},{11,7},{12,8},{13,9},{1... | collective-permute-start | bytes 1769480 | tf_op jit(solution)/shard_map/ppermute | solution.py:164
  33.6 11.7 %collective-permute-start.9 = (bf16[128,1280]{1,0:T(8,128)(2,1)S(1)}, bf16[128,1280]{1,0:T(8,128)(2,1)S(1)}, u32[]{:S(2)}, u32[]{:S(2)}) collective-permute-start(bf16[128,1280]{1,0:T(8,128)(2,1)S(1)} %far.2), channel_id=1, source_target_pairs={{0,4},{1,5},{2,6},{3,7},{4,8},{5,9},{6,10},{7,11},{8,12},{9,13},{1... | collective-permute-start | bytes 983048 | tf_op jit(solution)/shard_map/ppermute | solution.py:164
  41.3 12.1 %collective-permute-start.8 = (bf16[128,1280]{1,0:T(8,128)(2,1)S(1)}, bf16[128,1280]{1,0:T(8,128)(2,1)S(1)}, u32[]{:S(2)}, u32[]{:S(2)}) collective-permute-start(bf16[128,1280]{1,0:T(8,128)(2,1)S(1)} %far.3), channel_id=1, source_target_pairs={{0,4},{1,5},{2,6},{3,7},{4,8},{5,9},{6,10},{7,11},{8,12},{9,13},{1... | collective-permute-start | bytes 983048 | tf_op jit(solution)/shard_map/ppermute | solution.py:164
  46.4 18.2 %collective-permute-start.12 = (bf16[128,1280]{1,0:T(8,128)(2,1)S(1)}, bf16[128,1280]{1,0:T(8,128)(2,1)S(1)}, u32[]{:S(2)}, u32[]{:S(2)}) collective-permute-start(bf16[128,1280]{1,0:T(8,128)(2,1)S(1)} %near.2), channel_id=1, source_target_pairs={{0,4},{1,5},{2,6},{3,7},{4,8},{5,9},{6,10},{7,11},{8,12},{9,13},{1... | collective-permute-start | bytes 983048 | tf_op jit(solution)/shard_map/ppermute | solution.py:164
  54.5 13.0 %collective-permute-start.11 = (bf16[128,1280]{1,0:T(8,128)(2,1)S(1)}, bf16[128,1280]{1,0:T(8,128)(2,1)S(1)}, u32[]{:S(2)}, u32[]{:S(2)}) collective-permute-start(bf16[128,1280]{1,0:T(8,128)(2,1)S(1)} %near.3), channel_id=1, source_target_pairs={{0,4},{1,5},{2,6},{3,7},{4,8},{5,9},{6,10},{7,11},{8,12},{9,13},{1... | collective-permute-start | bytes 983048 | tf_op jit(solution)/shard_map/ppermute | solution.py:164
  61.2 16.3 %collective-permute-start.14 = (bf16[128,2432]{1,0:T(8,128)(2,1)S(1)}, bf16[128,2432]{1,0:T(8,128)(2,1)S(1)}, u32[]{:S(2)}, u32[]{:S(2)}) collective-permute-start(bf16[128,2432]{1,0:T(8,128)(2,1)S(1)} %both.1), channel_id=1, source_target_pairs={{0,4},{1,5},{2,6},{3,7},{4,8},{5,9},{6,10},{7,11},{8,12},{9,13},{1... | collective-permute-start | bytes 1867784 | tf_op jit(solution)/shard_map/ppermute | solution.py:164

commit v3 on v2

--- a/solution.py
+++ b/solution.py
@@ -11,11 +11,10 @@
 HEAD_DIM = 64
 BLOCK = 128
 TILE = 2 * HEAD_DIM
-FIELD = 21
 ABSENT = -1e30
 WEIGHT = 30
 FACTOR = math.log2(math.e) / math.sqrt(HEAD_DIM)
-FAR, NEAR, BOTH, OWN = range(4)
+FAR, NEAR, BOTH, OWN, LOCAL = range(5)
 
 
 def iota(shape, dimension):
@@ -39,22 +38,55 @@
     within = iota((BLOCK, TILE), 1) % HEAD_DIM < tiles
     packed = jnp.where(within, parts[0], 0.0)
     for place, part in enumerate(parts[1:], 1):
-        packed = packed + pltpu.roll(jnp.where(within, part, 0.0), place * FIELD, 1)
-    return packed.astype(jnp.bfloat16)
-
-
-def field_sum(packed, start, count):
-    packed = packed.astype(jnp.float32)
-    return sum(
-        packed if i == 0 else pltpu.roll(packed, TILE - i * FIELD, 1) for i in range(start, start + count)
-    )
-
-
-def spreader():
-    row, column = iota((TILE, 2 * TILE), 0), iota((TILE, 2 * TILE), 1)
+        packed = packed + pltpu.roll(jnp.where(within, part, 0.0), place * tiles, 1)
+    return packed
+
+
+def spreader(tiles):
+    row, column = iota((TILE, TILE), 0), iota((TILE, TILE), 1)
     place = row % HEAD_DIM
-    same = (row // HEAD_DIM == (column // HEAD_DIM) % 2) & (place < 2 * FIELD)
-    return jnp.where(same & (column < TILE), place % FIELD, -1).astype(jnp.int16)
+    same = (row // HEAD_DIM == column // HEAD_DIM) & (place < 2 * tiles)
+    return jnp.where(same, place % tiles, -1).astype(jnp.int16)
+
+
+def tile_rows(j):
+    return slice(j * BLOCK, (j + 1) * BLOCK)
+
+
+def log_rows(tiles):
+    return -(-6 * tiles // 16) * 16 if 6 * tiles <= HEAD_DIM else TILE
+
+
+def pack(out_ref, logs, tiles):
+    packed = fields(pieces(logs, 3), tiles)
+    if 6 * tiles <= HEAD_DIM:
+        packed = packed + pltpu.roll(packed, TILE - HEAD_DIM + 3 * tiles, 1)
+    out_ref[tiles * BLOCK :, :] = packed.T[: log_rows(tiles)].astype(jnp.bfloat16)
+
+
+def unpack(payload_ref, tiles):
+    rows = payload_ref[tiles * BLOCK :, :].astype(jnp.float32)
+    if rows.shape[0] < TILE:
+        rows = jnp.concatenate([rows, jnp.zeros((TILE - rows.shape[0], BLOCK), jnp.float32)], 0)
+    packed = rows.T
+    if 6 * tiles <= HEAD_DIM:
+        packed = jnp.where(iota((BLOCK, TILE), 1) < HEAD_DIM, packed, pltpu.roll(packed, HEAD_DIM - 3 * tiles, 1))
+    return packed + pltpu.roll(packed, TILE - tiles, 1) + pltpu.roll(packed, TILE - 2 * tiles, 1)
+
+
+def mix(top, total, far_top, far_total, tiles):
+    most = jnp.maximum(top, far_top)
+    here, there = jnp.exp2(top - most), jnp.exp2(far_top - most)
+    whole = here * total + there * far_total
+    weights = [fields(pieces(x / whole, 2), tiles).astype(jnp.bfloat16) for x in (here, there)]
+    return jnp.concatenate(weights, 0), most + jnp.log2(whole)
+
+
+def blend(mixed, spread, j, sums_ref, far_ref, columns):
+    pick = jnp.where(spread == j, 1.0, 0.0).astype(jnp.bfloat16)
+    both = jnp.dot(mixed, pick, preferred_element_type=jnp.float32)
+    result = both[:BLOCK] * sums_ref[:, columns] + both[BLOCK:] * far_ref[tile_rows(j), :].astype(jnp.float32)
+    return result.astype(jnp.bfloat16)
 
 
 def share(query, key, value, low, heads, causal=None):
@@ -77,78 +109,91 @@
 
 def kernel(tiles, first, part, *refs):
     query_ref, key_ref, value_ref, *refs = refs
-    width = tiles * TILE
     if part in (NEAR, OWN):
         other_ref, flags_ref, *refs = refs
     elif part == BOTH:
         far_pair_ref, flags_ref, *refs = refs
-    if part != FAR:
+    if part in (NEAR, BOTH, OWN):
         sums_ref = refs.pop()
     if part == BOTH:
         far_ref = refs.pop()
     out_ref = refs[-1]
+    if part == LOCAL:
+        sums_ref, state_ref = refs
     lane = iota((BLOCK, TILE), 1)
     low = lane < HEAD_DIM
     place = lane % HEAD_DIM
     low16 = lax.broadcasted_iota(jnp.int16, (BLOCK, TILE), 1) < HEAD_DIM
     heads = by_head(jnp.ones((BLOCK, TILE), jnp.bfloat16), low16)
-    causal = iota((BLOCK, BLOCK), 0) >= iota((BLOCK, BLOCK), 1) if part == OWN else None
+    causal = iota((BLOCK, BLOCK), 0) >= iota((BLOCK, BLOCK), 1) if part in (OWN, LOCAL) else None
     top = total = far_top = far_total = jnp.zeros((BLOCK, TILE), jnp.float32)
     for j in range(tiles):
         columns = slice(j * TILE, (j + 1) * TILE)
         there = slice((first + j) * TILE, (first + j + 1) * TILE)
-        query = query_ref[:, there if part == OWN else columns]
+        query = query_ref[:, there if part in (OWN, LOCAL) else columns]
         sums, totals, tops = share(query, key_ref[:, there], value_ref[:, there], low16, heads, causal)
         top = jnp.where(place == j, jnp.where(low, tops[0], tops[1]), top)
         total = jnp.where(place == j, totals, total)
         if part == FAR:
-            out_ref[:, columns] = (sums / totals).astype(jnp.bfloat16)
+            out_ref[tile_rows(j), :] = (sums / totals).astype(jnp.bfloat16)
         else:
             sums_ref[:, columns] = sums
         if part == BOTH:
             sums, totals, tops = share(query, far_pair_ref[:BLOCK, columns], far_pair_ref[BLOCK:, columns], low16, heads)
             far_top = jnp.where(place == j, jnp.where(low, tops[0], tops[1]), far_top)
             far_total = jnp.where(place == j, totals, far_total)
-            far_ref[:, columns] = sums
-    if part != FAR:
-        near, far = flags_ref[0:1, :] > 0, flags_ref[1:2, :] > 0
-        if part != BOTH:
-            far_ref = other_ref
-            far_top, far_total = field_sum(other_ref[:, width:], 0, 3), 1.0
-        far_top = jnp.where(near | far if part == OWN else far, far_top, ABSENT)
-        if part != OWN:
-            top = jnp.where(near, top, ABSENT)
-        most = jnp.maximum(top, far_top)
-        here, there = jnp.exp2(top - most), jnp.exp2(far_top - most)
-        top, total = most, here * total + there * far_total
-        spread = spreader()
-        here, there = fields(pieces(here / total, 2), tiles), fields(pieces(there / total, 2), tiles)
-        for j in range(tiles):
-            columns = slice(j * TILE, (j + 1) * TILE)
-            pick = jnp.where(spread[:, :TILE] == j, 1.0, 0.0).astype(jnp.bfloat16)
-            both = jnp.dot(jnp.concatenate([here, there], 0), pick, preferred_element_type=jnp.float32)
-            result = both[:BLOCK] * sums_ref[:, columns]
-            result = result + both[BLOCK:] * far_ref[:, columns].astype(jnp.float32)
-            if part == OWN:
-                columns = slice((first + j) * TILE, (first + j + 1) * TILE)
-            out_ref[:, columns] = result.astype(jnp.bfloat16)
+            far_ref[tile_rows(j), :] = sums
+    if part == LOCAL:
+        state_ref[:, :TILE] = top
+        state_ref[:, TILE:] = total
+        return
+    if part == FAR:
+        pack(out_ref, top + jnp.log2(total), tiles)
+        return
+    near, far = flags_ref[0:1, :] > 0, flags_ref[1:2, :] > 0
+    if part != BOTH:
+        far_ref = other_ref
+        far_top, far_total = unpack(other_ref, tiles), 1.0
+    far_top = jnp.where(near | far if part == OWN else far, far_top, ABSENT)
     if part != OWN:
-        out_ref[:, width:] = fields(pieces(top + jnp.log2(total), 3), tiles)
+        top = jnp.where(near, top, ABSENT)
+    mixed, log = mix(top, total, far_top, far_total, tiles)
+    spread = spreader(tiles)
+    for j in range(tiles):
+        columns = slice(j * TILE, (j + 1) * TILE)
+        result = blend(mixed, spread, j, sums_ref, far_ref, columns)
+        if part == OWN:
+            out_ref[:, (first + j) * TILE : (first + j + 1) * TILE] = result
+        else:
+            out_ref[tile_rows(j), :] = result
+    if part != OWN:
+        pack(out_ref, log, tiles)
 
 
 def attend(part, tiles, first, query, key, value, *others):
     width = tiles * TILE
     operands = (query, key, value) + others
-    out_shape = key.shape if part == OWN else (BLOCK, width + TILE)
+    if part == OWN:
+        out_shape = jax.ShapeDtypeStruct(key.shape, jnp.bfloat16)
+    elif part == LOCAL:
+        out_shape = tuple(jax.ShapeDtypeStruct((BLOCK, w), jnp.float32) for w in (width, 2 * TILE))
+    else:
+        out_shape = jax.ShapeDtypeStruct((tiles * BLOCK + log_rows(tiles), TILE), jnp.bfloat16)
     in_vmem = pl.BlockSpec(memory_space=pltpu.VMEM)
     return pl.pallas_call(
         functools.partial(kernel, tiles, first, part),
-        out_shape=jax.ShapeDtypeStruct(out_shape, jnp.bfloat16),
+        out_shape=out_shape,
         in_specs=[in_vmem] * len(operands),
-        out_specs=in_vmem,
-        scratch_shapes=[pltpu.VMEM((BLOCK, width), jnp.float32)] * (0, 1, 2, 1)[part],
+        out_specs=(in_vmem, in_vmem) if part == LOCAL else in_vmem,
+        scratch_shapes={
+            FAR: (),
+            NEAR: (pltpu.VMEM((BLOCK, width), jnp.float32),),
+            BOTH: (pltpu.VMEM((tiles * BLOCK, TILE), jnp.float32), pltpu.VMEM((BLOCK, width), jnp.float32)),
+            OWN: (pltpu.VMEM((BLOCK, width), jnp.float32),),
+            LOCAL: (),
+        }[part],
         input_output_aliases={len(operands) - 1: 0} if part == OWN and first else {},
-        name=("far", "near", "both", "own")[part],
+        name=("far", "near", "both", "own", "local")[part],
         compiler_params=pltpu.CompilerParams(vmem_limit_bytes=16 * 1024 * 1024),
         cost_estimate=pl.CostEstimate(
             flops=tiles * 8 * BLOCK * BLOCK * TILE * WEIGHT,
@@ -156,6 +201,53 @@
             transcendentals=tiles * 2 * BLOCK * BLOCK,
         ),
     )(*operands)
+
+
+def last_kernel(count, sums_ref, state_ref, other_ref, flags_ref, second_ref, forward_ref, handed_ref, first_ref, sems):
+    at_end = lax.axis_index("section") == lax.axis_size("section") - 1
+    step = -(-count // 3) * TILE
+
+    def copy(i, first_out, second_out):
+        if i == 0:
+            return pltpu.make_async_copy(second_ref, second_out.at[0], sems.at[0])
+        cut = slice((i - 1) * step, min(i * step, count * TILE))
+        return pltpu.make_async_copy(first_ref.at[:, cut], first_out.at[0, :, cut], sems.at[i])
+
+    def at_place(act):
+        pl.when(at_end)(lambda: act(handed_ref, forward_ref))
+        pl.when(jnp.logical_not(at_end))(lambda: act(forward_ref, handed_ref))
+
+    at_place(lambda *outs: copy(0, *outs).start())
+    there = unpack(other_ref, count)
+    there = jnp.where((flags_ref[0:1, :] > 0) | (flags_ref[1:2, :] > 0), there, ABSENT)
+    mixed, _ = mix(state_ref[:, :TILE], state_ref[:, TILE:], there, 1.0, count)
+    spread = spreader(count)
+    for j in range(count):
+        columns = slice(j * TILE, (j + 1) * TILE)
+        first_ref[:, columns] = blend(mixed, spread, j, sums_ref, other_ref, columns)
+        if (j + 1) * TILE % step == 0 or j == count - 1:
+            at_place(lambda *outs, i=j * TILE // step + 1: copy(i, *outs).start())
+
+    def wait(*outs):
+        for i in range(-(-count * TILE // step) + 1):
+            copy(i, *outs).wait()
+
+    at_place(wait)
+
+
+def finish(sums, state, came, flags, second):
+    in_vmem, anywhere = pl.BlockSpec(memory_space=pltpu.VMEM), pl.BlockSpec(memory_space=pl.ANY)
+    out = jax.ShapeDtypeStruct((1,) + second.shape, second.dtype)
+    return pl.pallas_call(
+        functools.partial(last_kernel, second.shape[1] // TILE),
+        out_shape=(out, out),
+        in_specs=[in_vmem] * 5,
+        out_specs=(anywhere, anywhere),
+        scratch_shapes=[pltpu.VMEM(second.shape, second.dtype), pltpu.SemaphoreType.DMA((4,))],
+        name="last",
+        compiler_params=pltpu.CompilerParams(vmem_limit_bytes=16 * 1024 * 1024),
+        cost_estimate=pl.CostEstimate(flops=WEIGHT << 26, bytes_accessed=5 * second.size, transcendentals=0),
+    )(sums, state, came, flags, second)
 
 
 def shifted(block, axis, distance):
@@ -201,12 +293,12 @@
     once_b = onward(query2[:, half * TILE :])
     twice_a = onward(once_a)
     twice_b = onward(after(once_b, once_a))
-    once = onward(after(query, once_b))
     flags = spread_flags(key_blocks)
     next_blocks = onward(key_blocks)
 
     far_a = attend(FAR, half, 0, twice_a, key2, value2)
     back_a = back(far_a)
+    once = onward(after(query, far_a))
     far_b = attend(FAR, count - half, half, after(twice_b, far_a, far), key2, value2)
     back_b = back(far_b)
     next_flags = spread_flags(after(next_blocks, far_b))
@@ -218,12 +310,8 @@
     done = back(near)
     out2 = attend(OWN, half, 0, query2, key2, value2, after(done_a, near), flags)
     out2 = attend(OWN, count - half, half, query2, key2, value2, done_b, flags, out2)
-    out = attend(OWN, count, 0, query, key, value, after(done, out2), flags)
-
-    at_end = lax.axis_index("section") == lax.axis_size("section") - 1
-    forward = jnp.where(at_end, out2, out)
-    handed = jnp.where(at_end, out, out2)
-    return forward[None], handed[None]
+    sums, state = attend(LOCAL, count, 0, after(query, out2), key, value)
+    return finish(sums, state, after(done, sums), flags, out2)
 
 
 def solution(mesh):

time: 80.6 us -> 76.6 us (0.950)
  waiting for transfers between devices: 32.8 us -> 29.1 us
  Pallas kernels: 9.66 us -> 11.1 us
  other arithmetic: 2.75 us -> 1.67 us
    ppermute x12, waiting for transfers between devices: 32.8 us -> 29.1 us  [shifted(): return lax.ppermute(block, axis, route)]
    select_n x0 -> x1, other arithmetic: none -> 1.42 us  [crosses(): jnp.where(section == size - 1, above, below)]
    select_n x3 -> x2, other arithmetic: 1.58 us -> 0.16 us  [stays(): here = jnp.where(section == size - 1, below, above)]
    pallas_call x8 -> x9, Pallas kernels: 9.66 us -> 11.1 us  [the longest x8 9.59 us: attend(): pl.pallas_call(functools.partial(kernel, tiles, first, part), out_shape=o...]
    broadcast_in_dim x1 -> x0, other arithmetic: 1.09 us -> none  [on_device(): return (forward[None], handed[None])]
  transfers between devices with their start and end apart: 15 -> 15, of which waited for: 7 -> 8; matrix products, arithmetic and copies ran while one was open for 1% -> 1% of each run, Pallas kernels for 10% -> 13%
where the time goes in v3:
time: 76.6 us; the launch traced here: 76.2 us
  starting transfers between devices  32.6 us (43%)
  waiting for transfers between devices  29.1 us (38%)
  Pallas kernels  11.1 us (14%)
  other arithmetic  1.67 us (2%)
  between operations  0.93 us (1%)
    ppermute x12, starting transfers between devices, shifted(): return lax.ppermute(block, axis, route)  31.9 us
    ppermute x12, waiting for transfers between devices, shifted(): return lax.ppermute(block, axis, route)  29.1 us
    pallas_call x8, Pallas kernels, attend(): pl.pallas_call(functools.partial(kernel, tiles, first, part), out_shape=o...  9.59 us
  transfers between devices with their start and end apart: 15, of which 8 were waited for; matrix products, arithmetic and copies ran while one was open for 1% of the time, Pallas kernels for 13%

profile of v3, /device:TPU:0, one launch (start us, length us, event | category | flops | bytes accessed | tf_op | source)
XLA Modules:
  0.0 76.2 jit_solution(4480700064387584040)
XLA Ops:
  0.7 1.4 %select_bitcast_fusion.4 = (bf16[128,2304]{1,0:T(8,128)(2,1)S(1)}, bf16[128,2304]{1,0:T(8,128)(2,1)S(1)}) fusion(bf16[1,128,2304]{2,1,0:T(8,128)(2,1)} %param.10, bf16[1,128,2304]{2,1,0:T(8,128)(2,1)} %param.7, pred[]{:T(512)S(6)} %eq.2), kind=kLoop, calls=%fused_computation.5 | loop fusion | flops 589824 | bytes 2359297 | tf_op jit(solution)/shard_map/jit(_where)/select_n | solution.py:270
  3.5 5.0 %collective-permute-start.7 = (bf16[256,2304]{1,0:T(8,128)(2,1)S(1)}, bf16[256,2304]{1,0:T(8,128)(2,1)S(1)}, u32[]{:S(2)}, u32[]{:S(2)}) collective-permute-start(bf16[256,2304]{1,0:T(8,128)(2,1)S(1)} %pad_maximum_fusion), channel_id=1, source_target_pairs={{0,4},{1,5},{2,6},{3,7},{4,8},{5,9},{6,10},{7,11},{8,12},{9,13},{1... | collective-permute-start | bytes 3538952 | tf_op jit(solution)/shard_map/ppermute | solution.py:256
  8.6 1.3 %collective-permute-start.4 = (bf16[128,1152]{1,0:T(8,128)(2,1)S(1)}, bf16[128,1152]{1,0:T(8,128)(2,1)S(1)}, u32[]{:S(2)}, u32[]{:S(2)}) collective-permute-start(bf16[128,1152]{1,0:T(8,128)(2,1)S(1)} %get-tuple-element.32), channel_id=1, source_target_pairs={{4,0},{5,1},{6,2},{7,3},{8,4},{9,5},{10,6},{11,7},{12,8},{13,9},{1... | collective-permute-start | bytes 884744 | tf_op jit(solution)/shard_map/ppermute | solution.py:256
  10.0 1.3 %collective-permute-start.3 = (bf16[128,1152]{1,0:T(8,128)(2,1)S(1)}, bf16[128,1152]{1,0:T(8,128)(2,1)S(1)}, u32[]{:S(2)}, u32[]{:S(2)}) collective-permute-start(bf16[128,1152]{1,0:T(8,128)(2,1)S(1)} %get-tuple-element.33), channel_id=1, source_target_pairs={{4,0},{5,1},{6,2},{7,3},{8,4},{9,5},{10,6},{11,7},{12,8},{13,9},{1... | collective-permute-start | bytes 884744 | tf_op jit(solution)/shard_map/ppermute | solution.py:256
  11.3 9.1 %collective-permute-done.4.refs_0_ = bf16[128,1152]{1,0:T(8,128)(2,1)S(1)} collective-permute-done((bf16[128,1152]{1,0:T(8,128)(2,1)S(1)}, bf16[128,1152]{1,0:T(8,128)(2,1)S(1)}, u32[]{:S(2)}, u32[]{:S(2)}) %collective-permute-start.4) | collective-permute-done | bytes 294944 | tf_op jit(solution)/shard_map/ppermute | solution.py:256
  20.4 1.3 %collective-permute-start.6 = (bf16[128,1152]{1,0:T(8,128)(2,1)S(1)}, bf16[128,1152]{1,0:T(8,128)(2,1)S(1)}, u32[]{:S(2)}, u32[]{:S(2)}) collective-permute-start(bf16[128,1152]{1,0:T(8,128)(2,1)S(1)} %collective-permute-done.4.refs_0_), channel_id=1, source_target_pairs={{4,0},{5,1},{6,2},{7,3},{8,4},{9,5},{10,6},{11,7},{12,8},{13,9},{1... | collective-permute-start | bytes 884744 | tf_op jit(solution)/shard_map/ppermute | solution.py:256
  21.8 5.0 %collective-permute-done.3.refs_0_ = bf16[128,1152]{1,0:T(8,128)(2,1)S(1)} collective-permute-done((bf16[128,1152]{1,0:T(8,128)(2,1)S(1)}, bf16[128,1152]{1,0:T(8,128)(2,1)S(1)}, u32[]{:S(2)}, u32[]{:S(2)}) %collective-permute-start.3) | collective-permute-done | bytes 294944 | tf_op jit(solution)/shard_map/ppermute | solution.py:256
  26.8 1.3 %collective-permute-start.10 = (s32[1,2]{1,0:T(1,128)S(1)}, s32[1,2]{1,0:T(1,128)S(1)}, u32[]{:S(2)}, u32[]{:S(2)}) collective-permute-start(s32[1,2]{1,0:T(1,128)S(1)} %copy-done.4), channel_id=1, source_target_pairs={{4,0},{5,1},{6,2},{7,3},{8,4},{9,5},{10,6},{11,7},{12,8},{13,9},{1... | collective-permute-start | bytes 32 | tf_op jit(solution)/shard_map/ppermute | solution.py:256
  28.1 1.3 %collective-permute-start.5 = (bf16[128,1152]{1,0:T(8,128)(2,1)S(1)}, bf16[128,1152]{1,0:T(8,128)(2,1)S(1)}, u32[]{:S(2)}, u32[]{:S(2)}) collective-permute-start(bf16[128,1152]{1,0:T(8,128)(2,1)S(1)} %collective-permute-done.3.refs_0_), channel_id=1, source_target_pairs={{4,0},{5,1},{6,2},{7,3},{8,4},{9,5},{10,6},{11,7},{12,8},{13,9},{1... | collective-permute-start | bytes 884744 | tf_op jit(solution)/shard_map/ppermute | solution.py:256
  29.4 3.4 %collective-permute-done.6.refs_0_ = bf16[128,1152]{1,0:T(8,128)(2,1)S(1)} collective-permute-done((bf16[128,1152]{1,0:T(8,128)(2,1)S(1)}, bf16[128,1152]{1,0:T(8,128)(2,1)S(1)}, u32[]{:S(2)}, u32[]{:S(2)}) %collective-permute-start.6) | collective-permute-done | bytes 294944 | tf_op jit(solution)/shard_map/ppermute | solution.py:256
  33.7 3.2 %collective-permute-start.9 = (bf16[1216,128]{1,0:T(8,128)(2,1)S(1)}, bf16[1216,128]{1,0:T(8,128)(2,1)S(1)}, u32[]{:S(2)}, u32[]{:S(2)}) collective-permute-start(bf16[1216,128]{1,0:T(8,128)(2,1)S(1)} %far.2), channel_id=1, source_target_pairs={{0,4},{1,5},{2,6},{3,7},{4,8},{5,9},{6,10},{7,11},{8,12},{9,13},{1... | collective-permute-start | bytes 933896 | tf_op jit(solution)/shard_map/ppermute | solution.py:256
  36.9 1.0 %collective-permute-done.5.refs_0_ = bf16[128,1152]{1,0:T(8,128)(2,1)S(1)} collective-permute-done((bf16[128,1152]{1,0:T(8,128)(2,1)S(1)}, bf16[128,1152]{1,0:T(8,128)(2,1)S(1)}, u32[]{:S(2)}, u32[]{:S(2)}) %collective-permute-start.5) | collective-permute-done | bytes 294944 | tf_op jit(solution)/shard_map/ppermute | solution.py:256
  38.8 3.4 %collective-permute-start.8 = (bf16[1216,128]{1,0:T(8,128)(2,1)S(1)}, bf16[1216,128]{1,0:T(8,128)(2,1)S(1)}, u32[]{:S(2)}, u32[]{:S(2)}) collective-permute-start(bf16[1216,128]{1,0:T(8,128)(2,1)S(1)} %far.3), channel_id=1, source_target_pairs={{0,4},{1,5},{2,6},{3,7},{4,8},{5,9},{6,10},{7,11},{8,12},{9,13},{1... | collective-permute-start | bytes 933896 | tf_op jit(solution)/shard_map/ppermute | solution.py:256
  42.3 1.3 %collective-permute-start.13 = (bf16[128,2304]{1,0:T(8,128)(2,1)S(1)}, bf16[128,2304]{1,0:T(8,128)(2,1)S(1)}, u32[]{:S(2)}, u32[]{:S(2)}) collective-permute-start(bf16[128,2304]{1,0:T(8,128)(2,1)S(1)} %get-tuple-element.22.refs_0_), channel_id=1, source_target_pairs={{4,0},{5,1},{6,2},{7,3},{8,4},{9,5},{10,6},{11,7},{12,8},{13,9},{1... | collective-permute-start | bytes 1769480 | tf_op jit(solution)/shard_map/ppermute | solution.py:256
  43.7 1.1 %near.2 = bf16[1216,128]{1,0:T(8,128)(2,1)S(1)} custom-call(bf16[128,1152]{1,0:T(8,128)(2,1)S(1)} %collective-permute-done.4.refs_0_, bf16[128,2304]{1,0:T(8,128)(2,1)S(1)} %collective-permute-done.1.refs_1_, bf16[128,2304]{1,0:T(8,128)(2,1)S(1)} %collective-permute-done.2.refs_2_, bf16[1216,128]{1,0:T(8,128)(2,1)S(1)} %collective-permute-done.9.refs_3_, ...), custom_call_target="tpu_custom_call" | custom-call | flops 4529848320 | bytes 1474560 | tf_op jit(solution)/shard_map/near/pallas_call | solution.py:183
  44.8 4.6 %collective-permute-start.12 = (bf16[1216,128]{1,0:T(8,128)(2,1)S(1)}, bf16[1216,128]{1,0:T(8,128)(2,1)S(1)}, u32[]{:S(2)}, u32[]{:S(2)}) collective-permute-start(bf16[1216,128]{1,0:T(8,128)(2,1)S(1)} %near.2), channel_id=1, source_target_pairs={{0,4},{1,5},{2,6},{3,7},{4,8},{5,9},{6,10},{7,11},{8,12},{9,13},{1... | collective-permute-start | bytes 933896 | tf_op jit(solution)/shard_map/ppermute | solution.py:256
  50.1 1.1 %near.3 = bf16[1216,128]{1,0:T(8,128)(2,1)S(1)} custom-call(bf16[128,1152]{1,0:T(8,128)(2,1)S(1)} %collective-permute-done.3.refs_0_, bf16[128,2304]{1,0:T(8,128)(2,1)S(1)} %collective-permute-done.1.refs_1_, bf16[128,2304]{1,0:T(8,128)(2,1)S(1)} %collective-permute-done.2.refs_2_, bf16[1216,128]{1,0:T(8,128)(2,1)S(1)} %collective-permute-done.8.refs_3_, ...), custom_call_target="tpu_custom_call" | custom-call | flops 4529848320 | bytes 1474560 | tf_op jit(solution)/shard_map/near/pallas_call | solution.py:183
  51.2 4.4 %collective-permute-start.11 = (bf16[1216,128]{1,0:T(8,128)(2,1)S(1)}, bf16[1216,128]{1,0:T(8,128)(2,1)S(1)}, u32[]{:S(2)}, u32[]{:S(2)}) collective-permute-start(bf16[1216,128]{1,0:T(8,128)(2,1)S(1)} %near.3), channel_id=1, source_target_pairs={{0,4},{1,5},{2,6},{3,7},{4,8},{5,9},{6,10},{7,11},{8,12},{9,13},{1... | collective-permute-start | bytes 933896 | tf_op jit(solution)/shard_map/ppermute | solution.py:256
  56.2 2.3 %both.1 = bf16[2432,128]{1,0:T(8,128)(2,1)S(1)} custom-call(bf16[128,2304]{1,0:T(8,128)(2,1)S(1)} %collective-permute-done.13.refs_0_, bf16[128,2304]{1,0:T(8,128)(2,1)S(1)} %get-tuple-element.26.refs_1_, bf16[128,2304]{1,0:T(8,128)(2,1)S(1)} %get-tuple-element.28.refs_2_, bf16[256,2304]{1,0:T(8,128)(2,1)S(1)} %collective-permute-done.7.refs_3_, ...), custom_call_target="tpu_custom_call" | custom-call | flops 9059696640 | bytes 2949120 | tf_op jit(solution)/shard_map/both/pallas_call | solution.py:183
  58.5 3.6 %collective-permute-start.14 = (bf16[2432,128]{1,0:T(8,128)(2,1)S(1)}, bf16[2432,128]{1,0:T(8,128)(2,1)S(1)}, u32[]{:S(2)}, u32[]{:S(2)}) collective-permute-start(bf16[2432,128]{1,0:T(8,128)(2,1)S(1)} %both.1), channel_id=1, source_target_pairs={{0,4},{1,5},{2,6},{3,7},{4,8},{5,9},{6,10},{7,11},{8,12},{9,13},{1... | collective-permute-start | bytes 1867784 | tf_op jit(solution)/shard_map/ppermute | solution.py:256
  62.2 1.1 %own.2.refs_5_ = bf16[128,2304]{1,0:T(8,128)(2,1)S(1)} custom-call(bf16[128,2304]{1,0:T(8,128)(2,1)S(1)} %collective-permute-done.refs_0_, bf16[128,2304]{1,0:T(8,128)(2,1)S(1)} %collective-permute-done.1.refs_1_, bf16[128,2304]{1,0:T(8,128)(2,1)S(1)} %collective-permute-done.2.refs_2_, bf16[1216,128]{1,0:T(8,128)(2,1)S(1)} %collective-permute-done.12.refs_3_, ...), custom_call_target="tpu_custom_call" | custom-call | flops 4529848320 | bytes 1474560 | tf_op jit(solution)/shard_map/own/pallas_call | solution.py:183
  63.8 1.1 %own.3.second_ref = bf16[128,2304]{1,0:T(8,128)(2,1)S(1)} custom-call(bf16[128,2304]{1,0:T(8,128)(2,1)S(1)} %collective-permute-done.refs_0_, bf16[128,2304]{1,0:T(8,128)(2,1)S(1)} %collective-permute-done.1.refs_1_, bf16[128,2304]{1,0:T(8,128)(2,1)S(1)} %collective-permute-done.2.refs_2_, ...), custom_call_target="tpu_custom_call", output_to_operand_aliasing={{}: (5, {})} | custom-call | flops 4529848320 | bytes 1474560 | tf_op jit(solution)/shard_map/own/pallas_call | solution.py:183
  66.0 8.7 %collective-permute-done.14.other_ref = bf16[2432,128]{1,0:T(8,128)(2,1)S(1)} collective-permute-done((bf16[2432,128]{1,0:T(8,128)(2,1)S(1)}, bf16[2432,128]{1,0:T(8,128)(2,1)S(1)}, u32[]{:S(2)}, u32[]{:S(2)}) %collective-permute-start.14) | collective-permute-done | bytes 622624 | tf_op jit(solution)/shard_map/ppermute | solution.py:256
  74.7 1.5 %last.1 = (bf16[1,128,2304]{2,1,0:T(8,128)(2,1)}, bf16[1,128,2304]{2,1,0:T(8,128)(2,1)}) custom-call(f32[128,2304]{1,0:T(8,128)S(1)} %get-tuple-element.23.sums_ref, f32[128,256]{1,0:T(8,128)S(1)} %get-tuple-element.24.state_ref, bf16[2432,128]{1,0:T(8,128)(2,1)S(1)} %collective-permute-done.14.other_ref, f32[2,128]{1,0:T(2,128)S(1)} %broadcast_in_dim.29.refs_4_.flags_ref, ...), custom_call_target="tpu_custom_call" | custom-call | flops 2013265920 | bytes 1474560 | tf_op jit(solution)/shard_map/last/pallas_call | solution.py:241
  (34 shorter events, 6.3 us)
Async XLA Ops:
  0.6 2.0 %copy-start = (bf16[1,128,2304]{2,1,0:T(8,128)(2,1)S(1)}, bf16[1,128,2304]{2,1,0:T(8,128)(2,1)}, u32[]{:S(2)}) copy-start(bf16[1,128,2304]{2,1,0:T(8,128)(2,1)} %param.8) | copy-start | bytes 1769476
  0.6 2.0 %copy-start.1 = (bf16[1,128,2304]{2,1,0:T(8,128)(2,1)S(1)}, bf16[1,128,2304]{2,1,0:T(8,128)(2,1)}, u32[]{:S(2)}) copy-start(bf16[1,128,2304]{2,1,0:T(8,128)(2,1)} %param.11) | copy-start | bytes 1769476
  2.1 1.1 %copy-start.2 = (bf16[1,128,2304]{2,1,0:T(8,128)(2,1)S(1)}, bf16[1,128,2304]{2,1,0:T(8,128)(2,1)}, u32[]{:S(2)}) copy-start(bf16[1,128,2304]{2,1,0:T(8,128)(2,1)} %param.9) | copy-start | bytes 1769476
  2.1 1.3 %copy-start.3 = (bf16[1,128,2304]{2,1,0:T(8,128)(2,1)S(1)}, bf16[1,128,2304]{2,1,0:T(8,128)(2,1)}, u32[]{:S(2)}) copy-start(bf16[1,128,2304]{2,1,0:T(8,128)(2,1)} %param.12) | copy-start | bytes 1769476
  2.1 6.5 %collective-permute-start = (bf16[128,2304]{1,0:T(8,128)(2,1)S(1)}, bf16[128,2304]{1,0:T(8,128)(2,1)S(1)}, u32[]{:S(2)}, u32[]{:S(2)}) collective-permute-start(bf16[128,2304]{1,0:T(8,128)(2,1)S(1)} %get-tuple-element.30), channel_id=1, source_target_pairs={{0,16},{16,0},{1,17},{17,1},{2,18},{18,2},{3,19},{19,3},{4,20},{20... | collective-permute-start | bytes 1769480 | tf_op jit(solution)/shard_map/ppermute | solution.py:270
  2.7 25.3 %collective-permute-start.1 = (bf16[128,2304]{1,0:T(8,128)(2,1)S(1)}, bf16[128,2304]{1,0:T(8,128)(2,1)S(1)}, u32[]{:S(2)}, u32[]{:S(2)}) collective-permute-start(bf16[128,2304]{1,0:T(8,128)(2,1)S(1)} %get-tuple-element.27), channel_id=1, source_target_pairs={{0,16},{16,0},{1,17},{17,1},{2,18},{18,2},{3,19},{19,3},{4,20},{20... | collective-permute-start | bytes 1769480 | tf_op jit(solution)/shard_map/ppermute | solution.py:270
  3.5 18.2 %copy-start.4 = (s32[1,2]{1,0:T(1,128)S(1)}, s32[1,2]{1,0:T(1,128)}, u32[]{:S(2)}) copy-start(s32[1,2]{1,0:T(1,128)} %param.13) | copy-start | bytes 28
  3.5 34.4 %collective-permute-start.7 = (bf16[256,2304]{1,0:T(8,128)(2,1)S(1)}, bf16[256,2304]{1,0:T(8,128)(2,1)S(1)}, u32[]{:S(2)}, u32[]{:S(2)}) collective-permute-start(bf16[256,2304]{1,0:T(8,128)(2,1)S(1)} %pad_maximum_fusion), channel_id=1, source_target_pairs={{0,4},{1,5},{2,6},{3,7},{4,8},{5,9},{6,10},{7,11},{8,12},{9,13},{1... | collective-permute-start | bytes 3538952 | tf_op jit(solution)/shard_map/ppermute | solution.py:256
  8.6 11.8 %collective-permute-start.4 = (bf16[128,1152]{1,0:T(8,128)(2,1)S(1)}, bf16[128,1152]{1,0:T(8,128)(2,1)S(1)}, u32[]{:S(2)}, u32[]{:S(2)}) collective-permute-start(bf16[128,1152]{1,0:T(8,128)(2,1)S(1)} %get-tuple-element.32), channel_id=1, source_target_pairs={{4,0},{5,1},{6,2},{7,3},{8,4},{9,5},{10,6},{11,7},{12,8},{13,9},{1... | collective-permute-start | bytes 884744 | tf_op jit(solution)/shard_map/ppermute | solution.py:256
  9.9 19.4 %collective-permute-start.2 = (bf16[128,2304]{1,0:T(8,128)(2,1)S(1)}, bf16[128,2304]{1,0:T(8,128)(2,1)S(1)}, u32[]{:S(2)}, u32[]{:S(2)}) collective-permute-start(bf16[128,2304]{1,0:T(8,128)(2,1)S(1)} %get-tuple-element.29), channel_id=1, source_target_pairs={{0,16},{16,0},{1,17},{17,1},{2,18},{18,2},{3,19},{19,3},{4,20},{20... | collective-permute-start | bytes 1769480 | tf_op jit(solution)/shard_map/ppermute | solution.py:270
  10.0 16.8 %collective-permute-start.3 = (bf16[128,1152]{1,0:T(8,128)(2,1)S(1)}, bf16[128,1152]{1,0:T(8,128)(2,1)S(1)}, u32[]{:S(2)}, u32[]{:S(2)}) collective-permute-start(bf16[128,1152]{1,0:T(8,128)(2,1)S(1)} %get-tuple-element.33), channel_id=1, source_target_pairs={{4,0},{5,1},{6,2},{7,3},{8,4},{9,5},{10,6},{11,7},{12,8},{13,9},{1... | collective-permute-start | bytes 884744 | tf_op jit(solution)/shard_map/ppermute | solution.py:256
  20.4 12.4 %collective-permute-start.6 = (bf16[128,1152]{1,0:T(8,128)(2,1)S(1)}, bf16[128,1152]{1,0:T(8,128)(2,1)S(1)}, u32[]{:S(2)}, u32[]{:S(2)}) collective-permute-start(bf16[128,1152]{1,0:T(8,128)(2,1)S(1)} %collective-permute-done.4.refs_0_), channel_id=1, source_target_pairs={{4,0},{5,1},{6,2},{7,3},{8,4},{9,5},{10,6},{11,7},{12,8},{13,9},{1... | collective-permute-start | bytes 884744 | tf_op jit(solution)/shard_map/ppermute | solution.py:256
  26.8 15.5 %collective-permute-start.10 = (s32[1,2]{1,0:T(1,128)S(1)}, s32[1,2]{1,0:T(1,128)S(1)}, u32[]{:S(2)}, u32[]{:S(2)}) collective-permute-start(s32[1,2]{1,0:T(1,128)S(1)} %copy-done.4), channel_id=1, source_target_pairs={{4,0},{5,1},{6,2},{7,3},{8,4},{9,5},{10,6},{11,7},{12,8},{13,9},{1... | collective-permute-start | bytes 32 | tf_op jit(solution)/shard_map/ppermute | solution.py:256
  28.1 9.9 %collective-permute-start.5 = (bf16[128,1152]{1,0:T(8,128)(2,1)S(1)}, bf16[128,1152]{1,0:T(8,128)(2,1)S(1)}, u32[]{:S(2)}, u32[]{:S(2)}) collective-permute-start(bf16[128,1152]{1,0:T(8,128)(2,1)S(1)} %collective-permute-done.3.refs_0_), channel_id=1, source_target_pairs={{4,0},{5,1},{6,2},{7,3},{8,4},{9,5},{10,6},{11,7},{12,8},{13,9},{1... | collective-permute-start | bytes 884744 | tf_op jit(solution)/shard_map/ppermute | solution.py:256
  33.7 9.9 %collective-permute-start.9 = (bf16[1216,128]{1,0:T(8,128)(2,1)S(1)}, bf16[1216,128]{1,0:T(8,128)(2,1)S(1)}, u32[]{:S(2)}, u32[]{:S(2)}) collective-permute-start(bf16[1216,128]{1,0:T(8,128)(2,1)S(1)} %far.2), channel_id=1, source_target_pairs={{0,4},{1,5},{2,6},{3,7},{4,8},{5,9},{6,10},{7,11},{8,12},{9,13},{1... | collective-permute-start | bytes 933896 | tf_op jit(solution)/shard_map/ppermute | solution.py:256
  38.8 11.2 %collective-permute-start.8 = (bf16[1216,128]{1,0:T(8,128)(2,1)S(1)}, bf16[1216,128]{1,0:T(8,128)(2,1)S(1)}, u32[]{:S(2)}, u32[]{:S(2)}) collective-permute-start(bf16[1216,128]{1,0:T(8,128)(2,1)S(1)} %far.3), channel_id=1, source_target_pairs={{0,4},{1,5},{2,6},{3,7},{4,8},{5,9},{6,10},{7,11},{8,12},{9,13},{1... | collective-permute-start | bytes 933896 | tf_op jit(solution)/shard_map/ppermute | solution.py:256
  42.3 13.9 %collective-permute-start.13 = (bf16[128,2304]{1,0:T(8,128)(2,1)S(1)}, bf16[128,2304]{1,0:T(8,128)(2,1)S(1)}, u32[]{:S(2)}, u32[]{:S(2)}) collective-permute-start(bf16[128,2304]{1,0:T(8,128)(2,1)S(1)} %get-tuple-element.22.refs_0_), channel_id=1, source_target_pairs={{4,0},{5,1},{6,2},{7,3},{8,4},{9,5},{10,6},{11,7},{12,8},{13,9},{1... | collective-permute-start | bytes 1769480 | tf_op jit(solution)/shard_map/ppermute | solution.py:256
  44.8 17.3 %collective-permute-start.12 = (bf16[1216,128]{1,0:T(8,128)(2,1)S(1)}, bf16[1216,128]{1,0:T(8,128)(2,1)S(1)}, u32[]{:S(2)}, u32[]{:S(2)}) collective-permute-start(bf16[1216,128]{1,0:T(8,128)(2,1)S(1)} %near.2), channel_id=1, source_target_pairs={{0,4},{1,5},{2,6},{3,7},{4,8},{5,9},{6,10},{7,11},{8,12},{9,13},{1... | collective-permute-start | bytes 933896 | tf_op jit(solution)/shard_map/ppermute | solution.py:256
  51.2 12.6 %collective-permute-start.11 = (bf16[1216,128]{1,0:T(8,128)(2,1)S(1)}, bf16[1216,128]{1,0:T(8,128)(2,1)S(1)}, u32[]{:S(2)}, u32[]{:S(2)}) collective-permute-start(bf16[1216,128]{1,0:T(8,128)(2,1)S(1)} %near.3), channel_id=1, source_target_pairs={{0,4},{1,5},{2,6},{3,7},{4,8},{5,9},{6,10},{7,11},{8,12},{9,13},{1... | collective-permute-start | bytes 933896 | tf_op jit(solution)/shard_map/ppermute | solution.py:256
  58.5 16.2 %collective-permute-start.14 = (bf16[2432,128]{1,0:T(8,128)(2,1)S(1)}, bf16[2432,128]{1,0:T(8,128)(2,1)S(1)}, u32[]{:S(2)}, u32[]{:S(2)}) collective-permute-start(bf16[2432,128]{1,0:T(8,128)(2,1)S(1)} %both.1), channel_id=1, source_target_pairs={{0,4},{1,5},{2,6},{3,7},{4,8},{5,9},{6,10},{7,11},{8,12},{9,13},{1... | collective-permute-start | bytes 1867784 | tf_op jit(solution)/shard_map/ppermute | solution.py:256

commit v4 on v3

--- a/solution.py
+++ b/solution.py
@@ -139,7 +139,7 @@
         else:
             sums_ref[:, columns] = sums
         if part == BOTH:
-            sums, totals, tops = share(query, far_pair_ref[:BLOCK, columns], far_pair_ref[BLOCK:, columns], low16, heads)
+            sums, totals, tops = share(query, far_pair_ref[:BLOCK, there], far_pair_ref[BLOCK:, there], low16, heads)
             far_top = jnp.where(place == j, jnp.where(low, tops[0], tops[1]), far_top)
             far_total = jnp.where(place == j, totals, far_total)
             far_ref[tile_rows(j), :] = sums
@@ -203,51 +203,63 @@
     )(*operands)
 
 
-def last_kernel(count, sums_ref, state_ref, other_ref, flags_ref, second_ref, forward_ref, handed_ref, first_ref, sems):
+def last_kernel(begin, count, sums_ref, state_ref, other_ref, flags_ref, first_ref, second_ref, forward_ref, handed_ref, rest_ref, sems):
     at_end = lax.axis_index("section") == lax.axis_size("section") - 1
-    step = -(-count // 3) * TILE
+    tiles = count - begin
+    step = -(-tiles // 3) * TILE
+    done = slice(0, begin * TILE)
 
     def copy(i, first_out, second_out):
         if i == 0:
-            return pltpu.make_async_copy(second_ref, second_out.at[0], sems.at[0])
-        cut = slice((i - 1) * step, min(i * step, count * TILE))
-        return pltpu.make_async_copy(first_ref.at[:, cut], first_out.at[0, :, cut], sems.at[i])
+            return pltpu.make_async_copy(first_ref, first_out.at[0], sems.at[0])
+        if i == 1:
+            return pltpu.make_async_copy(second_ref.at[:, done], second_out.at[0, :, done], sems.at[1])
+        cut = slice((i - 2) * step, min((i - 1) * step, tiles * TILE))
+        there = slice(begin * TILE + cut.start, begin * TILE + cut.stop)
+        return pltpu.make_async_copy(rest_ref.at[:, cut], second_out.at[0, :, there], sems.at[i])
 
     def at_place(act):
-        pl.when(at_end)(lambda: act(handed_ref, forward_ref))
-        pl.when(jnp.logical_not(at_end))(lambda: act(forward_ref, handed_ref))
-
-    at_place(lambda *outs: copy(0, *outs).start())
-    there = unpack(other_ref, count)
+        pl.when(at_end)(lambda: act(forward_ref, handed_ref))
+        pl.when(jnp.logical_not(at_end))(lambda: act(handed_ref, forward_ref))
+
+    def start(numbers):
+        def act(*outs):
+            for i in numbers:
+                copy(i, *outs).start()
+
+        at_place(act)
+
+    def wait(*outs):
+        for i in range(-(-tiles * TILE // step) + 2):
+            copy(i, *outs).wait()
+
+    start((0, 1))
+    there = unpack(other_ref, tiles)
     there = jnp.where((flags_ref[0:1, :] > 0) | (flags_ref[1:2, :] > 0), there, ABSENT)
-    mixed, _ = mix(state_ref[:, :TILE], state_ref[:, TILE:], there, 1.0, count)
-    spread = spreader(count)
-    for j in range(count):
+    mixed, _ = mix(state_ref[:, :TILE], state_ref[:, TILE:], there, 1.0, tiles)
+    spread = spreader(tiles)
+    for j in range(tiles):
         columns = slice(j * TILE, (j + 1) * TILE)
-        first_ref[:, columns] = blend(mixed, spread, j, sums_ref, other_ref, columns)
-        if (j + 1) * TILE % step == 0 or j == count - 1:
-            at_place(lambda *outs, i=j * TILE // step + 1: copy(i, *outs).start())
-
-    def wait(*outs):
-        for i in range(-(-count * TILE // step) + 1):
-            copy(i, *outs).wait()
-
+        rest_ref[:, columns] = blend(mixed, spread, j, sums_ref, other_ref, columns)
+        if (j + 1) * TILE % step == 0 or j == tiles - 1:
+            start((j * TILE // step + 2,))
     at_place(wait)
 
 
-def finish(sums, state, came, flags, second):
+def finish(begin, sums, state, came, flags, first, second):
     in_vmem, anywhere = pl.BlockSpec(memory_space=pltpu.VMEM), pl.BlockSpec(memory_space=pl.ANY)
     out = jax.ShapeDtypeStruct((1,) + second.shape, second.dtype)
+    count = second.shape[1] // TILE
     return pl.pallas_call(
-        functools.partial(last_kernel, second.shape[1] // TILE),
+        functools.partial(last_kernel, begin, count),
         out_shape=(out, out),
-        in_specs=[in_vmem] * 5,
+        in_specs=[in_vmem] * 6,
         out_specs=(anywhere, anywhere),
-        scratch_shapes=[pltpu.VMEM(second.shape, second.dtype), pltpu.SemaphoreType.DMA((4,))],
+        scratch_shapes=[pltpu.VMEM((BLOCK, (count - begin) * TILE), second.dtype), pltpu.SemaphoreType.DMA((5,))],
         name="last",
         compiler_params=pltpu.CompilerParams(vmem_limit_bytes=16 * 1024 * 1024),
         cost_estimate=pl.CostEstimate(flops=WEIGHT << 26, bytes_accessed=5 * second.size, transcendentals=0),
-    )(sums, state, came, flags, second)
+    )(sums, state, came, flags, first, second)
 
 
 def shifted(block, axis, distance):
@@ -306,12 +318,15 @@
     done_a = back(near_a)
     near_b = attend(NEAR, count - half, half, once_b, key2, value2, after(back_b, near_a), next_flags)
     done_b = back(near_b)
-    near = attend(BOTH, count, 0, after(once, near_b), key, value, far, next_flags)
-    done = back(near)
-    out2 = attend(OWN, half, 0, query2, key2, value2, after(done_a, near), flags)
+    near_c = attend(BOTH, half, 0, after(once[:, : half * TILE], near_b), key, value, far, next_flags)
+    done_c = back(near_c)
+    near_d = attend(BOTH, count - half, half, after(once[:, half * TILE :], near_c), key, value, far, next_flags)
+    done_d = back(near_d)
+    out2 = attend(OWN, half, 0, query2, key2, value2, after(done_a, near_d), flags)
     out2 = attend(OWN, count - half, half, query2, key2, value2, done_b, flags, out2)
-    sums, state = attend(LOCAL, count, 0, after(query, out2), key, value)
-    return finish(sums, state, after(done, sums), flags, out2)
+    sums, state = attend(LOCAL, count - half, half, after(query, out2), key, value)
+    out = attend(OWN, half, 0, query, key, value, after(done_c, sums), flags)
+    return finish(half, sums, state, after(done_d, out), flags, out2, out)
 
 
 def solution(mesh):

time: 76.6 us -> 76.6 us (level)
  waiting for transfers between devices: 29.1 us -> 25.4 us
  starting transfers between devices: 32.6 us -> 35 us
  Pallas kernels: 11.1 us -> 12.1 us
    ppermute x12 -> x13, waiting for transfers between devices: 29.1 us -> 25.4 us  [shifted(): return lax.ppermute(block, axis, route)]
    ppermute x12 -> x13, starting transfers between devices: 31.9 us -> 34.3 us  [shifted(): return lax.ppermute(block, axis, route)]
    pallas_call x8 -> x10, Pallas kernels: 9.59 us -> 10.8 us  [attend(): pl.pallas_call(functools.partial(kernel, tiles, first, part), out_shape=o...]
  transfers between devices with their start and end apart: 15 -> 16, of which waited for: 8 -> 8; matrix products, arithmetic and copies ran while one was open for 1% -> 1% of each run, Pallas kernels for 13% -> 14%
where the time goes in v4:
time: 76.6 us; the launch traced here: 76.2 us
  starting transfers between devices  35 us (46%)
  waiting for transfers between devices  25.4 us (33%)
  Pallas kernels  12.1 us (16%)
  other arithmetic  1.67 us (2%)
  between operations  1.13 us (1%)
  local copies, waits for them, and re-layouts  0.77 us (1%)
    ppermute x13, starting transfers between devices, shifted(): return lax.ppermute(block, axis, route)  34.3 us
    ppermute x13, waiting for transfers between devices, shifted(): return lax.ppermute(block, axis, route)  25.4 us
    pallas_call x10, Pallas kernels, attend(): pl.pallas_call(functools.partial(kernel, tiles, first, part), out_shape=o...  10.8 us
  transfers between devices with their start and end apart: 16, of which 8 were waited for; matrix products, arithmetic and copies ran while one was open for 1% of the time, Pallas kernels for 14%

profile of v4, /device:TPU:0, one launch (start us, length us, event | category | flops | bytes accessed | tf_op | source)
XLA Modules:
  0.0 76.2 jit_solution(4397001556047057390)
XLA Ops:
  0.7 1.4 %select_bitcast_fusion.4 = (bf16[128,2304]{1,0:T(8,128)(2,1)S(1)}, bf16[128,2304]{1,0:T(8,128)(2,1)S(1)}) fusion(bf16[1,128,2304]{2,1,0:T(8,128)(2,1)} %param.10, bf16[1,128,2304]{2,1,0:T(8,128)(2,1)} %param.7, pred[]{:T(512)S(6)} %eq.2), kind=kLoop, calls=%fused_computation.5 | loop fusion | flops 589824 | bytes 2359297 | tf_op jit(solution)/shard_map/jit(_where)/select_n | solution.py:282
  3.5 5.0 %collective-permute-start.7 = (bf16[256,2304]{1,0:T(8,128)(2,1)S(1)}, bf16[256,2304]{1,0:T(8,128)(2,1)S(1)}, u32[]{:S(2)}, u32[]{:S(2)}) collective-permute-start(bf16[256,2304]{1,0:T(8,128)(2,1)S(1)} %pad_maximum_fusion), channel_id=1, source_target_pairs={{0,4},{1,5},{2,6},{3,7},{4,8},{5,9},{6,10},{7,11},{8,12},{9,13},{1... | collective-permute-start | bytes 3538952 | tf_op jit(solution)/shard_map/ppermute | solution.py:268
  8.6 1.3 %collective-permute-start.4 = (bf16[128,1152]{1,0:T(8,128)(2,1)S(1)}, bf16[128,1152]{1,0:T(8,128)(2,1)S(1)}, u32[]{:S(2)}, u32[]{:S(2)}) collective-permute-start(bf16[128,1152]{1,0:T(8,128)(2,1)S(1)} %get-tuple-element.38), channel_id=1, source_target_pairs={{4,0},{5,1},{6,2},{7,3},{8,4},{9,5},{10,6},{11,7},{12,8},{13,9},{1... | collective-permute-start | bytes 884744 | tf_op jit(solution)/shard_map/ppermute | solution.py:268
  10.0 1.3 %collective-permute-start.3 = (bf16[128,1152]{1,0:T(8,128)(2,1)S(1)}, bf16[128,1152]{1,0:T(8,128)(2,1)S(1)}, u32[]{:S(2)}, u32[]{:S(2)}) collective-permute-start(bf16[128,1152]{1,0:T(8,128)(2,1)S(1)} %get-tuple-element.39), channel_id=1, source_target_pairs={{4,0},{5,1},{6,2},{7,3},{8,4},{9,5},{10,6},{11,7},{12,8},{13,9},{1... | collective-permute-start | bytes 884744 | tf_op jit(solution)/shard_map/ppermute | solution.py:268
  11.3 9.1 %collective-permute-done.4.refs_0_ = bf16[128,1152]{1,0:T(8,128)(2,1)S(1)} collective-permute-done((bf16[128,1152]{1,0:T(8,128)(2,1)S(1)}, bf16[128,1152]{1,0:T(8,128)(2,1)S(1)}, u32[]{:S(2)}, u32[]{:S(2)}) %collective-permute-start.4) | collective-permute-done | bytes 294944 | tf_op jit(solution)/shard_map/ppermute | solution.py:268
  20.4 1.3 %collective-permute-start.6 = (bf16[128,1152]{1,0:T(8,128)(2,1)S(1)}, bf16[128,1152]{1,0:T(8,128)(2,1)S(1)}, u32[]{:S(2)}, u32[]{:S(2)}) collective-permute-start(bf16[128,1152]{1,0:T(8,128)(2,1)S(1)} %collective-permute-done.4.refs_0_), channel_id=1, source_target_pairs={{4,0},{5,1},{6,2},{7,3},{8,4},{9,5},{10,6},{11,7},{12,8},{13,9},{1... | collective-permute-start | bytes 884744 | tf_op jit(solution)/shard_map/ppermute | solution.py:268
  21.8 5.0 %collective-permute-done.3.refs_0_ = bf16[128,1152]{1,0:T(8,128)(2,1)S(1)} collective-permute-done((bf16[128,1152]{1,0:T(8,128)(2,1)S(1)}, bf16[128,1152]{1,0:T(8,128)(2,1)S(1)}, u32[]{:S(2)}, u32[]{:S(2)}) %collective-permute-start.3) | collective-permute-done | bytes 294944 | tf_op jit(solution)/shard_map/ppermute | solution.py:268
  26.8 1.3 %collective-permute-start.10 = (s32[1,2]{1,0:T(1,128)S(1)}, s32[1,2]{1,0:T(1,128)S(1)}, u32[]{:S(2)}, u32[]{:S(2)}) collective-permute-start(s32[1,2]{1,0:T(1,128)S(1)} %copy-done.4), channel_id=1, source_target_pairs={{4,0},{5,1},{6,2},{7,3},{8,4},{9,5},{10,6},{11,7},{12,8},{13,9},{1... | collective-permute-start | bytes 32 | tf_op jit(solution)/shard_map/ppermute | solution.py:268
  28.1 1.3 %collective-permute-start.5 = (bf16[128,1152]{1,0:T(8,128)(2,1)S(1)}, bf16[128,1152]{1,0:T(8,128)(2,1)S(1)}, u32[]{:S(2)}, u32[]{:S(2)}) collective-permute-start(bf16[128,1152]{1,0:T(8,128)(2,1)S(1)} %collective-permute-done.3.refs_0_), channel_id=1, source_target_pairs={{4,0},{5,1},{6,2},{7,3},{8,4},{9,5},{10,6},{11,7},{12,8},{13,9},{1... | collective-permute-start | bytes 884744 | tf_op jit(solution)/shard_map/ppermute | solution.py:268
  29.4 3.4 %collective-permute-done.6.refs_0_ = bf16[128,1152]{1,0:T(8,128)(2,1)S(1)} collective-permute-done((bf16[128,1152]{1,0:T(8,128)(2,1)S(1)}, bf16[128,1152]{1,0:T(8,128)(2,1)S(1)}, u32[]{:S(2)}, u32[]{:S(2)}) %collective-permute-start.6) | collective-permute-done | bytes 294944 | tf_op jit(solution)/shard_map/ppermute | solution.py:268
  33.7 3.2 %collective-permute-start.9 = (bf16[1216,128]{1,0:T(8,128)(2,1)S(1)}, bf16[1216,128]{1,0:T(8,128)(2,1)S(1)}, u32[]{:S(2)}, u32[]{:S(2)}) collective-permute-start(bf16[1216,128]{1,0:T(8,128)(2,1)S(1)} %far.2), channel_id=1, source_target_pairs={{0,4},{1,5},{2,6},{3,7},{4,8},{5,9},{6,10},{7,11},{8,12},{9,13},{1... | collective-permute-start | bytes 933896 | tf_op jit(solution)/shard_map/ppermute | solution.py:268
  38.8 3.4 %collective-permute-start.8 = (bf16[1216,128]{1,0:T(8,128)(2,1)S(1)}, bf16[1216,128]{1,0:T(8,128)(2,1)S(1)}, u32[]{:S(2)}, u32[]{:S(2)}) collective-permute-start(bf16[1216,128]{1,0:T(8,128)(2,1)S(1)} %far.3), channel_id=1, source_target_pairs={{0,4},{1,5},{2,6},{3,7},{4,8},{5,9},{6,10},{7,11},{8,12},{9,13},{1... | collective-permute-start | bytes 933896 | tf_op jit(solution)/shard_map/ppermute | solution.py:268
  42.3 1.3 %collective-permute-start.13 = (bf16[128,2304]{1,0:T(8,128)(2,1)S(1)}, bf16[128,2304]{1,0:T(8,128)(2,1)S(1)}, u32[]{:S(2)}, u32[]{:S(2)}) collective-permute-start(bf16[128,2304]{1,0:T(8,128)(2,1)S(1)} %get-tuple-element.25.refs_0_), channel_id=1, source_target_pairs={{4,0},{5,1},{6,2},{7,3},{8,4},{9,5},{10,6},{11,7},{12,8},{13,9},{1... | collective-permute-start | bytes 1769480 | tf_op jit(solution)/shard_map/ppermute | solution.py:268
  43.7 1.1 %near.2 = bf16[1216,128]{1,0:T(8,128)(2,1)S(1)} custom-call(bf16[128,1152]{1,0:T(8,128)(2,1)S(1)} %collective-permute-done.4.refs_0_, bf16[128,2304]{1,0:T(8,128)(2,1)S(1)} %collective-permute-done.1.refs_1_, bf16[128,2304]{1,0:T(8,128)(2,1)S(1)} %collective-permute-done.2.refs_2_, bf16[1216,128]{1,0:T(8,128)(2,1)S(1)} %collective-permute-done.9.refs_3_, ...), custom_call_target="tpu_custom_call" | custom-call | flops 4529848320 | bytes 1474560 | tf_op jit(solution)/shard_map/near/pallas_call | solution.py:183
  44.8 4.6 %collective-permute-start.12 = (bf16[1216,128]{1,0:T(8,128)(2,1)S(1)}, bf16[1216,128]{1,0:T(8,128)(2,1)S(1)}, u32[]{:S(2)}, u32[]{:S(2)}) collective-permute-start(bf16[1216,128]{1,0:T(8,128)(2,1)S(1)} %near.2), channel_id=1, source_target_pairs={{0,4},{1,5},{2,6},{3,7},{4,8},{5,9},{6,10},{7,11},{8,12},{9,13},{1... | collective-permute-start | bytes 933896 | tf_op jit(solution)/shard_map/ppermute | solution.py:268
  50.0 1.1 %near.3 = bf16[1216,128]{1,0:T(8,128)(2,1)S(1)} custom-call(bf16[128,1152]{1,0:T(8,128)(2,1)S(1)} %collective-permute-done.3.refs_0_, bf16[128,2304]{1,0:T(8,128)(2,1)S(1)} %collective-permute-done.1.refs_1_, bf16[128,2304]{1,0:T(8,128)(2,1)S(1)} %collective-permute-done.2.refs_2_, bf16[1216,128]{1,0:T(8,128)(2,1)S(1)} %collective-permute-done.8.refs_3_, ...), custom_call_target="tpu_custom_call" | custom-call | flops 4529848320 | bytes 1474560 | tf_op jit(solution)/shard_map/near/pallas_call | solution.py:183
  51.2 4.4 %collective-permute-start.11 = (bf16[1216,128]{1,0:T(8,128)(2,1)S(1)}, bf16[1216,128]{1,0:T(8,128)(2,1)S(1)}, u32[]{:S(2)}, u32[]{:S(2)}) collective-permute-start(bf16[1216,128]{1,0:T(8,128)(2,1)S(1)} %near.3), channel_id=1, source_target_pairs={{0,4},{1,5},{2,6},{3,7},{4,8},{5,9},{6,10},{7,11},{8,12},{9,13},{1... | collective-permute-start | bytes 933896 | tf_op jit(solution)/shard_map/ppermute | solution.py:268
  56.2 1.4 %both.2 = bf16[1216,128]{1,0:T(8,128)(2,1)S(1)} custom-call(bf16[128,1152]{1,0:T(8,128)(2,1)S(1)} %get-tuple-element.22.refs_0_, bf16[128,2304]{1,0:T(8,128)(2,1)S(1)} %get-tuple-element.30.refs_1_, bf16[128,2304]{1,0:T(8,128)(2,1)S(1)} %get-tuple-element.32.refs_2_, bf16[256,2304]{1,0:T(8,128)(2,1)S(1)} %collective-permute-done.7.refs_3_, ...), custom_call_target="tpu_custom_call" | custom-call | flops 4529848320 | bytes 1474560 | tf_op jit(solution)/shard_map/both/pallas_call | solution.py:183
  57.6 3.6 %collective-permute-start.15 = (bf16[1216,128]{1,0:T(8,128)(2,1)S(1)}, bf16[1216,128]{1,0:T(8,128)(2,1)S(1)}, u32[]{:S(2)}, u32[]{:S(2)}) collective-permute-start(bf16[1216,128]{1,0:T(8,128)(2,1)S(1)} %both.2), channel_id=1, source_target_pairs={{0,4},{1,5},{2,6},{3,7},{4,8},{5,9},{6,10},{7,11},{8,12},{9,13},{1... | collective-permute-start | bytes 933896 | tf_op jit(solution)/shard_map/ppermute | solution.py:268
  61.2 1.4 %both.3 = bf16[1216,128]{1,0:T(8,128)(2,1)S(1)} custom-call(bf16[128,1152]{1,0:T(8,128)(2,1)S(1)} %get-tuple-element.23.refs_0_, bf16[128,2304]{1,0:T(8,128)(2,1)S(1)} %get-tuple-element.30.refs_1_, bf16[128,2304]{1,0:T(8,128)(2,1)S(1)} %get-tuple-element.32.refs_2_, bf16[256,2304]{1,0:T(8,128)(2,1)S(1)} %collective-permute-done.7.refs_3_, ...), custom_call_target="tpu_custom_call" | custom-call | flops 4529848320 | bytes 1474560 | tf_op jit(solution)/shard_map/both/pallas_call | solution.py:183
  62.6 2.4 %collective-permute-start.14 = (bf16[1216,128]{1,0:T(8,128)(2,1)S(1)}, bf16[1216,128]{1,0:T(8,128)(2,1)S(1)}, u32[]{:S(2)}, u32[]{:S(2)}) collective-permute-start(bf16[1216,128]{1,0:T(8,128)(2,1)S(1)} %both.3), channel_id=1, source_target_pairs={{0,4},{1,5},{2,6},{3,7},{4,8},{5,9},{6,10},{7,11},{8,12},{9,13},{1... | collective-permute-start | bytes 933896 | tf_op jit(solution)/shard_map/ppermute | solution.py:268
  68.0 2.5 %collective-permute-done.15.refs_3_ = bf16[1216,128]{1,0:T(8,128)(2,1)S(1)} collective-permute-done((bf16[1216,128]{1,0:T(8,128)(2,1)S(1)}, bf16[1216,128]{1,0:T(8,128)(2,1)S(1)}, u32[]{:S(2)}, u32[]{:S(2)}) %collective-permute-start.15) | collective-permute-done | bytes 311328 | tf_op jit(solution)/shard_map/ppermute | solution.py:268
  71.6 3.1 %collective-permute-done.14.other_ref = bf16[1216,128]{1,0:T(8,128)(2,1)S(1)} collective-permute-done((bf16[1216,128]{1,0:T(8,128)(2,1)S(1)}, bf16[1216,128]{1,0:T(8,128)(2,1)S(1)}, u32[]{:S(2)}, u32[]{:S(2)}) %collective-permute-start.14) | collective-permute-done | bytes 311328 | tf_op jit(solution)/shard_map/ppermute | solution.py:268
  74.7 1.3 %last.1 = (bf16[1,128,2304]{2,1,0:T(8,128)(2,1)}, bf16[1,128,2304]{2,1,0:T(8,128)(2,1)}) custom-call(f32[128,1152]{1,0:T(8,128)S(1)} %get-tuple-element.26.sums_ref, f32[128,256]{1,0:T(8,128)S(1)} %get-tuple-element.27.state_ref, bf16[1216,128]{1,0:T(8,128)(2,1)S(1)} %collective-permute-done.14.other_ref, f32[2,128]{1,0:T(2,128)S(1)} %broadcast_in_dim.29.refs_4_.flags_ref, ...), custom_call_target="tpu_custom_call" | custom-call | flops 2013265920 | bytes 1474560 | tf_op jit(solution)/shard_map/last/pallas_call | solution.py:253
  (39 shorter events, 9.8 us)
Async XLA Ops:
  0.6 2.0 %copy-start = (bf16[1,128,2304]{2,1,0:T(8,128)(2,1)S(1)}, bf16[1,128,2304]{2,1,0:T(8,128)(2,1)}, u32[]{:S(2)}) copy-start(bf16[1,128,2304]{2,1,0:T(8,128)(2,1)} %param.8) | copy-start | bytes 1769476
  0.6 2.0 %copy-start.1 = (bf16[1,128,2304]{2,1,0:T(8,128)(2,1)S(1)}, bf16[1,128,2304]{2,1,0:T(8,128)(2,1)}, u32[]{:S(2)}) copy-start(bf16[1,128,2304]{2,1,0:T(8,128)(2,1)} %param.11) | copy-start | bytes 1769476
  2.1 1.1 %copy-start.2 = (bf16[1,128,2304]{2,1,0:T(8,128)(2,1)S(1)}, bf16[1,128,2304]{2,1,0:T(8,128)(2,1)}, u32[]{:S(2)}) copy-start(bf16[1,128,2304]{2,1,0:T(8,128)(2,1)} %param.9) | copy-start | bytes 1769476
  2.1 1.3 %copy-start.3 = (bf16[1,128,2304]{2,1,0:T(8,128)(2,1)S(1)}, bf16[1,128,2304]{2,1,0:T(8,128)(2,1)}, u32[]{:S(2)}) copy-start(bf16[1,128,2304]{2,1,0:T(8,128)(2,1)} %param.12) | copy-start | bytes 1769476
  2.1 6.5 %collective-permute-start = (bf16[128,2304]{1,0:T(8,128)(2,1)S(1)}, bf16[128,2304]{1,0:T(8,128)(2,1)S(1)}, u32[]{:S(2)}, u32[]{:S(2)}) collective-permute-start(bf16[128,2304]{1,0:T(8,128)(2,1)S(1)} %get-tuple-element.34), channel_id=1, source_target_pairs={{0,16},{16,0},{1,17},{17,1},{2,18},{18,2},{3,19},{19,3},{4,20},{20... | collective-permute-start | bytes 1769480 | tf_op jit(solution)/shard_map/ppermute | solution.py:282
  2.7 25.3 %collective-permute-start.1 = (bf16[128,2304]{1,0:T(8,128)(2,1)S(1)}, bf16[128,2304]{1,0:T(8,128)(2,1)S(1)}, u32[]{:S(2)}, u32[]{:S(2)}) collective-permute-start(bf16[128,2304]{1,0:T(8,128)(2,1)S(1)} %get-tuple-element.31), channel_id=1, source_target_pairs={{0,16},{16,0},{1,17},{17,1},{2,18},{18,2},{3,19},{19,3},{4,20},{20... | collective-permute-start | bytes 1769480 | tf_op jit(solution)/shard_map/ppermute | solution.py:282
  3.5 18.2 %copy-start.4 = (s32[1,2]{1,0:T(1,128)S(1)}, s32[1,2]{1,0:T(1,128)}, u32[]{:S(2)}) copy-start(s32[1,2]{1,0:T(1,128)} %param.13) | copy-start | bytes 28
  3.5 33.4 %collective-permute-start.7 = (bf16[256,2304]{1,0:T(8,128)(2,1)S(1)}, bf16[256,2304]{1,0:T(8,128)(2,1)S(1)}, u32[]{:S(2)}, u32[]{:S(2)}) collective-permute-start(bf16[256,2304]{1,0:T(8,128)(2,1)S(1)} %pad_maximum_fusion), channel_id=1, source_target_pairs={{0,4},{1,5},{2,6},{3,7},{4,8},{5,9},{6,10},{7,11},{8,12},{9,13},{1... | collective-permute-start | bytes 3538952 | tf_op jit(solution)/shard_map/ppermute | solution.py:268
  8.6 11.8 %collective-permute-start.4 = (bf16[128,1152]{1,0:T(8,128)(2,1)S(1)}, bf16[128,1152]{1,0:T(8,128)(2,1)S(1)}, u32[]{:S(2)}, u32[]{:S(2)}) collective-permute-start(bf16[128,1152]{1,0:T(8,128)(2,1)S(1)} %get-tuple-element.38), channel_id=1, source_target_pairs={{4,0},{5,1},{6,2},{7,3},{8,4},{9,5},{10,6},{11,7},{12,8},{13,9},{1... | collective-permute-start | bytes 884744 | tf_op jit(solution)/shard_map/ppermute | solution.py:268
  9.9 19.4 %collective-permute-start.2 = (bf16[128,2304]{1,0:T(8,128)(2,1)S(1)}, bf16[128,2304]{1,0:T(8,128)(2,1)S(1)}, u32[]{:S(2)}, u32[]{:S(2)}) collective-permute-start(bf16[128,2304]{1,0:T(8,128)(2,1)S(1)} %get-tuple-element.33), channel_id=1, source_target_pairs={{0,16},{16,0},{1,17},{17,1},{2,18},{18,2},{3,19},{19,3},{4,20},{20... | collective-permute-start | bytes 1769480 | tf_op jit(solution)/shard_map/ppermute | solution.py:282
  10.0 16.8 %collective-permute-start.3 = (bf16[128,1152]{1,0:T(8,128)(2,1)S(1)}, bf16[128,1152]{1,0:T(8,128)(2,1)S(1)}, u32[]{:S(2)}, u32[]{:S(2)}) collective-permute-start(bf16[128,1152]{1,0:T(8,128)(2,1)S(1)} %get-tuple-element.39), channel_id=1, source_target_pairs={{4,0},{5,1},{6,2},{7,3},{8,4},{9,5},{10,6},{11,7},{12,8},{13,9},{1... | collective-permute-start | bytes 884744 | tf_op jit(solution)/shard_map/ppermute | solution.py:268
  20.4 12.4 %collective-permute-start.6 = (bf16[128,1152]{1,0:T(8,128)(2,1)S(1)}, bf16[128,1152]{1,0:T(8,128)(2,1)S(1)}, u32[]{:S(2)}, u32[]{:S(2)}) collective-permute-start(bf16[128,1152]{1,0:T(8,128)(2,1)S(1)} %collective-permute-done.4.refs_0_), channel_id=1, source_target_pairs={{4,0},{5,1},{6,2},{7,3},{8,4},{9,5},{10,6},{11,7},{12,8},{13,9},{1... | collective-permute-start | bytes 884744 | tf_op jit(solution)/shard_map/ppermute | solution.py:268
  26.8 15.5 %collective-permute-start.10 = (s32[1,2]{1,0:T(1,128)S(1)}, s32[1,2]{1,0:T(1,128)S(1)}, u32[]{:S(2)}, u32[]{:S(2)}) collective-permute-start(s32[1,2]{1,0:T(1,128)S(1)} %copy-done.4), channel_id=1, source_target_pairs={{4,0},{5,1},{6,2},{7,3},{8,4},{9,5},{10,6},{11,7},{12,8},{13,9},{1... | collective-permute-start | bytes 32 | tf_op jit(solution)/shard_map/ppermute | solution.py:268
  28.1 9.9 %collective-permute-start.5 = (bf16[128,1152]{1,0:T(8,128)(2,1)S(1)}, bf16[128,1152]{1,0:T(8,128)(2,1)S(1)}, u32[]{:S(2)}, u32[]{:S(2)}) collective-permute-start(bf16[128,1152]{1,0:T(8,128)(2,1)S(1)} %collective-permute-done.3.refs_0_), channel_id=1, source_target_pairs={{4,0},{5,1},{6,2},{7,3},{8,4},{9,5},{10,6},{11,7},{12,8},{13,9},{1... | collective-permute-start | bytes 884744 | tf_op jit(solution)/shard_map/ppermute | solution.py:268
  33.7 9.9 %collective-permute-start.9 = (bf16[1216,128]{1,0:T(8,128)(2,1)S(1)}, bf16[1216,128]{1,0:T(8,128)(2,1)S(1)}, u32[]{:S(2)}, u32[]{:S(2)}) collective-permute-start(bf16[1216,128]{1,0:T(8,128)(2,1)S(1)} %far.2), channel_id=1, source_target_pairs={{0,4},{1,5},{2,6},{3,7},{4,8},{5,9},{6,10},{7,11},{8,12},{9,13},{1... | collective-permute-start | bytes 933896 | tf_op jit(solution)/shard_map/ppermute | solution.py:268
  38.8 11.2 %collective-permute-start.8 = (bf16[1216,128]{1,0:T(8,128)(2,1)S(1)}, bf16[1216,128]{1,0:T(8,128)(2,1)S(1)}, u32[]{:S(2)}, u32[]{:S(2)}) collective-permute-start(bf16[1216,128]{1,0:T(8,128)(2,1)S(1)} %far.3), channel_id=1, source_target_pairs={{0,4},{1,5},{2,6},{3,7},{4,8},{5,9},{6,10},{7,11},{8,12},{9,13},{1... | collective-permute-start | bytes 933896 | tf_op jit(solution)/shard_map/ppermute | solution.py:268
  42.3 13.9 %collective-permute-start.13 = (bf16[128,2304]{1,0:T(8,128)(2,1)S(1)}, bf16[128,2304]{1,0:T(8,128)(2,1)S(1)}, u32[]{:S(2)}, u32[]{:S(2)}) collective-permute-start(bf16[128,2304]{1,0:T(8,128)(2,1)S(1)} %get-tuple-element.25.refs_0_), channel_id=1, source_target_pairs={{4,0},{5,1},{6,2},{7,3},{8,4},{9,5},{10,6},{11,7},{12,8},{13,9},{1... | collective-permute-start | bytes 1769480 | tf_op jit(solution)/shard_map/ppermute | solution.py:268
  44.8 20.2 %collective-permute-start.12 = (bf16[1216,128]{1,0:T(8,128)(2,1)S(1)}, bf16[1216,128]{1,0:T(8,128)(2,1)S(1)}, u32[]{:S(2)}, u32[]{:S(2)}) collective-permute-start(bf16[1216,128]{1,0:T(8,128)(2,1)S(1)} %near.2), channel_id=1, source_target_pairs={{0,4},{1,5},{2,6},{3,7},{4,8},{5,9},{6,10},{7,11},{8,12},{9,13},{1... | collective-permute-start | bytes 933896 | tf_op jit(solution)/shard_map/ppermute | solution.py:268
  51.2 15.0 %collective-permute-start.11 = (bf16[1216,128]{1,0:T(8,128)(2,1)S(1)}, bf16[1216,128]{1,0:T(8,128)(2,1)S(1)}, u32[]{:S(2)}, u32[]{:S(2)}) collective-permute-start(bf16[1216,128]{1,0:T(8,128)(2,1)S(1)} %near.3), channel_id=1, source_target_pairs={{0,4},{1,5},{2,6},{3,7},{4,8},{5,9},{6,10},{7,11},{8,12},{9,13},{1... | collective-permute-start | bytes 933896 | tf_op jit(solution)/shard_map/ppermute | solution.py:268
  57.6 12.9 %collective-permute-start.15 = (bf16[1216,128]{1,0:T(8,128)(2,1)S(1)}, bf16[1216,128]{1,0:T(8,128)(2,1)S(1)}, u32[]{:S(2)}, u32[]{:S(2)}) collective-permute-start(bf16[1216,128]{1,0:T(8,128)(2,1)S(1)} %both.2), channel_id=1, source_target_pairs={{0,4},{1,5},{2,6},{3,7},{4,8},{5,9},{6,10},{7,11},{8,12},{9,13},{1... | collective-permute-start | bytes 933896 | tf_op jit(solution)/shard_map/ppermute | solution.py:268
  62.6 12.1 %collective-permute-start.14 = (bf16[1216,128]{1,0:T(8,128)(2,1)S(1)}, bf16[1216,128]{1,0:T(8,128)(2,1)S(1)}, u32[]{:S(2)}, u32[]{:S(2)}) collective-permute-start(bf16[1216,128]{1,0:T(8,128)(2,1)S(1)} %both.3), channel_id=1, source_target_pairs={{0,4},{1,5},{2,6},{3,7},{4,8},{5,9},{6,10},{7,11},{8,12},{9,13},{1... | collective-permute-start | bytes 933896 | tf_op jit(solution)/shard_map/ppermute | solution.py:268

commit v5 on v3

--- a/solution.py
+++ b/solution.py
@@ -205,7 +205,7 @@
 
 def last_kernel(count, sums_ref, state_ref, other_ref, flags_ref, second_ref, forward_ref, handed_ref, first_ref, sems):
     at_end = lax.axis_index("section") == lax.axis_size("section") - 1
-    step = -(-count // 3) * TILE
+    step = -(-count // 6) * TILE
 
     def copy(i, first_out, second_out):
         if i == 0:
@@ -243,7 +243,7 @@
         out_shape=(out, out),
         in_specs=[in_vmem] * 5,
         out_specs=(anywhere, anywhere),
-        scratch_shapes=[pltpu.VMEM(second.shape, second.dtype), pltpu.SemaphoreType.DMA((4,))],
+        scratch_shapes=[pltpu.VMEM(second.shape, second.dtype), pltpu.SemaphoreType.DMA((7,))],
         name="last",
         compiler_params=pltpu.CompilerParams(vmem_limit_bytes=16 * 1024 * 1024),
         cost_estimate=pl.CostEstimate(flops=WEIGHT << 26, bytes_accessed=5 * second.size, transcendentals=0),

time: 76.6 us -> 76.6 us (level)
  no operation moved by 1% of the time
where the time goes in v5:
time: 76.6 us; the launch traced here: 76.2 us
  starting transfers between devices  32.6 us (43%)
  waiting for transfers between devices  29.1 us (38%)
  Pallas kernels  11.1 us (14%)
  other arithmetic  1.67 us (2%)
  between operations  0.93 us (1%)
    ppermute x12, starting transfers between devices, shifted(): return lax.ppermute(block, axis, route)  31.9 us
    ppermute x12, waiting for transfers between devices, shifted(): return lax.ppermute(block, axis, route)  29.1 us
    pallas_call x8, Pallas kernels, attend(): pl.pallas_call(functools.partial(kernel, tiles, first, part), out_shape=o...  9.59 us
  transfers between devices with their start and end apart: 15, of which 8 were waited for; matrix products, arithmetic and copies ran while one was open for 1% of the time, Pallas kernels for 13%

profile of v5, /device:TPU:0, one launch (start us, length us, event | category | flops | bytes accessed | tf_op | source)
XLA Modules:
  0.0 76.2 jit_solution(15004613343158478240)
XLA Ops:
  0.7 1.4 %select_bitcast_fusion.4 = (bf16[128,2304]{1,0:T(8,128)(2,1)S(1)}, bf16[128,2304]{1,0:T(8,128)(2,1)S(1)}) fusion(bf16[1,128,2304]{2,1,0:T(8,128)(2,1)} %param.10, bf16[1,128,2304]{2,1,0:T(8,128)(2,1)} %param.7, pred[]{:T(512)S(6)} %eq.2), kind=kLoop, calls=%fused_computation.5 | loop fusion | flops 589824 | bytes 2359297 | tf_op jit(solution)/shard_map/jit(_where)/select_n | solution.py:270
  3.5 5.0 %collective-permute-start.7 = (bf16[256,2304]{1,0:T(8,128)(2,1)S(1)}, bf16[256,2304]{1,0:T(8,128)(2,1)S(1)}, u32[]{:S(2)}, u32[]{:S(2)}) collective-permute-start(bf16[256,2304]{1,0:T(8,128)(2,1)S(1)} %pad_maximum_fusion), channel_id=1, source_target_pairs={{0,4},{1,5},{2,6},{3,7},{4,8},{5,9},{6,10},{7,11},{8,12},{9,13},{1... | collective-permute-start | bytes 3538952 | tf_op jit(solution)/shard_map/ppermute | solution.py:256
  8.6 1.3 %collective-permute-start.4 = (bf16[128,1152]{1,0:T(8,128)(2,1)S(1)}, bf16[128,1152]{1,0:T(8,128)(2,1)S(1)}, u32[]{:S(2)}, u32[]{:S(2)}) collective-permute-start(bf16[128,1152]{1,0:T(8,128)(2,1)S(1)} %get-tuple-element.32), channel_id=1, source_target_pairs={{4,0},{5,1},{6,2},{7,3},{8,4},{9,5},{10,6},{11,7},{12,8},{13,9},{1... | collective-permute-start | bytes 884744 | tf_op jit(solution)/shard_map/ppermute | solution.py:256
  10.0 1.3 %collective-permute-start.3 = (bf16[128,1152]{1,0:T(8,128)(2,1)S(1)}, bf16[128,1152]{1,0:T(8,128)(2,1)S(1)}, u32[]{:S(2)}, u32[]{:S(2)}) collective-permute-start(bf16[128,1152]{1,0:T(8,128)(2,1)S(1)} %get-tuple-element.33), channel_id=1, source_target_pairs={{4,0},{5,1},{6,2},{7,3},{8,4},{9,5},{10,6},{11,7},{12,8},{13,9},{1... | collective-permute-start | bytes 884744 | tf_op jit(solution)/shard_map/ppermute | solution.py:256
  11.3 9.1 %collective-permute-done.4.refs_0_ = bf16[128,1152]{1,0:T(8,128)(2,1)S(1)} collective-permute-done((bf16[128,1152]{1,0:T(8,128)(2,1)S(1)}, bf16[128,1152]{1,0:T(8,128)(2,1)S(1)}, u32[]{:S(2)}, u32[]{:S(2)}) %collective-permute-start.4) | collective-permute-done | bytes 294944 | tf_op jit(solution)/shard_map/ppermute | solution.py:256
  20.4 1.3 %collective-permute-start.6 = (bf16[128,1152]{1,0:T(8,128)(2,1)S(1)}, bf16[128,1152]{1,0:T(8,128)(2,1)S(1)}, u32[]{:S(2)}, u32[]{:S(2)}) collective-permute-start(bf16[128,1152]{1,0:T(8,128)(2,1)S(1)} %collective-permute-done.4.refs_0_), channel_id=1, source_target_pairs={{4,0},{5,1},{6,2},{7,3},{8,4},{9,5},{10,6},{11,7},{12,8},{13,9},{1... | collective-permute-start | bytes 884744 | tf_op jit(solution)/shard_map/ppermute | solution.py:256
  21.8 5.0 %collective-permute-done.3.refs_0_ = bf16[128,1152]{1,0:T(8,128)(2,1)S(1)} collective-permute-done((bf16[128,1152]{1,0:T(8,128)(2,1)S(1)}, bf16[128,1152]{1,0:T(8,128)(2,1)S(1)}, u32[]{:S(2)}, u32[]{:S(2)}) %collective-permute-start.3) | collective-permute-done | bytes 294944 | tf_op jit(solution)/shard_map/ppermute | solution.py:256
  26.8 1.3 %collective-permute-start.10 = (s32[1,2]{1,0:T(1,128)S(1)}, s32[1,2]{1,0:T(1,128)S(1)}, u32[]{:S(2)}, u32[]{:S(2)}) collective-permute-start(s32[1,2]{1,0:T(1,128)S(1)} %copy-done.4), channel_id=1, source_target_pairs={{4,0},{5,1},{6,2},{7,3},{8,4},{9,5},{10,6},{11,7},{12,8},{13,9},{1... | collective-permute-start | bytes 32 | tf_op jit(solution)/shard_map/ppermute | solution.py:256
  28.1 1.3 %collective-permute-start.5 = (bf16[128,1152]{1,0:T(8,128)(2,1)S(1)}, bf16[128,1152]{1,0:T(8,128)(2,1)S(1)}, u32[]{:S(2)}, u32[]{:S(2)}) collective-permute-start(bf16[128,1152]{1,0:T(8,128)(2,1)S(1)} %collective-permute-done.3.refs_0_), channel_id=1, source_target_pairs={{4,0},{5,1},{6,2},{7,3},{8,4},{9,5},{10,6},{11,7},{12,8},{13,9},{1... | collective-permute-start | bytes 884744 | tf_op jit(solution)/shard_map/ppermute | solution.py:256
  29.4 3.4 %collective-permute-done.6.refs_0_ = bf16[128,1152]{1,0:T(8,128)(2,1)S(1)} collective-permute-done((bf16[128,1152]{1,0:T(8,128)(2,1)S(1)}, bf16[128,1152]{1,0:T(8,128)(2,1)S(1)}, u32[]{:S(2)}, u32[]{:S(2)}) %collective-permute-start.6) | collective-permute-done | bytes 294944 | tf_op jit(solution)/shard_map/ppermute | solution.py:256
  33.7 3.2 %collective-permute-start.9 = (bf16[1216,128]{1,0:T(8,128)(2,1)S(1)}, bf16[1216,128]{1,0:T(8,128)(2,1)S(1)}, u32[]{:S(2)}, u32[]{:S(2)}) collective-permute-start(bf16[1216,128]{1,0:T(8,128)(2,1)S(1)} %far.2), channel_id=1, source_target_pairs={{0,4},{1,5},{2,6},{3,7},{4,8},{5,9},{6,10},{7,11},{8,12},{9,13},{1... | collective-permute-start | bytes 933896 | tf_op jit(solution)/shard_map/ppermute | solution.py:256
  36.9 1.0 %collective-permute-done.5.refs_0_ = bf16[128,1152]{1,0:T(8,128)(2,1)S(1)} collective-permute-done((bf16[128,1152]{1,0:T(8,128)(2,1)S(1)}, bf16[128,1152]{1,0:T(8,128)(2,1)S(1)}, u32[]{:S(2)}, u32[]{:S(2)}) %collective-permute-start.5) | collective-permute-done | bytes 294944 | tf_op jit(solution)/shard_map/ppermute | solution.py:256
  38.8 3.4 %collective-permute-start.8 = (bf16[1216,128]{1,0:T(8,128)(2,1)S(1)}, bf16[1216,128]{1,0:T(8,128)(2,1)S(1)}, u32[]{:S(2)}, u32[]{:S(2)}) collective-permute-start(bf16[1216,128]{1,0:T(8,128)(2,1)S(1)} %far.3), channel_id=1, source_target_pairs={{0,4},{1,5},{2,6},{3,7},{4,8},{5,9},{6,10},{7,11},{8,12},{9,13},{1... | collective-permute-start | bytes 933896 | tf_op jit(solution)/shard_map/ppermute | solution.py:256
  42.3 1.3 %collective-permute-start.13 = (bf16[128,2304]{1,0:T(8,128)(2,1)S(1)}, bf16[128,2304]{1,0:T(8,128)(2,1)S(1)}, u32[]{:S(2)}, u32[]{:S(2)}) collective-permute-start(bf16[128,2304]{1,0:T(8,128)(2,1)S(1)} %get-tuple-element.22.refs_0_), channel_id=1, source_target_pairs={{4,0},{5,1},{6,2},{7,3},{8,4},{9,5},{10,6},{11,7},{12,8},{13,9},{1... | collective-permute-start | bytes 1769480 | tf_op jit(solution)/shard_map/ppermute | solution.py:256
  43.7 1.1 %near.2 = bf16[1216,128]{1,0:T(8,128)(2,1)S(1)} custom-call(bf16[128,1152]{1,0:T(8,128)(2,1)S(1)} %collective-permute-done.4.refs_0_, bf16[128,2304]{1,0:T(8,128)(2,1)S(1)} %collective-permute-done.1.refs_1_, bf16[128,2304]{1,0:T(8,128)(2,1)S(1)} %collective-permute-done.2.refs_2_, bf16[1216,128]{1,0:T(8,128)(2,1)S(1)} %collective-permute-done.9.refs_3_, ...), custom_call_target="tpu_custom_call" | custom-call | flops 4529848320 | bytes 1474560 | tf_op jit(solution)/shard_map/near/pallas_call | solution.py:183
  44.8 4.6 %collective-permute-start.12 = (bf16[1216,128]{1,0:T(8,128)(2,1)S(1)}, bf16[1216,128]{1,0:T(8,128)(2,1)S(1)}, u32[]{:S(2)}, u32[]{:S(2)}) collective-permute-start(bf16[1216,128]{1,0:T(8,128)(2,1)S(1)} %near.2), channel_id=1, source_target_pairs={{0,4},{1,5},{2,6},{3,7},{4,8},{5,9},{6,10},{7,11},{8,12},{9,13},{1... | collective-permute-start | bytes 933896 | tf_op jit(solution)/shard_map/ppermute | solution.py:256
  50.1 1.1 %near.3 = bf16[1216,128]{1,0:T(8,128)(2,1)S(1)} custom-call(bf16[128,1152]{1,0:T(8,128)(2,1)S(1)} %collective-permute-done.3.refs_0_, bf16[128,2304]{1,0:T(8,128)(2,1)S(1)} %collective-permute-done.1.refs_1_, bf16[128,2304]{1,0:T(8,128)(2,1)S(1)} %collective-permute-done.2.refs_2_, bf16[1216,128]{1,0:T(8,128)(2,1)S(1)} %collective-permute-done.8.refs_3_, ...), custom_call_target="tpu_custom_call" | custom-call | flops 4529848320 | bytes 1474560 | tf_op jit(solution)/shard_map/near/pallas_call | solution.py:183
  51.2 4.4 %collective-permute-start.11 = (bf16[1216,128]{1,0:T(8,128)(2,1)S(1)}, bf16[1216,128]{1,0:T(8,128)(2,1)S(1)}, u32[]{:S(2)}, u32[]{:S(2)}) collective-permute-start(bf16[1216,128]{1,0:T(8,128)(2,1)S(1)} %near.3), channel_id=1, source_target_pairs={{0,4},{1,5},{2,6},{3,7},{4,8},{5,9},{6,10},{7,11},{8,12},{9,13},{1... | collective-permute-start | bytes 933896 | tf_op jit(solution)/shard_map/ppermute | solution.py:256
  56.2 2.3 %both.1 = bf16[2432,128]{1,0:T(8,128)(2,1)S(1)} custom-call(bf16[128,2304]{1,0:T(8,128)(2,1)S(1)} %collective-permute-done.13.refs_0_, bf16[128,2304]{1,0:T(8,128)(2,1)S(1)} %get-tuple-element.26.refs_1_, bf16[128,2304]{1,0:T(8,128)(2,1)S(1)} %get-tuple-element.28.refs_2_, bf16[256,2304]{1,0:T(8,128)(2,1)S(1)} %collective-permute-done.7.refs_3_, ...), custom_call_target="tpu_custom_call" | custom-call | flops 9059696640 | bytes 2949120 | tf_op jit(solution)/shard_map/both/pallas_call | solution.py:183
  58.5 3.6 %collective-permute-start.14 = (bf16[2432,128]{1,0:T(8,128)(2,1)S(1)}, bf16[2432,128]{1,0:T(8,128)(2,1)S(1)}, u32[]{:S(2)}, u32[]{:S(2)}) collective-permute-start(bf16[2432,128]{1,0:T(8,128)(2,1)S(1)} %both.1), channel_id=1, source_target_pairs={{0,4},{1,5},{2,6},{3,7},{4,8},{5,9},{6,10},{7,11},{8,12},{9,13},{1... | collective-permute-start | bytes 1867784 | tf_op jit(solution)/shard_map/ppermute | solution.py:256
  62.2 1.1 %own.2.refs_5_ = bf16[128,2304]{1,0:T(8,128)(2,1)S(1)} custom-call(bf16[128,2304]{1,0:T(8,128)(2,1)S(1)} %collective-permute-done.refs_0_, bf16[128,2304]{1,0:T(8,128)(2,1)S(1)} %collective-permute-done.1.refs_1_, bf16[128,2304]{1,0:T(8,128)(2,1)S(1)} %collective-permute-done.2.refs_2_, bf16[1216,128]{1,0:T(8,128)(2,1)S(1)} %collective-permute-done.12.refs_3_, ...), custom_call_target="tpu_custom_call" | custom-call | flops 4529848320 | bytes 1474560 | tf_op jit(solution)/shard_map/own/pallas_call | solution.py:183
  63.8 1.1 %own.3.second_ref = bf16[128,2304]{1,0:T(8,128)(2,1)S(1)} custom-call(bf16[128,2304]{1,0:T(8,128)(2,1)S(1)} %collective-permute-done.refs_0_, bf16[128,2304]{1,0:T(8,128)(2,1)S(1)} %collective-permute-done.1.refs_1_, bf16[128,2304]{1,0:T(8,128)(2,1)S(1)} %collective-permute-done.2.refs_2_, ...), custom_call_target="tpu_custom_call", output_to_operand_aliasing={{}: (5, {})} | custom-call | flops 4529848320 | bytes 1474560 | tf_op jit(solution)/shard_map/own/pallas_call | solution.py:183
  66.0 8.7 %collective-permute-done.14.other_ref = bf16[2432,128]{1,0:T(8,128)(2,1)S(1)} collective-permute-done((bf16[2432,128]{1,0:T(8,128)(2,1)S(1)}, bf16[2432,128]{1,0:T(8,128)(2,1)S(1)}, u32[]{:S(2)}, u32[]{:S(2)}) %collective-permute-start.14) | collective-permute-done | bytes 622624 | tf_op jit(solution)/shard_map/ppermute | solution.py:256
  74.7 1.5 %last.1 = (bf16[1,128,2304]{2,1,0:T(8,128)(2,1)}, bf16[1,128,2304]{2,1,0:T(8,128)(2,1)}) custom-call(f32[128,2304]{1,0:T(8,128)S(1)} %get-tuple-element.23.sums_ref, f32[128,256]{1,0:T(8,128)S(1)} %get-tuple-element.24.state_ref, bf16[2432,128]{1,0:T(8,128)(2,1)S(1)} %collective-permute-done.14.other_ref, f32[2,128]{1,0:T(2,128)S(1)} %broadcast_in_dim.29.refs_4_.flags_ref, ...), custom_call_target="tpu_custom_call" | custom-call | flops 2013265920 | bytes 1474560 | tf_op jit(solution)/shard_map/last/pallas_call | solution.py:241
  (34 shorter events, 6.3 us)
Async XLA Ops:
  0.6 2.0 %copy-start = (bf16[1,128,2304]{2,1,0:T(8,128)(2,1)S(1)}, bf16[1,128,2304]{2,1,0:T(8,128)(2,1)}, u32[]{:S(2)}) copy-start(bf16[1,128,2304]{2,1,0:T(8,128)(2,1)} %param.8) | copy-start | bytes 1769476
  0.6 2.0 %copy-start.1 = (bf16[1,128,2304]{2,1,0:T(8,128)(2,1)S(1)}, bf16[1,128,2304]{2,1,0:T(8,128)(2,1)}, u32[]{:S(2)}) copy-start(bf16[1,128,2304]{2,1,0:T(8,128)(2,1)} %param.11) | copy-start | bytes 1769476
  2.1 1.1 %copy-start.2 = (bf16[1,128,2304]{2,1,0:T(8,128)(2,1)S(1)}, bf16[1,128,2304]{2,1,0:T(8,128)(2,1)}, u32[]{:S(2)}) copy-start(bf16[1,128,2304]{2,1,0:T(8,128)(2,1)} %param.9) | copy-start | bytes 1769476
  2.1 1.3 %copy-start.3 = (bf16[1,128,2304]{2,1,0:T(8,128)(2,1)S(1)}, bf16[1,128,2304]{2,1,0:T(8,128)(2,1)}, u32[]{:S(2)}) copy-start(bf16[1,128,2304]{2,1,0:T(8,128)(2,1)} %param.12) | copy-start | bytes 1769476
  2.1 6.5 %collective-permute-start = (bf16[128,2304]{1,0:T(8,128)(2,1)S(1)}, bf16[128,2304]{1,0:T(8,128)(2,1)S(1)}, u32[]{:S(2)}, u32[]{:S(2)}) collective-permute-start(bf16[128,2304]{1,0:T(8,128)(2,1)S(1)} %get-tuple-element.30), channel_id=1, source_target_pairs={{0,16},{16,0},{1,17},{17,1},{2,18},{18,2},{3,19},{19,3},{4,20},{20... | collective-permute-start | bytes 1769480 | tf_op jit(solution)/shard_map/ppermute | solution.py:270
  2.7 25.3 %collective-permute-start.1 = (bf16[128,2304]{1,0:T(8,128)(2,1)S(1)}, bf16[128,2304]{1,0:T(8,128)(2,1)S(1)}, u32[]{:S(2)}, u32[]{:S(2)}) collective-permute-start(bf16[128,2304]{1,0:T(8,128)(2,1)S(1)} %get-tuple-element.27), channel_id=1, source_target_pairs={{0,16},{16,0},{1,17},{17,1},{2,18},{18,2},{3,19},{19,3},{4,20},{20... | collective-permute-start | bytes 1769480 | tf_op jit(solution)/shard_map/ppermute | solution.py:270
  3.5 18.2 %copy-start.4 = (s32[1,2]{1,0:T(1,128)S(1)}, s32[1,2]{1,0:T(1,128)}, u32[]{:S(2)}) copy-start(s32[1,2]{1,0:T(1,128)} %param.13) | copy-start | bytes 28
  3.5 34.4 %collective-permute-start.7 = (bf16[256,2304]{1,0:T(8,128)(2,1)S(1)}, bf16[256,2304]{1,0:T(8,128)(2,1)S(1)}, u32[]{:S(2)}, u32[]{:S(2)}) collective-permute-start(bf16[256,2304]{1,0:T(8,128)(2,1)S(1)} %pad_maximum_fusion), channel_id=1, source_target_pairs={{0,4},{1,5},{2,6},{3,7},{4,8},{5,9},{6,10},{7,11},{8,12},{9,13},{1... | collective-permute-start | bytes 3538952 | tf_op jit(solution)/shard_map/ppermute | solution.py:256
  8.6 11.8 %collective-permute-start.4 = (bf16[128,1152]{1,0:T(8,128)(2,1)S(1)}, bf16[128,1152]{1,0:T(8,128)(2,1)S(1)}, u32[]{:S(2)}, u32[]{:S(2)}) collective-permute-start(bf16[128,1152]{1,0:T(8,128)(2,1)S(1)} %get-tuple-element.32), channel_id=1, source_target_pairs={{4,0},{5,1},{6,2},{7,3},{8,4},{9,5},{10,6},{11,7},{12,8},{13,9},{1... | collective-permute-start | bytes 884744 | tf_op jit(solution)/shard_map/ppermute | solution.py:256
  9.9 19.4 %collective-permute-start.2 = (bf16[128,2304]{1,0:T(8,128)(2,1)S(1)}, bf16[128,2304]{1,0:T(8,128)(2,1)S(1)}, u32[]{:S(2)}, u32[]{:S(2)}) collective-permute-start(bf16[128,2304]{1,0:T(8,128)(2,1)S(1)} %get-tuple-element.29), channel_id=1, source_target_pairs={{0,16},{16,0},{1,17},{17,1},{2,18},{18,2},{3,19},{19,3},{4,20},{20... | collective-permute-start | bytes 1769480 | tf_op jit(solution)/shard_map/ppermute | solution.py:270
  10.0 16.8 %collective-permute-start.3 = (bf16[128,1152]{1,0:T(8,128)(2,1)S(1)}, bf16[128,1152]{1,0:T(8,128)(2,1)S(1)}, u32[]{:S(2)}, u32[]{:S(2)}) collective-permute-start(bf16[128,1152]{1,0:T(8,128)(2,1)S(1)} %get-tuple-element.33), channel_id=1, source_target_pairs={{4,0},{5,1},{6,2},{7,3},{8,4},{9,5},{10,6},{11,7},{12,8},{13,9},{1... | collective-permute-start | bytes 884744 | tf_op jit(solution)/shard_map/ppermute | solution.py:256
  20.4 12.4 %collective-permute-start.6 = (bf16[128,1152]{1,0:T(8,128)(2,1)S(1)}, bf16[128,1152]{1,0:T(8,128)(2,1)S(1)}, u32[]{:S(2)}, u32[]{:S(2)}) collective-permute-start(bf16[128,1152]{1,0:T(8,128)(2,1)S(1)} %collective-permute-done.4.refs_0_), channel_id=1, source_target_pairs={{4,0},{5,1},{6,2},{7,3},{8,4},{9,5},{10,6},{11,7},{12,8},{13,9},{1... | collective-permute-start | bytes 884744 | tf_op jit(solution)/shard_map/ppermute | solution.py:256
  26.8 15.5 %collective-permute-start.10 = (s32[1,2]{1,0:T(1,128)S(1)}, s32[1,2]{1,0:T(1,128)S(1)}, u32[]{:S(2)}, u32[]{:S(2)}) collective-permute-start(s32[1,2]{1,0:T(1,128)S(1)} %copy-done.4), channel_id=1, source_target_pairs={{4,0},{5,1},{6,2},{7,3},{8,4},{9,5},{10,6},{11,7},{12,8},{13,9},{1... | collective-permute-start | bytes 32 | tf_op jit(solution)/shard_map/ppermute | solution.py:256
  28.1 9.9 %collective-permute-start.5 = (bf16[128,1152]{1,0:T(8,128)(2,1)S(1)}, bf16[128,1152]{1,0:T(8,128)(2,1)S(1)}, u32[]{:S(2)}, u32[]{:S(2)}) collective-permute-start(bf16[128,1152]{1,0:T(8,128)(2,1)S(1)} %collective-permute-done.3.refs_0_), channel_id=1, source_target_pairs={{4,0},{5,1},{6,2},{7,3},{8,4},{9,5},{10,6},{11,7},{12,8},{13,9},{1... | collective-permute-start | bytes 884744 | tf_op jit(solution)/shard_map/ppermute | solution.py:256
  33.7 9.9 %collective-permute-start.9 = (bf16[1216,128]{1,0:T(8,128)(2,1)S(1)}, bf16[1216,128]{1,0:T(8,128)(2,1)S(1)}, u32[]{:S(2)}, u32[]{:S(2)}) collective-permute-start(bf16[1216,128]{1,0:T(8,128)(2,1)S(1)} %far.2), channel_id=1, source_target_pairs={{0,4},{1,5},{2,6},{3,7},{4,8},{5,9},{6,10},{7,11},{8,12},{9,13},{1... | collective-permute-start | bytes 933896 | tf_op jit(solution)/shard_map/ppermute | solution.py:256
  38.8 11.2 %collective-permute-start.8 = (bf16[1216,128]{1,0:T(8,128)(2,1)S(1)}, bf16[1216,128]{1,0:T(8,128)(2,1)S(1)}, u32[]{:S(2)}, u32[]{:S(2)}) collective-permute-start(bf16[1216,128]{1,0:T(8,128)(2,1)S(1)} %far.3), channel_id=1, source_target_pairs={{0,4},{1,5},{2,6},{3,7},{4,8},{5,9},{6,10},{7,11},{8,12},{9,13},{1... | collective-permute-start | bytes 933896 | tf_op jit(solution)/shard_map/ppermute | solution.py:256
  42.3 13.9 %collective-permute-start.13 = (bf16[128,2304]{1,0:T(8,128)(2,1)S(1)}, bf16[128,2304]{1,0:T(8,128)(2,1)S(1)}, u32[]{:S(2)}, u32[]{:S(2)}) collective-permute-start(bf16[128,2304]{1,0:T(8,128)(2,1)S(1)} %get-tuple-element.22.refs_0_), channel_id=1, source_target_pairs={{4,0},{5,1},{6,2},{7,3},{8,4},{9,5},{10,6},{11,7},{12,8},{13,9},{1... | collective-permute-start | bytes 1769480 | tf_op jit(solution)/shard_map/ppermute | solution.py:256
  44.8 17.3 %collective-permute-start.12 = (bf16[1216,128]{1,0:T(8,128)(2,1)S(1)}, bf16[1216,128]{1,0:T(8,128)(2,1)S(1)}, u32[]{:S(2)}, u32[]{:S(2)}) collective-permute-start(bf16[1216,128]{1,0:T(8,128)(2,1)S(1)} %near.2), channel_id=1, source_target_pairs={{0,4},{1,5},{2,6},{3,7},{4,8},{5,9},{6,10},{7,11},{8,12},{9,13},{1... | collective-permute-start | bytes 933896 | tf_op jit(solution)/shard_map/ppermute | solution.py:256
  51.2 12.6 %collective-permute-start.11 = (bf16[1216,128]{1,0:T(8,128)(2,1)S(1)}, bf16[1216,128]{1,0:T(8,128)(2,1)S(1)}, u32[]{:S(2)}, u32[]{:S(2)}) collective-permute-start(bf16[1216,128]{1,0:T(8,128)(2,1)S(1)} %near.3), channel_id=1, source_target_pairs={{0,4},{1,5},{2,6},{3,7},{4,8},{5,9},{6,10},{7,11},{8,12},{9,13},{1... | collective-permute-start | bytes 933896 | tf_op jit(solution)/shard_map/ppermute | solution.py:256
  58.5 16.2 %collective-permute-start.14 = (bf16[2432,128]{1,0:T(8,128)(2,1)S(1)}, bf16[2432,128]{1,0:T(8,128)(2,1)S(1)}, u32[]{:S(2)}, u32[]{:S(2)}) collective-permute-start(bf16[2432,128]{1,0:T(8,128)(2,1)S(1)} %both.1), channel_id=1, source_target_pairs={{0,4},{1,5},{2,6},{3,7},{4,8},{5,9},{6,10},{7,11},{8,12},{9,13},{1... | collective-permute-start | bytes 1867784 | tf_op jit(solution)/shard_map/ppermute | solution.py:256
